TPU v7x, 32 devices: a whole 2x2x4 slice. The times are simulated.
32 devices in a mesh: walk: 4 (over y, x), chol: 8 (over z, core).
Axes of the slice: x: 2, y: 2, z: 4, core: 2. Of those that a mesh axis runs over, the one named last changes fastest.
Arguments:
- trial: float32 [512, 64], replicated
- walkers: float32 [64, 512, 64], P(('walk', 'chol')), as said below
- chol: float32 [2560, 262144], P(None, ('walk', 'chol'))
- field_noise: float32 [64, 2560], P(('walk', 'chol')), may hold values from -6 to 6
- log_weight: float32 [64], P(('walk', 'chol')), may hold values from -1 to 1
- parent: int32 [64], P(('walk', 'chol')), may hold values from 0 to 63, as said below
Outputs:
- new_walkers: float32 [64, 512, 64], P(('walk', 'chol'))
- new_log_weight: float32 [64], P(('walk', 'chol'))
Inputs may be any that keep to these rules, and one draw needn't show every extreme that they name: parent[w] // 16 equals w // 16: a walker copies one of the walkers whose slots share its index along walk; some parents are copied many times and others not at all. trial and walkers are such that intersection[w] has a dominant diagonal.
All inputs are finite; a program needn't handle non-finite values.
Results may differ from a plain program's by a relative error of at most 0.0003.
Values sent between devices are 32-bit elements; how exact they have to be, the bound alone decides.
No kernel may reach another device: no remote copies, remote signals or barrier semaphores. Data moves between devices by JAX's collectives and lax.ppermute only.
A program may use at most 128 MiB of HBM per device.

v0:
```python
import jax
import jax.numpy as jnp
from jax import lax
from jax.sharding import PartitionSpec as P

TERMS = 6


PRECISE = lax.Precision.HIGHEST
TIME_ROOT = 0.1


def solve_single(factor, intersection):
    return jax.scipy.linalg.cho_solve((factor, True), intersection.T)


def rotate(trial, walkers):
    intersection = jnp.einsum("mn,wmk->wnk", trial, walkers, precision=PRECISE)
    normal = jnp.einsum("wkn,wkm->wnm", intersection, intersection, precision=PRECISE)
    factor = jnp.linalg.cholesky(normal)
    inverse = jax.vmap(solve_single)(factor, intersection)
    return jnp.einsum("wmn,wnk->wmk", walkers, inverse, precision=PRECISE)


def expand(rotated, trial):
    return jnp.einsum("wmk,ik->wmi", rotated, trial, precision=PRECISE)


def per_device(trial, walkers, chol, field_noise, log_weight, parent):
    own_walkers = walkers.shape[0]
    orbitals = walkers.shape[1]
    walk_size = lax.axis_size("walk")
    chol_size = lax.axis_size("chol")
    pairs_here = chol.shape[1]
    everyone = own_walkers * walk_size * chol_size
    rotated = rotate(trial, walkers)
    owned_rows = lax.all_to_all(rotated, ("walk", "chol"), split_axis=1, concat_axis=0, tiled=True)
    green_tiles = expand(owned_rows, trial).reshape(everyone, pairs_here)
    partial_value = lax.dot_general(
        green_tiles,
        chol,
        (((1,), (1,)), ((), ())),
        precision=PRECISE,
        preferred_element_type=jnp.float32,
    )
    position = lax.axis_index(("walk", "chol"))
    bias = lax.psum(partial_value, ("walk", "chol"))
    noise_all = lax.all_gather(field_noise, ("walk", "chol"), axis=0, tiled=True)
    shift_all = TIME_ROOT * bias
    fields = noise_all - shift_all
    own_shift = lax.dynamic_slice_in_dim(shift_all, position * own_walkers, own_walkers, 0)
    weight = log_weight + jnp.sum(0.5 * own_shift * own_shift - field_noise * own_shift, axis=1)
    pot_tiles = TIME_ROOT * jnp.dot(
        fields, chol, precision=PRECISE, preferred_element_type=jnp.float32
    )
    potential = lax.all_to_all(pot_tiles, ("walk", "chol"), split_axis=0, concat_axis=1, tiled=True)
    potential = potential.reshape(own_walkers, orbitals, orbitals)
    running = walkers
    taylor_term = walkers
    for order in range(1, TERMS):
        taylor_term = jnp.einsum("wij,wjn->win", potential, taylor_term, precision=PRECISE) / order
        running = running + taylor_term
    first_index = lax.axis_index("walk") * (own_walkers * chol_size)
    local_parent = parent - first_index
    initial = (jnp.zeros_like(running), jnp.zeros_like(weight))
    piece = (
        lax.all_gather(running, "chol", axis=0, tiled=True),
        lax.all_gather(weight, "chol", axis=0, tiled=True),
    )
    rows_here = piece[0].shape[0]
    inside = (local_parent >= 0) & (local_parent < rows_here)
    picked = jnp.clip(local_parent, 0, rows_here - 1)
    states = jnp.take(piece[0], picked, axis=0)
    weights = jnp.take(piece[1], picked, axis=0)
    new_walkers = jnp.where(inside[:, None, None], states, initial[0])
    new_log_weight = jnp.where(inside, weights, initial[1])
    return (new_walkers, new_log_weight)


def solution(mesh):
    return jax.shard_map(
        per_device,
        mesh=mesh,
        in_specs=(
            P(),
            P(("walk", "chol"), None, None),
            P(None, ("walk", "chol")),
            P(("walk", "chol"), None),
            P(("walk", "chol")),
            P(("walk", "chol")),
        ),
        out_specs=(P(("walk", "chol"), None, None), P(("walk", "chol"))),
        check_vma=False,
    )
```

profile of v0, /device:TPU:0, one launch (start us, length us, event | category | flops | bytes accessed | tf_op | source)
XLA Modules:
  0.0 438.7 jit_solution(7123321231906888338)
XLA Ops:
  7.2 0.0 copy-start
  7.2 0.0 all-reduce.3.cloned.1.call-start
  7.3 0.8 copy-done
  8.1 1.3 fusion.4
  9.4 0.2 fusion.13
  9.6 0.1 copy.22
  9.7 11.7 %custom-call.11 = f32[2,64,64]{2,1,0:T(8,128)S(1)} custom-call(f32[2,64,64]{2,1,0:T(8,128)S(1)} %fusion.10), custom_call_target="Cholesky" | custom-call | tf_op jit(solution)/shard_map/jit(cholesky)/cholesky | solution.py:20
  21.5 0.1 compare_reduce_fusion
  21.6 0.1 select_bitcast_fusion
  21.7 9.8 %custom-call.12 = f32[2,1,64,64]{2,3,1,0:T(8,128)S(1)} custom-call(f32[2,1,64,64]{3,2,1,0:T(8,128)S(1)} %select_bitcast_fusion), custom_call_target="InvertDiagBlocksLowerTriangular" | custom-call | tf_op jit(solution)/shard_map/vmap(jit(_cho_solve))/triangular_solve | solution.py:14
  31.5 0.3 fusion.8
  31.8 0.3 fusion.6
  32.1 1.3 convolution_bitcast_fusion
  33.4 0.2 copy.25
  33.7 0.6 reshape.62
  34.3 17.5 %all_to_all.34 = f32[32,1,2048]{2,1,0:T(1,128)S(1)} all-to-all(f32[32,1,2048]{2,1,0:T(1,128)S(1)} %reshape.62), channel_id=1, replica_groups=mesh['walk'=4,'chol'=8] {'walk','chol'}, dimensions={0} | all-to-all | bytes 524288 | tf_op jit(solution)/shard_map/all_to_all | solution.py:37
  51.7 0.5 broadcast.128
  52.3 1.3 reduce.6
  53.5 0.4 reshape.63
  54.0 0.1 copy.27
  54.0 1.8 fusion.2
  55.8 1.2 copy.31
  57.0 0.0 copy-start.3
  57.0 86.8 %fusion.14 = f32[64,2560]{1,0:T(8,128)} fusion(f32[64,8192]{1,0:T(8,128)S(1)} %bitcast.50, f32[2560,8192]{1,0:T(8,128)} %param.8), kind=kOutput, calls=%fused_computation.37 | convolution fusion | flops 16106127360 | bytes 86638592 | tf_op jit(solution)/shard_map/dot_general | solution.py:39
  143.9 0.0 all-reduce.3.cloned.1.call-update
  143.9 0.0 all-gather.3.cloned.1.call-start
  143.9 0.0 copy-done.3
  143.9 41.7 %all-gather = f32[32,2,2560]{2,1,0:T(2,128)S(1)} all-gather(f32[1,2,2560]{2,1,0:T(2,128)S(1)} %bitcast.57), channel_id=1, replica_groups=mesh['walk'=4,'chol'=8] {'walk','chol'}, dimensions={0}, use_global_device_ids=true | all-gather | bytes 675840 | tf_op jit(solution)/shard_map/all_gather | solution.py:48
  185.6 0.5 reshape.58
  186.1 85.0 %all-reduce.3.cloned.1.call-done = f32[64,2560]{1,0:T(8,128)} async-done(((f32[64,2560]{1,0:T(8,128)}), f32[64,2560]{1,0:T(8,128)}) %all-reduce.3.cloned.1.call-update) | async-done | bytes 655376 | tf_op jit(solution)/shard_map/psum | solution.py:47
  271.1 58.9 %convolution_multiply_fusion = f32[64,8192]{1,0:T(8,128)S(1)} fusion(f32[2560,8192]{1,0:T(8,128)} %param.8, f32[64,2560]{1,0:T(8,128)S(1)} %reshape.58, f32[64,2560]{1,0:T(8,128)} %all-reduce.3.cloned.1.call-done), kind=kOutput, calls=%fused_computation.2 | convolution fusion | flops 16106979328 | bytes 87293952 | tf_op jit(solution)/shard_map/dot_general | solution.py:53
  330.0 2.3 all_to_all.29
  332.3 53.7 %all_to_all.35 = f32[32,2,8192]{2,1,0:T(2,128)S(1)} all-to-all(f32[32,2,8192]{2,1,0:T(2,128)} %all_to_all.29), channel_id=1, replica_groups=mesh['walk'=4,'chol'=8] {'walk','chol'}, dimensions={0} | all-to-all | bytes 4194304 | tf_op jit(solution)/shard_map/all_to_all | solution.py:56
  386.0 2.6 copy.28
  388.5 0.0 copy-start.1
  388.5 1.8 reshape.35
  390.3 0.0 copy-done.1
  390.3 2.2 fusion.15
  392.5 2.2 convolution_multiply_fusion.4
  394.7 2.2 convolution_multiply_fusion.3
  396.8 2.2 convolution_multiply_fusion.2
  399.0 0.0 copy-start.6
  399.0 0.0 copy-start.4
  399.0 0.0 copy-start.2
  399.0 0.0 copy-start.5
  399.0 2.9 fusion
  401.9 0.0 all-gather.3.cloned.1.call-update
  401.9 0.0 copy-done.6
  401.9 0.6 dynamic-slice
  403.2 0.0 copy-done.4
  403.2 0.0 copy-done.2
  403.2 0.1 broadcast_multiply_fusion
  403.3 0.1 fusion.12
  403.4 0.0 copy-done.5
  403.5 0.1 add_dynamic-update-slice_fusion
  403.6 13.9 %all-reduce = f32[16]{0:T(128)S(1)} all-reduce(f32[16]{0:T(128)S(1)} %add_dynamic-update-slice_fusion), channel_id=1, replica_groups=mesh['walk'=4,'chol'=8] {'chol'}, use_global_device_ids=true, to_apply=%add | all-reduce | flops 16 | bytes 128
  417.5 0.6 gather_fusion.1
  418.1 0.5 select_select_fusion.1
  418.6 10.3 %all-gather.3.cloned.1.call-done = f32[16,512,64]{1,2,0:T(8,128)} async-done(((f32[2,512,64]{1,2,0:T(8,128)}), f32[16,512,64]{1,2,0:T(8,128)}) %all-gather.3.cloned.1.call-update) | async-done | bytes 2097168 | tf_op jit(solution)/shard_map/all_gather | solution.py:67
  428.9 2.2 gather_fusion
  431.1 0.8 select_select_fusion
  (8 shorter events, 0.1 us)
Async XLA Ops:
  7.2 0.9 copy-start
  7.2 263.9 %all-reduce.3.cloned.1.call-start = ((), (), s32[]{:S(2)}) async-start(), calls=%async_computation.2 | async-start | bytes 1310720 | tf_op jit(solution)/shard_map/psum | solution.py:47
  57.0 86.9 %copy-start.3 = (f32[2,2560]{1,0:T(2,128)S(1)}, f32[2,2560]{1,0:T(2,128)}, u32[]{:S(2)}) copy-start(f32[2,2560]{1,0:T(2,128)} %param.9) | copy-start | bytes 61444
  143.9 285.1 %all-gather.3.cloned.1.call-start = ((), (), s32[]{:S(2)}) async-start(), calls=%async_computation.3 | async-start | bytes 2359296 | tf_op jit(solution)/shard_map/all_gather | solution.py:67
  388.5 1.8 copy-start.1
  399.0 3.0 copy-start.6
  399.0 4.2 copy-start.4
  399.0 4.2 copy-start.2
  399.0 4.4 %copy-start.5 = (f32[2]{0:T(128)S(1)}, f32[2]{0:T(128)}, u32[]{:S(2)}) copy-start(f32[2]{0:T(128)} %param.10) | copy-start | bytes 28
Sparse Core Ops, SparseCore 0:
  144.0 127.0 all-reduce.2
  402.0 26.8 all-gather.2
where the time goes:
time: 439 us
  matrix products  162 us (37%)
  blocking collectives  127 us (29%)
  waiting for transfers between devices  95.3 us (22%)
  other arithmetic  24.7 us (6%)
  between operations  15 us (3%)
  local copies, waits for them, and re-layouts  14.4 us (3%)
    dot_general x1, matrix products, per_device(): lax.dot_general(green_tiles, chol, (((1,), (1,)), ((), ())), precision=PR...  86.8 us
    psum x1, waiting for transfers between devices, per_device(): bias = lax.psum(partial_value, ('walk', 'chol'))  85 us
    dot_general x1, matrix products, per_device(): jnp.dot(fields, chol, precision=PRECISE, preferred_element_type=jnp.float32)  58.9 us
    all_to_all x1, blocking collectives, per_device(): lax.all_to_all(pot_tiles, ('walk', 'chol'), split_axis=0, concat_axis=1,...  53.7 us
    all_gather x1, blocking collectives, per_device(): lax.all_gather(field_noise, ('walk', 'chol'), axis=0, tiled=True)  41.7 us
    all_to_all x1, blocking collectives, per_device(): lax.all_to_all(rotated, ('walk', 'chol'), split_axis=1, concat_axis=0, ti...  17.5 us
    unnamed x1, blocking collectives  13.9 us
    another operation x4, other arithmetic, rotate(): factor = jnp.linalg.cholesky(normal)  11.9 us
  transfers between devices with their start and end apart: 2, of which 2 were waited for; matrix products, arithmetic and copies ran while one was open for 1% of the time, Pallas kernels for 0%

commit v1 on v0

v1 whole, which is shorter than its diff:
```python
import functools
import math

import jax
import jax.numpy as jnp
from jax import lax
from jax.experimental import pallas as pl
from jax.experimental.pallas import tpu as pltpu
from jax.sharding import PartitionSpec as P

TERMS = 6
PRECISE = lax.Precision.HIGHEST
TIME_ROOT = 0.1
BOTH = ("walk", "chol")
LANES = 128
SUBLANES = 8
F32 = jnp.float32
BF16 = jnp.bfloat16
VMEM_BYTES = 48 * 1024 * 1024


def params():
    return pltpu.CompilerParams(vmem_limit_bytes=VMEM_BYTES)


def whole(shape):
    zeros = (0,) * len(shape)
    return pl.BlockSpec(shape, lambda *_: zeros)


def dot(a, b):
    return jnp.dot(a, b, preferred_element_type=F32)


def dot_nt(a, b):
    return lax.dot_general(a, b, (((1,), (1,)), ((), ())), preferred_element_type=F32)


def split(x):
    high = x.astype(BF16)
    low = (x - high.astype(F32)).astype(BF16)
    return high, low


def rotate_kernel(devices, parent, weight, trial, walkers, noise, sent, pack):
    own, orbitals, occupied = walkers.shape
    half = orbitals // devices // 2
    rows = jax.lax.broadcasted_iota(jnp.int32, (occupied, 1), 0)
    state = []
    for s in range(own):
        crossed = lax.dot_general(
            walkers[s], trial[...], (((0,), (0,)), ((), ())),
            precision=PRECISE, preferred_element_type=F32,
        )
        normal = lax.dot_general(
            crossed, crossed, (((1,), (1,)), ((), ())),
            precision=PRECISE, preferred_element_type=F32,
        )
        state.append(jnp.concatenate([normal, crossed], axis=1))
    for k in range(occupied):
        for s in range(own):
            m = state[s]
            pivot = m[k : k + 1, :]
            scaled = pivot / m[k : k + 1, k : k + 1]
            state[s] = jnp.where(rows == k, scaled, m - m[:, k : k + 1] * scaled)
    lane = jax.lax.broadcasted_iota(jnp.int32, (SUBLANES, LANES), 1)
    extra = jnp.zeros((SUBLANES, LANES), F32)
    levels = jnp.zeros((SUBLANES, LANES), F32)
    for s in range(own):
        inverse = state[s][:, occupied:]
        rotated = jnp.dot(walkers[s], inverse, precision=PRECISE, preferred_element_type=F32)
        blocks = rotated.reshape(devices, 2, half, occupied)
        sent[:, s * half : (s + 1) * half, :] = jnp.concatenate([blocks[:, 0], blocks[:, 1]], axis=2)
        extra = jnp.where(lane == s, parent[s].astype(F32), extra)
        levels = jnp.where(lane == s, weight[s], levels)
        pack[:orbitals, s * occupied : (s + 1) * occupied] = walkers[s]
        width = noise.shape[1] // LANES
        for t in range(width):
            at = orbitals + s * width + t
            pack[at : at + 1, :] = noise[s : s + 1, t * LANES : (t + 1) * LANES]
    tail = sent.shape[1] - own * half
    sent[:, own * half :, :] = jnp.broadcast_to(extra[None, :tail], (devices, tail, LANES))
    first = pack.shape[0] - SUBLANES
    pack[first:, :] = levels


def rotate_plain(devices, parent, weight, trial, walkers, noise, sent_rows, pack_rows):
    own, orbitals, occupied = walkers.shape
    half = orbitals // devices // 2
    crossed = jnp.einsum("wmk,mn->wkn", walkers, trial, precision=PRECISE)
    normal = jnp.einsum("wkn,wln->wkl", crossed, crossed, precision=PRECISE)
    factor = jnp.linalg.cholesky(normal)
    inverse = jax.vmap(lambda f, c: jax.scipy.linalg.cho_solve((f, True), c))(factor, crossed)
    rotated = jnp.einsum("wmk,wkn->wmn", walkers, inverse, precision=PRECISE)
    sent = rotated.reshape(own, devices, 2, half, occupied).transpose(1, 0, 3, 2, 4)
    sent = sent.reshape(devices, own * half, 2 * occupied)
    extra = jnp.zeros((sent_rows - own * half, LANES), F32).at[0, :own].set(parent.astype(F32))
    sent = jnp.concatenate([sent, jnp.broadcast_to(extra[None], (devices,) + extra.shape)], axis=1)
    levels = jnp.zeros((SUBLANES, LANES), F32).at[0, :own].set(weight)
    pack = jnp.concatenate(
        [walkers.transpose(1, 0, 2).reshape(orbitals, own * occupied), noise.reshape(-1, LANES), levels], axis=0
    )
    return sent, pack


def rotate(devices, parent, weight, trial, walkers, noise):
    own, orbitals, occupied = walkers.shape
    half = orbitals // devices // 2
    sent_rows = -(-(own * half + 1) // SUBLANES) * SUBLANES
    pack_rows = orbitals + noise.size // LANES + SUBLANES
    if half % SUBLANES:
        return rotate_plain(devices, parent, weight, trial, walkers, noise, sent_rows, pack_rows)
    smem = pl.BlockSpec(memory_space=pltpu.SMEM)
    return pl.pallas_call(
        functools.partial(rotate_kernel, devices),
        out_shape=(
            jax.ShapeDtypeStruct((devices, sent_rows, LANES), F32),
            jax.ShapeDtypeStruct((pack_rows, LANES), F32),
        ),
        in_specs=[smem, smem] + [pl.BlockSpec(memory_space=pltpu.VMEM)] * 3,
        out_specs=(pl.BlockSpec(memory_space=pltpu.VMEM),) * 2,
        compiler_params=params(),
    )(parent, weight, trial, walkers, noise)


def contract_kernel(trial, chol, out):
    orbitals, occupied = trial.shape
    half = chol.shape[1] // orbitals // 2
    high, low = split(trial[...])
    pair = jnp.concatenate([high, low], axis=1)
    alone = jnp.concatenate([high, jnp.zeros_like(high)], axis=1)
    lane = jax.lax.broadcasted_iota(jnp.int32, (1, 2 * occupied), 1)

    def one(i):
        chol_high, chol_low = split(chol[:, i * orbitals : (i + 1) * orbitals])
        both = dot(chol_high, pair) + dot(chol_low, alone)
        return both + pltpu.roll(both, occupied, 1)

    for i in range(half):
        out[:, i * 2 * occupied : (i + 1) * 2 * occupied] = jnp.where(lane < occupied, one(i), one(i + half))


def contract(trial, chol):
    vectors, pairs = chol.shape
    orbitals, occupied = trial.shape
    columns = pairs // orbitals * occupied
    block = 128
    return pl.pallas_call(
        contract_kernel,
        grid=(vectors // block,),
        out_shape=jax.ShapeDtypeStruct((vectors, columns), F32),
        in_specs=[whole(trial.shape), pl.BlockSpec((block, pairs), lambda g: (g, 0))],
        out_specs=pl.BlockSpec((block, columns), lambda g: (g, 0)),
        compiler_params=params(),
        cost_estimate=pl.CostEstimate(
            flops=2 * vectors * pairs * occupied * 3, bytes_accessed=4 * vectors * (pairs + columns), transcendentals=0
        ),
    )(trial, chol)


def bias_kernel(own, half, place, rotated, contracted, noise, out, high, low):
    devices = rotated.shape[0]

    @pl.when(pl.program_id(0) == 0)
    def _():
        for i in range(half):
            for s in range(own):
                part = rotated[:, s * half + i, :]
                part_high, part_low = split(part)
                high[s * devices : (s + 1) * devices, i * LANES : (i + 1) * LANES] = part_high
                low[s * devices : (s + 1) * devices, i * LANES : (i + 1) * LANES] = part_low

    b_high, b_low = split(contracted[...])
    bias = dot_nt(high[...], b_high) + dot_nt(low[...], b_high) + dot_nt(high[...], b_low)
    rows = jax.lax.broadcasted_iota(jnp.int32, (out.shape[0], 1), 0)
    value = -TIME_ROOT * bias
    for s in range(own):
        value += jnp.where(rows == s * devices + place[0], noise[s : s + 1, :], 0.0)
    out[...] = value


def partial_fields(own, half, place, rotated, contracted, noise):
    vectors, columns = contracted.shape
    devices = rotated.shape[0]
    block = 512
    return pl.pallas_call(
        functools.partial(bias_kernel, own, half),
        grid=(vectors // block,),
        out_shape=jax.ShapeDtypeStruct((own * devices, vectors), F32),
        in_specs=[
            pl.BlockSpec(memory_space=pltpu.SMEM),
            whole(rotated.shape),
            pl.BlockSpec((block, columns), lambda g: (g, 0)),
            pl.BlockSpec((own, block), lambda g: (0, g)),
        ],
        out_specs=pl.BlockSpec((own * devices, block), lambda g: (0, g)),
        scratch_shapes=[pltpu.VMEM((own * devices, columns), BF16)] * 2,
        compiler_params=params(),
    )(place, rotated, contracted, noise)


def send(x, walk_size, chol_size, target):
    return lax.ppermute(x, BOTH, [(i, target(i)) for i in range(walk_size * chol_size)])


def sum_everywhere(x, walk_size, chol_size):
    walk = lax.axis_index("walk")
    core = lax.axis_index("chol") % 2
    half = x.shape[0] // 2
    quarter = half // walk_size
    mine = lax.dynamic_slice_in_dim(x, core * half, half, 0)
    other = lax.dynamic_slice_in_dim(x, (1 - core) * half, half, 0)
    chip = mine + send(other, walk_size, chol_size, lambda i: i ^ 1)
    total = lax.dynamic_slice_in_dim(chip, walk * quarter, quarter, 0)
    got = [
        send(
            lax.dynamic_slice_in_dim(chip, (walk ^ r) * quarter, quarter, 0),
            walk_size, chol_size, lambda i, r=r: i ^ (r * chol_size),
        )
        for r in range(1, walk_size)
    ]
    for g in got:
        total = total + g
    got = [send(total, walk_size, chol_size, lambda i, r=r: i ^ (2 * r)) for r in range(1, chol_size // 2)]
    for g in got:
        total = total + g
    blocks = [total] + [
        send(total, walk_size, chol_size, lambda i, r=r: i ^ (r * chol_size)) for r in range(1, walk_size)
    ]
    here = jnp.concatenate(blocks, axis=0)
    there = send(here, walk_size, chol_size, lambda i: i ^ 1)
    return jnp.concatenate([here, there], axis=0)


def row_of(walker, own, walk_size, chol_size):
    everyone = own * walk_size * chol_size
    walk = lax.axis_index("walk")
    core = lax.axis_index("chol") % 2
    row = (walker % own) * (walk_size * chol_size) + walker // own
    half = everyone // 2
    quarter = half // walk_size
    inside = row % half
    return ((row // half) ^ core) * half + ((inside // quarter) ^ walk) * quarter + inside % quarter


def select_kernel(rows, fields, out):
    slots = fields.shape[0]
    lane = jax.lax.broadcasted_iota(jnp.int32, (slots, slots), 1)
    pick = jnp.where(lane == rows[...], 1.0, 0.0).astype(BF16)
    value = fields[...]
    first, rest = split(value)
    second, third = split(value - first.astype(F32))
    picked = dot(pick, first) + dot(pick, second) + dot(pick, third)
    high, low = split(TIME_ROOT * picked)
    out[:slots, :] = high
    out[slots:, :] = low


def select(rows, fields):
    slots, vectors = fields.shape
    block = 512
    return pl.pallas_call(
        select_kernel,
        grid=(vectors // block,),
        out_shape=jax.ShapeDtypeStruct((2 * slots, vectors), BF16),
        in_specs=[whole((slots, 1)), pl.BlockSpec((slots, block), lambda g: (0, g))],
        out_specs=pl.BlockSpec((2 * slots, block), lambda g: (0, g)),
        compiler_params=params(),
    )(rows.reshape(slots, 1), fields)


def potential_kernel(count, fields, chol, out):
    slots = fields.shape[0] // 2
    vectors = chol.shape[0]
    step = 512
    total = None
    for k in range(0, vectors, step):
        high, low = split(chol[k : k + step, :])
        both = dot(fields[:, k : k + step], high)
        value = both[:slots] + both[slots:] + dot(fields[:slots, k : k + step], low)
        total = value if total is None else total + value
    pieces = chol.shape[1] // LANES
    for t in range(pieces):
        at = pl.ds(t * count + pl.program_id(0), slots, stride=pieces * count)
        out[at, :] = total[:, t * LANES : (t + 1) * LANES]


def potential_tiles(fields, chol, orbitals, first, count):
    vectors = chol.shape[0]
    slots = fields.shape[0] // 2
    return pl.pallas_call(
        functools.partial(potential_kernel, count),
        grid=(count,),
        out_shape=jax.ShapeDtypeStruct((slots * count * orbitals // LANES, LANES), F32),
        in_specs=[whole(fields.shape), pl.BlockSpec((vectors, orbitals), lambda i: (0, first + i))],
        out_specs=whole((slots * count * orbitals // LANES, LANES)),
        compiler_params=params(),
        cost_estimate=pl.CostEstimate(
            flops=2 * slots * vectors * orbitals * count * 3,
            bytes_accessed=4 * vectors * orbitals * count,
            transcendentals=0,
        ),
    )(fields, chol)


def taylor_kernel(own, chunks, index, *refs):
    starts = refs[:own]
    tiles = refs[own : own + chunks]
    out = refs[own + chunks]
    high, low, term = refs[own + chunks + 1 :]
    orbitals, width = term.shape
    occupied = width // own
    pieces = orbitals // LANES
    devices = tiles[0].shape[0]
    count = tiles[0].shape[1] // (own * pieces)
    lane = jax.lax.broadcasted_iota(jnp.int32, (1, width), 1) // occupied
    rows = devices * own * count
    for c in range(chunks):
        for t in range(pieces):
            value = tiles[c][...].reshape(devices * own, pieces, count, LANES)[:, t].reshape(rows, LANES)
            value_high, value_low = split(value)
            high[c * rows : (c + 1) * rows, t * LANES : (t + 1) * LANES] = value_high
            low[c * rows : (c + 1) * rows, t * LANES : (t + 1) * LANES] = value_low
    total = jnp.zeros((orbitals, width), F32)
    for s in range(own):
        source = starts[s][0]
        inside = index[own + s]
        moved = source
        for shift in range(1, own):
            rolled = pltpu.roll(source, shift * occupied, 1)
            moved = jnp.where((inside + shift) % own == s, rolled, moved)
        total = jnp.where(lane == s, moved, total)
    term[...] = total
    for order in range(1, TERMS):
        term_high, term_low = split(term[...])
        pair = jnp.concatenate([term_high, term_low], axis=1)
        both = dot(high[...], pair)
        value = both[:, :width] + both[:, width:] + dot(low[...], term_high)
        value = value.reshape(chunks, devices, own, count, width)
        picked = value[:, :, 0]
        for s in range(1, own):
            picked = jnp.where(lane == s, value[:, :, s], picked)
        picked = picked / order
        placed = jnp.stack([picked[c] for c in range(chunks)], axis=1).reshape(orbitals, width)
        term[...] = placed
        total = total + placed
    for s in range(own):
        out[s] = total[:, s * occupied : (s + 1) * occupied]


def taylor_plain(index, gathered, tiles, own, orbitals, occupied):
    pieces = orbitals // LANES
    devices = tiles[0].shape[0]
    parts = [t.reshape(devices, own, pieces, -1, LANES).transpose(1, 0, 3, 2, 4) for t in tiles]
    potential = jnp.concatenate(parts, axis=2).reshape(own, orbitals, orbitals)
    picked = gathered[index[:own], :orbitals].reshape(own, orbitals, own, occupied)
    term = jnp.take_along_axis(picked, index[own:].reshape(own, 1, 1, 1), axis=2)[:, :, 0]
    running = term
    for order in range(1, TERMS):
        term = jnp.einsum("wij,wjn->win", potential, term, precision=PRECISE) / order
        running = running + term
    return running


def taylor(index, gathered, tiles, own, orbitals, occupied):
    width = own * occupied
    chunks = len(tiles)
    pieces = orbitals // LANES
    if (tiles[0].shape[1] // (own * pieces)) % SUBLANES:
        return taylor_plain(index, gathered, tiles, own, orbitals, occupied)
    rows = sum(t.shape[0] * t.shape[1] for t in tiles) // pieces

    def at(s):
        return pl.BlockSpec((1, orbitals, width), lambda i, index: (index[s], 0, 0))

    return pl.pallas_call(
        functools.partial(taylor_kernel, own, chunks),
        grid_spec=pltpu.PrefetchScalarGridSpec(
            num_scalar_prefetch=1,
            grid=(1,),
            in_specs=[at(s) for s in range(own)] + [whole(t.shape) for t in tiles],
            out_specs=whole((own, orbitals, occupied)),
            scratch_shapes=[
                pltpu.VMEM((rows, orbitals), BF16),
                pltpu.VMEM((rows, orbitals), BF16),
                pltpu.VMEM((orbitals, width), F32),
            ],
        ),
        out_shape=jax.ShapeDtypeStruct((own, orbitals, occupied), F32),
        compiler_params=params(),
    )(index, *[gathered] * own, *tiles)


def per_device(trial, walkers, chol, field_noise, log_weight, parent):
    own, orbitals, occupied = walkers.shape
    walk_size = lax.axis_size("walk")
    chol_size = lax.axis_size("chol")
    devices = walk_size * chol_size
    vectors, pairs = chol.shape
    rows_here = pairs // orbitals
    half = rows_here // 2
    place = lax.axis_index(BOTH)

    sent, pack = rotate(devices, parent, log_weight, trial, walkers, field_noise)
    rotated = lax.all_to_all(sent, BOTH, split_axis=0, concat_axis=0, tiled=True)
    gathered = lax.all_gather(pack, "chol", axis=0, tiled=False)
    contracted = contract(trial, chol)
    mine = partial_fields(own, half, place.reshape(1), rotated, contracted, field_noise)
    fields = sum_everywhere(mine, walk_size, chol_size)

    parents = rotated[:, own * half, :own].reshape(own * devices).astype(jnp.int32)
    parent_rows = row_of(parents, own, walk_size, chol_size)
    scaled = select(parent_rows, fields)

    count = math.gcd(rows_here, SUBLANES)
    tiles = []
    for first in range(0, rows_here, count):
        chunk = potential_tiles(scaled, chol, orbitals, first, count)
        chunk = chunk.reshape(devices, own * count * orbitals // LANES, LANES)
        tiles.append(lax.all_to_all(chunk, BOTH, split_axis=0, concat_axis=0, tiled=True))

    local = parent - lax.axis_index("walk") * (own * chol_size)
    source, inside = local // own, local % own
    new_walkers = taylor(
        jnp.concatenate([source, inside]), gathered, tiles, own, orbitals, occupied
    )

    width = vectors // LANES
    notes = gathered[:, orbitals : orbitals + own * width, :].reshape(own * chol_size, vectors)
    parent_noise = jnp.take(notes, local, axis=0)
    parent_level = jnp.take(gathered[:, -SUBLANES, :own].reshape(own * chol_size), local, axis=0)
    parent_fields = jnp.take(fields, row_of(parent, own, walk_size, chol_size), axis=0)
    shift = parent_noise - parent_fields
    new_log_weight = parent_level + jnp.sum(0.5 * shift * shift - parent_noise * shift, axis=1)
    return (new_walkers, new_log_weight)


def solution(mesh):
    return jax.shard_map(
        per_device,
        mesh=mesh,
        in_specs=(
            P(),
            P(BOTH, None, None),
            P(None, BOTH),
            P(BOTH, None),
            P(BOTH),
            P(BOTH),
        ),
        out_specs=(P(BOTH, None, None), P(BOTH)),
        check_vma=False,
    )
```

time: 439 us -> 211 us (0.48)
  matrix products: 162 us -> 0 us
  blocking collectives: 127 us -> 0 us
  Pallas kernels: 0 us -> 99.5 us
  waiting for transfers between devices: 95.3 us -> 51.3 us
  starting transfers between devices: 0.08 us -> 33 us
  other arithmetic: 24.7 us -> 1.12 us
    dot_general x11 -> x0, matrix products: 162 us -> none  [the longest x1 86.8 us: per_device(): lax.dot_general(green_tiles, chol, (((1,), (1,)), ((), ())), precision=PR...]
    pallas_call x0 -> x7, Pallas kernels: none -> 99.5 us  [the longest x1 41.4 us: contract(): pl.pallas_call(contract_kernel, grid=(vectors // block,), out_shape=jax.S...]
    psum x1 -> x0, waiting for transfers between devices: 85 us -> none  [per_device(): bias = lax.psum(partial_value, ('walk', 'chol'))]
    all_to_all x2 -> x0, blocking collectives: 71.2 us -> none  [the longest x1 53.7 us: per_device(): lax.all_to_all(pot_tiles, ('walk', 'chol'), split_axis=0, concat_axis=1,...]
    all_gather x1 -> x0, blocking collectives: 41.7 us -> none  [per_device(): lax.all_gather(field_noise, ('walk', 'chol'), axis=0, tiled=True)]
    all_to_all x0 -> x3, waiting for transfers between devices: none -> 33.4 us  [the longest x2 33.4 us: per_device(): lax.all_to_all(chunk, BOTH, split_axis=0, concat_axis=0, tiled=True)]
    another operation x7 -> x0, other arithmetic: 21.8 us -> none  [the longest x4 11.9 us: rotate(): factor = jnp.linalg.cholesky(normal)]
    all_to_all x0 -> x3, starting transfers between devices: none -> 21 us  [the longest x2 13.7 us: per_device(): lax.all_to_all(chunk, BOTH, split_axis=0, concat_axis=0, tiled=True)]
  transfers between devices with their start and end apart: 2 -> 15, of which waited for: 2 -> 12; matrix products, arithmetic and copies ran while one was open for 1% -> 2% of each run, Pallas kernels for 0% -> 37%
where the time goes in v1:
time: 211 us; the launch traced here: 210 us
  Pallas kernels  99.5 us (47%)
  waiting for transfers between devices  51.3 us (24%)
  starting transfers between devices  33 us (16%)
  between operations  14.3 us (7%)
  local copies, waits for them, and re-layouts  10.5 us (5%)
    pallas_call x1, Pallas kernels, contract(): pl.pallas_call(contract_kernel, grid=(vectors // block,), out_shape=jax.S...  41.4 us
    pallas_call x2, Pallas kernels, potential_tiles(): pl.pallas_call(functools.partial(potential_kernel, count), grid=(count,),...  35.7 us
    all_to_all x2, waiting for transfers between devices, per_device(): lax.all_to_all(chunk, BOTH, split_axis=0, concat_axis=0, tiled=True)  33.4 us
    ppermute x11, waiting for transfers between devices, send(): lax.ppermute(x, BOTH, [(i, target(i)) for i in range(walk_size * chol_siz...  17.9 us
    all_to_all x2, starting transfers between devices, per_device(): lax.all_to_all(chunk, BOTH, split_axis=0, concat_axis=0, tiled=True)  13.7 us
    ppermute x11, starting transfers between devices, send(): lax.ppermute(x, BOTH, [(i, target(i)) for i in range(walk_size * chol_siz...  11.9 us
    pallas_call x1, Pallas kernels, partial_fields(): pl.pallas_call(functools.partial(bias_kernel, own, half), grid=(vectors /...  8.77 us
    pallas_call x1, Pallas kernels, rotate(): pl.pallas_call(functools.partial(rotate_kernel, devices), out_shape=(jax....  8.27 us
  transfers between devices with their start and end apart: 15, of which 12 were waited for; matrix products, arithmetic and copies ran while one was open for 2% of the time, Pallas kernels for 37%

profile of v1, /device:TPU:0, one launch (start us, length us, event | category | flops | bytes accessed | tf_op | source)
XLA Modules:
  0.0 209.8 jit_solution(200640004023772750)
XLA Ops:
  7.2 1.0 copy.24.trial
  8.2 1.1 copy.25.walkers
  9.4 0.0 copy-start.1
  9.4 0.7 copy-done.1
  10.1 0.0 copy-start.3
  10.1 0.7 copy-done.3
  10.7 0.0 copy-start.5
  10.7 0.7 copy-done.5
  11.4 8.3 %shard_map.77 = (f32[32,24,128]{2,1,0:T(8,128)}, f32[560,128]{1,0:T(8,128)}) custom-call(s32[2]{0:T(128)S(1)} %copy-done.3, f32[2]{0:T(128)S(1)} %copy-done.5, f32[512,64]{1,0:T(8,128)S(1)} %copy.24.trial, f32[2,512,64]{2,1,0:T(8,128)S(1)} %copy.25.walkers, f32[2,2560]{1,0:T(2,128)S(1)} %copy-done.1), custom_call_target="tpu_custom_call" | custom-call | tf_op jit(solution)/shard_map/pallas_call | solution.py:114
  19.7 7.3 %all-to-all-start = ((f32[32,24,128]{2,1,0:T(8,128)}), f32[32,24,128]{2,1,0:T(8,128)S(1)}, u32[]{:S(2)}, u32[]{:S(2)}) async-start(f32[32,24,128]{2,1,0:T(8,128)} %get-tuple-element.5), calls=%async_computation | async-start | bytes 786432 | tf_op jit(solution)/shard_map/all_to_all | solution.py:405
  27.0 0.0 all-gather.3.cloned.1.call-start
  27.0 0.0 copy-start.2
  27.1 41.4 %shard_map.78.contracted = f32[2560,1024]{1,0:T(8,128)} custom-call(f32[512,64]{1,0:T(8,128)S(1)} %copy.24.trial, f32[2560,8192]{1,0:T(8,128)} %chol.5), custom_call_target="tpu_custom_call" | custom-call | flops 8053063680 | bytes 94371840 | tf_op jit(solution)/shard_map/pallas_call | solution.py:148
  68.4 0.0 all-to-all-done.rotated
  68.4 0.0 copy-done.2
  68.4 8.8 %shard_map.79 = f32[64,2560]{1,0:T(8,128)S(1)} custom-call(s32[1]{0:T(128)} %bitcast.1.place, f32[32,24,128]{2,1,0:T(8,128)S(1)} %all-to-all-done.rotated, f32[2560,1024]{1,0:T(8,128)} %shard_map.78.contracted, f32[2,2560]{1,0:T(2,128)S(1)} %copy-done.2), custom_call_target="tpu_custom_call" | custom-call | tf_op jit(solution)/shard_map/pallas_call | solution.py:186
  77.3 0.3 collective-permute-start
  77.6 1.4 collective-permute-done
  79.0 1.8 collective-permute-start.1
  80.9 1.5 collective-permute-start.2
  82.3 0.3 collective-permute-start.3
  82.6 0.0 all-gather.3.cloned.1.call-update
  82.6 1.1 collective-permute-done.1
  83.7 2.4 %collective-permute-done.2 = f32[8,2560]{1,0:T(8,128)S(1)} collective-permute-done((f32[8,2560]{1,0:T(8,128)S(1)}, f32[8,2560]{1,0:T(8,128)S(1)}, u32[]{:S(2)}, u32[]{:S(2)}) %collective-permute-start.2) | collective-permute-done | bytes 81952 | tf_op jit(solution)/shard_map/ppermute | solution.py:203
  86.1 1.6 collective-permute-done.3
  87.7 1.5 collective-permute-start.4
  89.2 2.4 %collective-permute-start.5 = (f32[8,2560]{1,0:T(8,128)S(1)}, f32[8,2560]{1,0:T(8,128)S(1)}, u32[]{:S(2)}, u32[]{:S(2)}) collective-permute-start(f32[8,2560]{1,0:T(8,128)S(1)} %add_add_fusion.1), channel_id=1, source_target_pairs={{0,4},{1,5},{2,6},{3,7},{4,0},{5,1},{6,2},{7,3},{8,12},{9,13},{10,... | collective-permute-start | bytes 245768 | tf_op jit(solution)/shard_map/ppermute | solution.py:203
  91.7 0.5 collective-permute-start.6
  92.2 0.1 fusion.20
  92.2 0.1 convert_element_type.15
  92.3 0.2 collective-permute-done.4
  92.5 7.2 %collective-permute-done.5 = f32[8,2560]{1,0:T(8,128)S(1)} collective-permute-done((f32[8,2560]{1,0:T(8,128)S(1)}, f32[8,2560]{1,0:T(8,128)S(1)}, u32[]{:S(2)}, u32[]{:S(2)}) %collective-permute-start.5) | collective-permute-done | bytes 81952 | tf_op jit(solution)/shard_map/ppermute | solution.py:203
  99.7 0.0 collective-permute-done.6
  99.7 0.6 collective-permute-start.7
  100.3 0.2 collective-permute-start.8
  100.5 2.7 %collective-permute-start.9 = (f32[8,2560]{1,0:T(8,128)S(1)}, f32[8,2560]{1,0:T(8,128)S(1)}, u32[]{:S(2)}, u32[]{:S(2)}) collective-permute-start(f32[8,2560]{1,0:T(8,128)S(1)} %get-tuple-element.17), channel_id=1, source_target_pairs={{0,24},{1,25},{2,26},{3,27},{4,28},{5,29},{6,30},{7,31},{8,16},{9,... | collective-permute-start | bytes 245768 | tf_op jit(solution)/shard_map/ppermute | solution.py:203
  103.3 0.1 fusion.5.rows
  103.4 0.8 collective-permute-done.7
  104.2 0.5 collective-permute-done.8
  104.7 1.1 collective-permute-done.9
  105.9 0.1 collective-permute-start.10
  106.0 1.6 collective-permute-done.10
  107.6 1.4 shard_map.80.fields
  109.1 17.9 %shard_map.81 = f32[2048,128]{1,0:T(8,128)} custom-call(bf16[128,2560]{1,0:T(8,128)(2,1)S(1)} %shard_map.80.fields, f32[2560,8192]{1,0:T(8,128)} %chol.5), custom_call_target="tpu_custom_call" | custom-call | flops 4026531840 | bytes 41943040 | tf_op jit(solution)/shard_map/pallas_call | solution.py:291
  127.0 10.9 %all-to-all-start.1 = ((f32[32,64,128]{2,1,0:T(8,128)}), f32[32,64,128]{2,1,0:T(8,128)S(1)}, u32[]{:S(2)}, u32[]{:S(2)}) async-start(f32[32,64,128]{2,1,0:T(8,128)} %bitcast.2), calls=%async_computation.1 | async-start | bytes 2097152 | tf_op jit(solution)/shard_map/all_to_all | solution.py:420
  137.9 0.0 copy-start.4
  137.9 17.8 %shard_map.82 = f32[2048,128]{1,0:T(8,128)} custom-call(bf16[128,2560]{1,0:T(8,128)(2,1)S(1)} %shard_map.80.fields, f32[2560,8192]{1,0:T(8,128)} %chol.5), custom_call_target="tpu_custom_call" | custom-call | flops 4026531840 | bytes 41943040 | tf_op jit(solution)/shard_map/pallas_call | solution.py:291
  155.7 9.8 %all-to-all-done.1.refs_2_ = f32[32,64,128]{2,1,0:T(8,128)S(1)} async-done(((f32[32,64,128]{2,1,0:T(8,128)}), f32[32,64,128]{2,1,0:T(8,128)S(1)}, u32[]{:S(2)}, u32[]{:S(2)}) %all-to-all-start.1) | async-done | bytes 1048608 | tf_op jit(solution)/shard_map/all_to_all | solution.py:420
  165.5 2.8 %all-to-all-start.2 = ((f32[32,64,128]{2,1,0:T(8,128)}), f32[32,64,128]{2,1,0:T(8,128)S(1)}, u32[]{:S(2)}, u32[]{:S(2)}) async-start(f32[32,64,128]{2,1,0:T(8,128)} %bitcast.3), calls=%async_computation.2 | async-start | bytes 2097152 | tf_op jit(solution)/shard_map/all_to_all | solution.py:420
  168.3 0.0 copy-done.4
  168.3 0.1 pad_add_fusion.index
  168.5 0.6 gather_fusion.2
  169.0 0.0 all-gather.3.cloned.1.call-done
  169.1 0.9 slice.20
  170.0 0.8 slice_reduce_fusion
  170.8 0.1 reshape_squeeze.4
  170.9 0.6 gather_fusion.1
  171.5 0.6 gather_fusion
  172.1 23.6 %all-to-all-done.2.refs_3_ = f32[32,64,128]{2,1,0:T(8,128)S(1)} async-done(((f32[32,64,128]{2,1,0:T(8,128)}), f32[32,64,128]{2,1,0:T(8,128)S(1)}, u32[]{:S(2)}, u32[]{:S(2)}) %all-to-all-start.2) | async-done | bytes 1048608 | tf_op jit(solution)/shard_map/all_to_all | solution.py:420
  195.7 1.6 copy-done
  197.4 4.0 %shard_map.83 = f32[2,512,64]{2,1,0:T(8,128)S(1)} custom-call(s32[4]{0:T(128)S(1)} %pad_add_fusion.index, f32[8,560,128]{2,1,0:T(8,128)S(1)} %bitcast.6, f32[8,560,128]{2,1,0:T(8,128)S(1)} %bitcast.7, f32[32,64,128]{2,1,0:T(8,128)S(1)} %all-to-all-done.1.refs_2_, f32[32,64,128]{2,1,0:T(8,128)S(1)} %all-to-all-done.2.refs_3_), custom_call_target="tpu_custom_call" | custom-call | tf_op jit(solution)/shard_map/pallas_call | solution.py:376
  201.3 0.9 copy.32
  202.2 0.2 fusion.19
  202.4 0.5 select_add_fusion
  (17 shorter events, 0.3 us)
Async XLA Ops:
  9.4 0.7 copy-start.1
  10.1 0.7 copy-start.3
  10.7 0.7 copy-start.5
  19.7 48.8 %all-to-all-start = ((f32[32,24,128]{2,1,0:T(8,128)}), f32[32,24,128]{2,1,0:T(8,128)S(1)}, u32[]{:S(2)}, u32[]{:S(2)}) async-start(f32[32,24,128]{2,1,0:T(8,128)} %get-tuple-element.5), calls=%async_computation | async-start | bytes 786432 | tf_op jit(solution)/shard_map/all_to_all | solution.py:405
  27.0 142.1 %all-gather.3.cloned.1.call-start = ((), (), s32[]{:S(2)}) async-start(), calls=%async_computation.3 | async-start | bytes 2580480 | tf_op jit(solution)/shard_map/all_gather | solution.py:406
  27.0 41.4 %copy-start.2 = (f32[2,2560]{1,0:T(2,128)S(1)}, f32[2,2560]{1,0:T(2,128)}, u32[]{:S(2)}) copy-start(f32[2,2560]{1,0:T(2,128)} %noise.3) | copy-start | bytes 61444
  77.3 1.7 collective-permute-start
  79.0 4.7 %collective-permute-start.1 = (f32[8,2560]{1,0:T(8,128)S(1)}, f32[8,2560]{1,0:T(8,128)S(1)}, u32[]{:S(2)}, u32[]{:S(2)}) collective-permute-start(f32[8,2560]{1,0:T(8,128)S(1)} %get-tuple-element.20), channel_id=1, source_target_pairs={{0,8},{1,9},{2,10},{3,11},{4,12},{5,13},{6,14},{7,15},{8,0},{9,1},... | collective-permute-start | bytes 245768 | tf_op jit(solution)/shard_map/ppermute | solution.py:203
  80.9 5.2 %collective-permute-start.2 = (f32[8,2560]{1,0:T(8,128)S(1)}, f32[8,2560]{1,0:T(8,128)S(1)}, u32[]{:S(2)}, u32[]{:S(2)}) collective-permute-start(f32[8,2560]{1,0:T(8,128)S(1)} %get-tuple-element.22), channel_id=1, source_target_pairs={{0,16},{1,17},{2,18},{3,19},{4,20},{5,21},{6,22},{7,23},{8,24},{9,... | collective-permute-start | bytes 245768 | tf_op jit(solution)/shard_map/ppermute | solution.py:203
  82.3 5.3 %collective-permute-start.3 = (f32[8,2560]{1,0:T(8,128)S(1)}, f32[8,2560]{1,0:T(8,128)S(1)}, u32[]{:S(2)}, u32[]{:S(2)}) collective-permute-start(f32[8,2560]{1,0:T(8,128)S(1)} %get-tuple-element.21), channel_id=1, source_target_pairs={{0,24},{1,25},{2,26},{3,27},{4,28},{5,29},{6,30},{7,31},{8,16},{9,... | collective-permute-start | bytes 245768 | tf_op jit(solution)/shard_map/ppermute | solution.py:203
  87.7 4.8 %collective-permute-start.4 = (f32[8,2560]{1,0:T(8,128)S(1)}, f32[8,2560]{1,0:T(8,128)S(1)}, u32[]{:S(2)}, u32[]{:S(2)}) collective-permute-start(f32[8,2560]{1,0:T(8,128)S(1)} %add_add_fusion.1), channel_id=1, source_target_pairs={{0,2},{1,3},{2,0},{3,1},{4,6},{5,7},{6,4},{7,5},{8,10},{9,11},{10,... | collective-permute-start | bytes 245768 | tf_op jit(solution)/shard_map/ppermute | solution.py:203
  89.2 10.4 %collective-permute-start.5 = (f32[8,2560]{1,0:T(8,128)S(1)}, f32[8,2560]{1,0:T(8,128)S(1)}, u32[]{:S(2)}, u32[]{:S(2)}) collective-permute-start(f32[8,2560]{1,0:T(8,128)S(1)} %add_add_fusion.1), channel_id=1, source_target_pairs={{0,4},{1,5},{2,6},{3,7},{4,0},{5,1},{6,2},{7,3},{8,12},{9,13},{10,... | collective-permute-start | bytes 245768 | tf_op jit(solution)/shard_map/ppermute | solution.py:203
  91.7 8.0 %collective-permute-start.6 = (f32[8,2560]{1,0:T(8,128)S(1)}, f32[8,2560]{1,0:T(8,128)S(1)}, u32[]{:S(2)}, u32[]{:S(2)}) collective-permute-start(f32[8,2560]{1,0:T(8,128)S(1)} %add_add_fusion.1), channel_id=1, source_target_pairs={{0,6},{1,7},{2,4},{3,5},{4,2},{5,3},{6,0},{7,1},{8,14},{9,15},{10,... | collective-permute-start | bytes 245768 | tf_op jit(solution)/shard_map/ppermute | solution.py:203
  99.7 4.5 %collective-permute-start.7 = (f32[8,2560]{1,0:T(8,128)S(1)}, f32[8,2560]{1,0:T(8,128)S(1)}, u32[]{:S(2)}, u32[]{:S(2)}) collective-permute-start(f32[8,2560]{1,0:T(8,128)S(1)} %get-tuple-element.17), channel_id=1, source_target_pairs={{0,8},{1,9},{2,10},{3,11},{4,12},{5,13},{6,14},{7,15},{8,0},{9,1},... | collective-permute-start | bytes 245768 | tf_op jit(solution)/shard_map/ppermute | solution.py:203
  100.3 4.4 %collective-permute-start.8 = (f32[8,2560]{1,0:T(8,128)S(1)}, f32[8,2560]{1,0:T(8,128)S(1)}, u32[]{:S(2)}, u32[]{:S(2)}) collective-permute-start(f32[8,2560]{1,0:T(8,128)S(1)} %get-tuple-element.17), channel_id=1, source_target_pairs={{0,16},{1,17},{2,18},{3,19},{4,20},{5,21},{6,22},{7,23},{8,24},{9,... | collective-permute-start | bytes 245768 | tf_op jit(solution)/shard_map/ppermute | solution.py:203
  100.5 5.3 %collective-permute-start.9 = (f32[8,2560]{1,0:T(8,128)S(1)}, f32[8,2560]{1,0:T(8,128)S(1)}, u32[]{:S(2)}, u32[]{:S(2)}) collective-permute-start(f32[8,2560]{1,0:T(8,128)S(1)} %get-tuple-element.17), channel_id=1, source_target_pairs={{0,24},{1,25},{2,26},{3,27},{4,28},{5,29},{6,30},{7,31},{8,16},{9,... | collective-permute-start | bytes 245768 | tf_op jit(solution)/shard_map/ppermute | solution.py:203
  105.9 1.7 collective-permute-start.10
  127.0 38.5 %all-to-all-start.1 = ((f32[32,64,128]{2,1,0:T(8,128)}), f32[32,64,128]{2,1,0:T(8,128)S(1)}, u32[]{:S(2)}, u32[]{:S(2)}) async-start(f32[32,64,128]{2,1,0:T(8,128)} %bitcast.2), calls=%async_computation.1 | async-start | bytes 2097152 | tf_op jit(solution)/shard_map/all_to_all | solution.py:420
  137.9 30.4 %copy-start.4 = (s32[2]{0:T(128)S(1)}, s32[2]{0:T(128)}, u32[]{:S(2)}) copy-start(s32[2]{0:T(128)} %parent.1) | copy-start | bytes 28
  165.5 30.2 %all-to-all-start.2 = ((f32[32,64,128]{2,1,0:T(8,128)}), f32[32,64,128]{2,1,0:T(8,128)S(1)}, u32[]{:S(2)}, u32[]{:S(2)}) async-start(f32[32,64,128]{2,1,0:T(8,128)} %bitcast.3), calls=%async_computation.2 | async-start | bytes 2097152 | tf_op jit(solution)/shard_map/all_to_all | solution.py:420
  195.7 1.6 copy-start
Sparse Core Ops, SparseCore 0:
  82.7 35.2 all-gather.2

commit v2 on v1

v2 whole, which is shorter than its diff:
```python
import functools

import jax
import jax.numpy as jnp
from jax import lax
from jax.experimental import pallas as pl
from jax.experimental.pallas import tpu as pltpu
from jax.sharding import PartitionSpec as P

TERMS = 6
PRECISE = lax.Precision.HIGHEST
TIME_ROOT = 0.1
BOTH = ("walk", "chol")
LANES = 128
SUBLANES = 8
F32 = jnp.float32
BF16 = jnp.bfloat16
MIB = 1024 * 1024
FIRST_UNITS = 1


def params(mib):
    return pltpu.CompilerParams(vmem_limit_bytes=mib * MIB)


def whole(shape):
    zeros = (0,) * len(shape)
    return pl.BlockSpec(shape, lambda *_: zeros)


def dot(a, b):
    return jnp.dot(a, b, preferred_element_type=F32)


def dot_nt(a, b):
    return lax.dot_general(a, b, (((1,), (1,)), ((), ())), preferred_element_type=F32)


def split(x):
    high = x.astype(BF16)
    low = (x - high.astype(F32)).astype(BF16)
    return high, low


def rotate_kernel(devices, parent, weight, trial, walkers, noise, sent, pack, pair):
    own, occupied, orbitals = walkers.shape
    half = orbitals // devices // 2
    rows = jax.lax.broadcasted_iota(jnp.int32, (occupied, 1), 0)
    state = []
    for s in range(own):
        crossed = lax.dot_general(
            walkers[s], trial[...], (((1,), (1,)), ((), ())), precision=PRECISE, preferred_element_type=F32
        )
        normal = lax.dot_general(
            crossed, crossed, (((1,), (1,)), ((), ())), precision=PRECISE, preferred_element_type=F32
        )
        state.append(jnp.concatenate([normal, crossed], axis=1))
    for k in range(occupied):
        for s in range(own):
            m = state[s]
            pivot = m[k : k + 1, :]
            scaled = pivot / m[k : k + 1, k : k + 1]
            state[s] = jnp.where(rows == k, scaled, m - m[:, k : k + 1] * scaled)
    lane = jax.lax.broadcasted_iota(jnp.int32, (1, LANES), 1)
    packed = jnp.concatenate([walkers[s] for s in range(own)], axis=0).T
    pack[:orbitals, :] = packed
    empty = jnp.zeros((occupied, occupied), F32)
    inverse = jnp.concatenate(
        [
            jnp.concatenate([state[s][:, occupied:] if s == c else empty for c in range(own)], axis=1)
            for s in range(own)
        ],
        axis=0,
    )
    rotated = jnp.dot(packed, inverse, precision=PRECISE, preferred_element_type=F32)
    blocks = rotated.reshape(devices, 2, half, LANES)
    first, second = blocks[:, 0], blocks[:, 1]
    sent[:, :half, :] = jnp.where(lane < occupied, first, pltpu.roll(second, occupied, 2))
    sent[:, half : 2 * half, :] = jnp.where(lane < occupied, pltpu.roll(first, occupied, 2), second)
    extra = jnp.zeros((SUBLANES, LANES), F32)
    levels = jnp.zeros((SUBLANES, LANES), F32)
    width = noise.shape[1] // LANES
    for s in range(own):
        extra = jnp.where(lane == s, parent[s].astype(F32), extra)
        levels = jnp.where(lane == s, weight[s], levels)
        for t in range(width):
            at = orbitals + s * width + t
            pack[at : at + 1, :] = noise[s : s + 1, t * LANES : (t + 1) * LANES]
    tail = sent.shape[1] - own * half
    sent[:, own * half :, :] = jnp.broadcast_to(extra[None, :tail], (devices, tail, LANES))
    pack[pack.shape[0] - SUBLANES :, :] = levels
    value = jnp.concatenate([trial[...]] * 2, axis=0).T
    high, low = split(value)
    pair[...] = jnp.where(lane < occupied, high, low)


def rotate_plain(devices, parent, weight, trial, walkers, noise, sent_rows, pack_rows):
    own, occupied, orbitals = walkers.shape
    half = orbitals // devices // 2
    crossed = jnp.einsum("wkm,nm->wkn", walkers, trial, precision=PRECISE)
    normal = jnp.einsum("wkn,wln->wkl", crossed, crossed, precision=PRECISE)
    factor = jnp.linalg.cholesky(normal)
    inverse = jax.vmap(lambda f, c: jax.scipy.linalg.cho_solve((f, True), c))(factor, crossed)
    rotated = jnp.einsum("wkm,wkn->wmn", walkers, inverse, precision=PRECISE)
    sent = rotated.reshape(own, devices, 2, half, occupied).transpose(1, 0, 3, 2, 4)
    sent = sent.reshape(devices, own * half, 2 * occupied)
    extra = jnp.zeros((sent_rows - own * half, LANES), F32).at[0, :own].set(parent.astype(F32))
    sent = jnp.concatenate([sent, jnp.broadcast_to(extra[None], (devices,) + extra.shape)], axis=1)
    levels = jnp.zeros((SUBLANES, LANES), F32).at[0, :own].set(weight)
    pack = jnp.concatenate(
        [walkers.transpose(2, 0, 1).reshape(orbitals, own * occupied), noise.reshape(-1, LANES), levels], axis=0
    )
    return sent, pack, jnp.concatenate(split(trial.T), axis=1)


def rotate(devices, parent, weight, trial, walkers, noise):
    own, occupied, orbitals = walkers.shape
    half = orbitals // devices // 2
    sent_rows = -(-(own * half + 1) // SUBLANES) * SUBLANES
    pack_rows = orbitals + noise.size // LANES + SUBLANES
    if half % SUBLANES or own != 2 or own * occupied != LANES:
        return rotate_plain(devices, parent, weight, trial, walkers, noise, sent_rows, pack_rows)
    smem = pl.BlockSpec(memory_space=pltpu.SMEM)
    return pl.pallas_call(
        functools.partial(rotate_kernel, devices),
        out_shape=(
            jax.ShapeDtypeStruct((devices, sent_rows, LANES), F32),
            jax.ShapeDtypeStruct((pack_rows, LANES), F32),
            jax.ShapeDtypeStruct((orbitals, 2 * occupied), BF16),
        ),
        in_specs=[smem, smem] + [pl.BlockSpec(memory_space=pltpu.VMEM)] * 3,
        out_specs=(pl.BlockSpec(memory_space=pltpu.VMEM),) * 3,
        compiler_params=params(16),
    )(parent, weight, trial, walkers, noise)


def contract_kernel(pair, chol, out):
    orbitals = pair.shape[0]
    occupied = pair.shape[1] // 2
    half = chol.shape[1] // orbitals // 2
    lane = jax.lax.broadcasted_iota(jnp.int32, (1, 2 * occupied), 1)
    both_parts = pair[...]
    alone = jnp.where(lane < occupied, both_parts, jnp.zeros_like(both_parts))

    def one(i):
        chol_high, chol_low = split(chol[:, i * orbitals : (i + 1) * orbitals])
        both = dot(chol_high, both_parts) + dot(chol_low, alone)
        return both + pltpu.roll(both, occupied, 1)

    for i in range(half):
        out[:, i * 2 * occupied : (i + 1) * 2 * occupied] = jnp.where(lane < occupied, one(i), one(i + half))


def contract(pair, chol):
    vectors, pairs = chol.shape
    orbitals, occupied = pair.shape[0], pair.shape[1] // 2
    columns = pairs // orbitals * occupied
    block = 256
    return pl.pallas_call(
        contract_kernel,
        grid=(vectors // block,),
        out_shape=jax.ShapeDtypeStruct((vectors, columns), F32),
        in_specs=[whole(pair.shape), pl.BlockSpec((block, pairs), lambda g: (g, 0))],
        out_specs=pl.BlockSpec((block, columns), lambda g: (g, 0)),
        compiler_params=params(32),
        cost_estimate=pl.CostEstimate(
            flops=2 * vectors * pairs * occupied * 3, bytes_accessed=4 * vectors * (pairs + columns), transcendentals=0
        ),
    )(pair, chol)


def bias_kernel(own, half, place, rotated, contracted, noise, out, high, low):
    devices = rotated.shape[0]
    for i in range(half):
        for s in range(own):
            part_high, part_low = split(rotated[:, s * half + i, :])
            high[s * devices : (s + 1) * devices, i * LANES : (i + 1) * LANES] = part_high
            low[s * devices : (s + 1) * devices, i * LANES : (i + 1) * LANES] = part_low
    rows = jax.lax.broadcasted_iota(jnp.int32, (out.shape[0], 1), 0)
    block = 512
    for g in range(0, out.shape[1], block):
        b_high, b_low = split(contracted[g : g + block, :])
        bias = dot_nt(high[...], b_high) + dot_nt(low[...], b_high) + dot_nt(high[...], b_low)
        value = -TIME_ROOT * bias
        for s in range(own):
            value += jnp.where(rows == s * devices + place[0], noise[s : s + 1, g : g + block], 0.0)
        out[:, g : g + block] = value


def partial_fields(own, half, place, rotated, contracted, noise):
    vectors, columns = contracted.shape
    devices = rotated.shape[0]
    return pl.pallas_call(
        functools.partial(bias_kernel, own, half),
        out_shape=jax.ShapeDtypeStruct((own * devices, vectors), F32),
        in_specs=[pl.BlockSpec(memory_space=pltpu.SMEM)] + [pl.BlockSpec(memory_space=pltpu.VMEM)] * 3,
        out_specs=pl.BlockSpec(memory_space=pltpu.VMEM),
        scratch_shapes=[pltpu.VMEM((own * devices, columns), BF16)] * 2,
        compiler_params=params(28),
    )(place, rotated, contracted, noise)


def send(x, walk_size, chol_size, target):
    return lax.ppermute(x, BOTH, [(i, target(i)) for i in range(walk_size * chol_size)])


def sum_everywhere(x, walk_size, chol_size):
    walk = lax.axis_index("walk")
    core = lax.axis_index("chol") % 2
    half = x.shape[0] // 2
    quarter = half // walk_size
    mine = lax.dynamic_slice_in_dim(x, core * half, half, 0)
    other = lax.dynamic_slice_in_dim(x, (1 - core) * half, half, 0)
    chip = mine + send(other, walk_size, chol_size, lambda i: i ^ 1)
    total = lax.dynamic_slice_in_dim(chip, walk * quarter, quarter, 0)
    got = [
        send(
            lax.dynamic_slice_in_dim(chip, (walk ^ r) * quarter, quarter, 0),
            walk_size, chol_size, lambda i, r=r: i ^ (r * chol_size),
        )
        for r in range(1, walk_size)
    ]
    for g in got:
        total = total + g
    got = [send(total, walk_size, chol_size, lambda i, r=r: i ^ (2 * r)) for r in range(1, chol_size // 2)]
    for g in got:
        total = total + g
    blocks = [total] + [
        send(total, walk_size, chol_size, lambda i, r=r: i ^ (r * chol_size)) for r in range(1, walk_size)
    ]
    here = jnp.concatenate(blocks, axis=0)
    there = send(here, walk_size, chol_size, lambda i: i ^ 1)
    return jnp.concatenate([here, there], axis=0)


def row_of(walker, own, walk_size, chol_size):
    everyone = own * walk_size * chol_size
    walk = lax.axis_index("walk")
    core = lax.axis_index("chol") % 2
    row = (walker % own) * (walk_size * chol_size) + walker // own
    half = everyone // 2
    quarter = half // walk_size
    inside = row % half
    return ((row // half) ^ core) * half + ((inside // quarter) ^ walk) * quarter + inside % quarter


def select_kernel(rows, fields, out):
    slots = fields.shape[0]
    lane = jax.lax.broadcasted_iota(jnp.int32, (slots, slots), 1)
    pick = jnp.where(lane == rows[...], 1.0, 0.0).astype(BF16)
    value = fields[...]
    first, rest = split(value)
    second, third = split(value - first.astype(F32))
    picked = dot(pick, first) + dot(pick, second) + dot(pick, third)
    high, low = split(TIME_ROOT * picked)
    out[:slots, :] = high
    out[slots:, :] = low


def select(rows, fields):
    slots, vectors = fields.shape
    block = 512
    return pl.pallas_call(
        select_kernel,
        grid=(vectors // block,),
        out_shape=jax.ShapeDtypeStruct((2 * slots, vectors), BF16),
        in_specs=[whole((slots, 1)), pl.BlockSpec((slots, block), lambda g: (0, g))],
        out_specs=pl.BlockSpec((2 * slots, block), lambda g: (0, g)),
        compiler_params=params(16),
    )(rows.reshape(slots, 1), fields)


def potential_kernel(own, parts, fields, *refs):
    chols, out = refs[:parts], refs[parts]
    slots = fields.shape[0] // 2
    devices = slots // own
    unit = SUBLANES // own
    step = chols[0].shape[0]
    pieces = chols[0].shape[1] // LANES
    total = None
    for p in range(parts):
        high, low = split(chols[p][...])
        part = fields[:, p * step : (p + 1) * step]
        value = dot(part, high) + dot(part, low)
        total = value if total is None else total + value
    total = total[:slots] + total[slots:]
    here = pl.program_id(0)
    start = here // unit * (pieces * SUBLANES) + here % unit
    stride = out.shape[0] // devices
    for t in range(pieces):
        for s in range(own):
            at = pl.ds(start + t * SUBLANES + s * unit, devices, stride=stride)
            out[at, :] = total[s * devices : (s + 1) * devices, t * LANES : (t + 1) * LANES]


def potential_tiles(own, fields, chol, orbitals, first, count):
    vectors = chol.shape[0]
    slots = fields.shape[0] // 2
    step = 256
    parts = vectors // step
    rows = slots * count * orbitals // LANES
    return pl.pallas_call(
        functools.partial(potential_kernel, own, parts),
        grid=(count,),
        out_shape=jax.ShapeDtypeStruct((rows, LANES), F32),
        in_specs=[whole(fields.shape)]
        + [pl.BlockSpec((step, orbitals), lambda i, p=p: (p, first + i)) for p in range(parts)],
        out_specs=whole((rows, LANES)),
        compiler_params=params(32),
        cost_estimate=pl.CostEstimate(
            flops=2 * slots * vectors * orbitals * count * 3,
            bytes_accessed=4 * vectors * orbitals * count,
            transcendentals=0,
        ),
    )(fields, *[chol] * parts)


def taylor_kernel(own, chunks, index, gathered, *refs):
    tiles = refs[:chunks]
    out, high, low, term, starts, sems = refs[chunks:]
    orbitals, width = term.shape
    occupied = width // own
    pieces = orbitals // LANES
    devices = tiles[0].shape[0]
    unit = SUBLANES // own
    copies = [
        pltpu.make_async_copy(gathered.at[index[s], pl.ds(0, orbitals)], starts.at[s], sems.at[s]) for s in range(own)
    ]
    for copy in copies:
        copy.start()
    lane = jax.lax.broadcasted_iota(jnp.int32, (1, width), 1) // occupied
    sub = jax.lax.broadcasted_iota(jnp.int32, (SUBLANES, 1), 0) // unit
    for t in range(pieces):
        parts = [tile[...].reshape(devices, -1, pieces, SUBLANES, LANES)[:, :, t] for tile in tiles]
        value_high, value_low = split(jnp.concatenate(parts, axis=1).reshape(-1, LANES))
        high[:, t * LANES : (t + 1) * LANES] = value_high
        low[:, t * LANES : (t + 1) * LANES] = value_low
    for copy in copies:
        copy.wait()
    total = jnp.zeros((orbitals, width), F32)
    for s in range(own):
        source = starts[s]
        inside = index[own + s]
        moved = source
        for shift in range(1, own):
            rolled = pltpu.roll(source, shift * occupied, 1)
            moved = jnp.where((inside + shift) % own == s, rolled, moved)
        total = jnp.where(lane == s, moved, total)
    term[...] = total
    for order in range(1, TERMS):
        term_high, term_low = split(term[...])
        pair = jnp.concatenate([term_high, term_low], axis=1)
        both = dot(high[...], pair)
        value = both[:, :width] + both[:, width:] + dot(low[...], term_high)
        value = value.reshape(-1, own, SUBLANES, width)
        placed = jnp.zeros((value.shape[0], SUBLANES, width), F32)
        for j in range(own):
            for s in range(own):
                shift = ((j - s) * unit) % SUBLANES
                moved = pltpu.roll(value[:, j], shift, 1) if shift else value[:, j]
                placed = jnp.where((sub == j) & (lane == s), moved, placed)
        placed = placed.reshape(orbitals, width) / order
        term[...] = placed
        total = total + placed
    flipped = total.T
    for s in range(own):
        out[s] = flipped[s * occupied : (s + 1) * occupied, :]


def taylor(index, gathered, tiles, own, orbitals, occupied):
    width = own * occupied
    chunks = len(tiles)
    rows = sum(t.shape[0] * t.shape[1] for t in tiles) // (orbitals // LANES)
    vmem = pl.BlockSpec(memory_space=pltpu.VMEM)
    return pl.pallas_call(
        functools.partial(taylor_kernel, own, chunks),
        out_shape=jax.ShapeDtypeStruct((own, occupied, orbitals), F32),
        in_specs=[pl.BlockSpec(memory_space=pltpu.SMEM), pl.BlockSpec(memory_space=pl.ANY)] + [vmem] * chunks,
        out_specs=vmem,
        scratch_shapes=[
            pltpu.VMEM((rows, orbitals), BF16),
            pltpu.VMEM((rows, orbitals), BF16),
            pltpu.VMEM((orbitals, width), F32),
            pltpu.VMEM((own, orbitals, width), F32),
            pltpu.SemaphoreType.DMA((own,)),
        ],
        compiler_params=params(24),
    )(index, gathered, *tiles)


def per_device(trial, walkers, chol, field_noise, log_weight, parent):
    own, orbitals, occupied = walkers.shape
    walk_size = lax.axis_size("walk")
    chol_size = lax.axis_size("chol")
    devices = walk_size * chol_size
    vectors, pairs = chol.shape
    rows_here = pairs // orbitals
    half = rows_here // 2
    place = lax.axis_index(BOTH)

    sent, pack, pair = rotate(
        devices, parent, log_weight, trial.T, walkers.transpose(0, 2, 1), field_noise
    )
    rotated = lax.all_to_all(sent, BOTH, split_axis=0, concat_axis=0, tiled=True)
    gathered = lax.all_gather(pack, "chol", axis=0, tiled=False)
    contracted = contract(pair, chol)
    mine = partial_fields(own, half, place.reshape(1), rotated, contracted, field_noise)
    fields = sum_everywhere(mine, walk_size, chol_size)

    parents = rotated[:, own * half, :own].T.reshape(own * devices).astype(jnp.int32)
    parent_rows = row_of(parents, own, walk_size, chol_size)
    scaled = select(parent_rows, fields)

    unit = SUBLANES // own
    units = rows_here // unit
    cuts = [0] + ([FIRST_UNITS] if units > FIRST_UNITS else []) + [units]
    tiles = []
    for begin, end in zip(cuts[:-1], cuts[1:]):
        chunk = potential_tiles(own, scaled, chol, orbitals, begin * unit, (end - begin) * unit)
        chunk = chunk.reshape(devices, -1, LANES)
        tiles.append(lax.all_to_all(chunk, BOTH, split_axis=0, concat_axis=0, tiled=True))

    local = parent - lax.axis_index("walk") * (own * chol_size)
    source, inside = local // own, local % own
    new_walkers = taylor(
        jnp.concatenate([source, inside]), gathered, tiles, own, orbitals, occupied
    ).transpose(0, 2, 1)

    width = vectors // LANES
    notes = gathered[:, orbitals : orbitals + own * width, :].reshape(own * chol_size, vectors)
    parent_noise = jnp.take(notes, local, axis=0)
    parent_level = jnp.take(gathered[:, -SUBLANES, :own].reshape(own * chol_size), local, axis=0)
    parent_fields = jnp.take(fields, row_of(parent, own, walk_size, chol_size), axis=0)
    shift = parent_noise - parent_fields
    new_log_weight = parent_level + jnp.sum(0.5 * shift * shift - parent_noise * shift, axis=1)
    return (new_walkers, new_log_weight)


def solution(mesh):
    return jax.shard_map(
        per_device,
        mesh=mesh,
        in_specs=(
            P(),
            P(BOTH, None, None),
            P(None, BOTH),
            P(BOTH, None),
            P(BOTH),
            P(BOTH),
        ),
        out_specs=(P(BOTH, None, None), P(BOTH)),
        check_vma=False,
    )
```

time: 211 us -> 210 us (level)
  Pallas kernels: 99.5 us -> 86.6 us
  local copies, waits for them, and re-layouts: 10.5 us -> 19.3 us
  starting transfers between devices: 33 us -> 36.4 us
    pallas_call x1, Pallas kernels: 41.4 us -> 32.4 us  [contract(): pl.pallas_call(contract_kernel, grid=(vectors // block,), out_shape=jax.S...]
    unnamed x18 -> x25, local copies, waits for them, and re-layouts: 6.78 us -> 14.4 us
    pallas_call x4, Pallas kernels: 48.4 us -> 44.4 us  [the longest x2 33.9 us: potential_tiles(): pl.pallas_call(functools.partial(potential_kernel, own, parts), grid=(cou...]
    all_to_all x2, starting transfers between devices: 13.7 us -> 17 us  [per_device(): lax.all_to_all(chunk, BOTH, split_axis=0, concat_axis=0, tiled=True)]
  transfers between devices with their start and end apart: 15 -> 15, of which waited for: 12 -> 11; matrix products, arithmetic and copies ran while one was open for 2% -> 3% of each run, Pallas kernels for 37% -> 32%
where the time goes in v2:
time: 210 us; the launch traced here: 209 us
  Pallas kernels  86.6 us (41%)
  waiting for transfers between devices  50.9 us (24%)
  starting transfers between devices  36.4 us (17%)
  local copies, waits for them, and re-layouts  19.3 us (9%)
  between operations  14.3 us (7%)
    pallas_call x2, Pallas kernels, potential_tiles(): pl.pallas_call(functools.partial(potential_kernel, own, parts), grid=(cou...  33.9 us
    all_to_all x2, waiting for transfers between devices, per_device(): lax.all_to_all(chunk, BOTH, split_axis=0, concat_axis=0, tiled=True)  33 us
    pallas_call x1, Pallas kernels, contract(): pl.pallas_call(contract_kernel, grid=(vectors // block,), out_shape=jax.S...  32.4 us
    ppermute x11, waiting for transfers between devices, send(): lax.ppermute(x, BOTH, [(i, target(i)) for i in range(walk_size * chol_siz...  17.8 us
    all_to_all x2, starting transfers between devices, per_device(): lax.all_to_all(chunk, BOTH, split_axis=0, concat_axis=0, tiled=True)  17 us
    unnamed x25, local copies, waits for them, and re-layouts  14.4 us
    ppermute x11, starting transfers between devices, send(): lax.ppermute(x, BOTH, [(i, target(i)) for i in range(walk_size * chol_siz...  11.9 us
    pallas_call x1, Pallas kernels, rotate(): pl.pallas_call(functools.partial(rotate_kernel, devices), out_shape=(jax....  8.3 us
  transfers between devices with their start and end apart: 15, of which 11 were waited for; matrix products, arithmetic and copies ran while one was open for 3% of the time, Pallas kernels for 32%

profile of v2, /device:TPU:0, one launch (start us, length us, event | category | flops | bytes accessed | tf_op | source)
XLA Modules:
  0.0 208.7 jit_solution(7444893241697933887)
XLA Ops:
  7.2 0.0 copy-start.4
  7.2 0.9 copy-done.4
  8.1 0.9 copy-done.5
  9.0 0.7 copy-done.6
  9.8 0.7 copy-done.8
  10.4 0.7 copy-done.10
  11.1 8.3 %shard_map.77 = (f32[32,24,128]{2,1,0:T(8,128)}, f32[560,128]{1,0:T(8,128)}, bf16[512,128]{1,0:T(8,128)(2,1)S(1)}) custom-call(s32[2]{0:T(128)S(1)} %copy-done.8, f32[2]{0:T(128)S(1)} %copy-done.10, f32[64,512]{1,0:T(8,128)S(1)} %bitcast.14, f32[2,64,512]{2,1,0:T(8,128)S(1)} %bitcast.13, f32[2,2560]{1,0:T(2,128)S(1)} %copy-done.6), custom_call_target="tpu_custom_call" | custom-call | tf_op jit(solution)/shard_map/pallas_call | solution.py:124
  19.4 7.3 %all-to-all-start = ((f32[32,24,128]{2,1,0:T(8,128)}), f32[32,24,128]{2,1,0:T(8,128)S(1)}, u32[]{:S(2)}, u32[]{:S(2)}) async-start(f32[32,24,128]{2,1,0:T(8,128)} %get-tuple-element.6), calls=%async_computation | async-start | bytes 786432 | tf_op jit(solution)/shard_map/all_to_all | solution.py:404
  26.7 0.2 all-gather.3.cloned.1.call-start
  26.9 0.0 copy-start.7
  26.9 32.4 %shard_map.78.contracted = f32[2560,1024]{1,0:T(8,128)S(1)} custom-call(bf16[512,128]{1,0:T(8,128)(2,1)S(1)} %get-tuple-element.7.pair, f32[2560,8192]{1,0:T(8,128)} %refs_9_.3), custom_call_target="tpu_custom_call" | custom-call | flops 8053063680 | bytes 94371840 | tf_op jit(solution)/shard_map/pallas_call | solution.py:159
  59.3 0.0 copy-start
  59.4 4.0 %copy-done = f32[2560,1024]{1,0:T(8,128)} copy-done((f32[2560,1024]{1,0:T(8,128)}, f32[2560,1024]{1,0:T(8,128)S(1)}, u32[]{:S(2)}) %copy-start) | copy-done | bytes 10485784
  63.4 0.0 all-to-all-done.rotated
  63.4 0.0 copy-done.7
  63.4 4.0 %copy-done.1 = f32[2560,1024]{1,0:T(8,128)S(1)} copy-done((f32[2560,1024]{1,0:T(8,128)S(1)}, f32[2560,1024]{1,0:T(8,128)}, u32[]{:S(2)}) %copy-start.1) | copy-done | bytes 10485784
  67.3 5.1 %shard_map.79 = f32[64,2560]{1,0:T(8,128)S(1)} custom-call(s32[1]{0:T(128)} %bitcast.6.place, f32[32,24,128]{2,1,0:T(8,128)S(1)} %all-to-all-done.rotated, f32[2560,1024]{1,0:T(8,128)S(1)} %copy-done.1, f32[2,2560]{1,0:T(2,128)S(1)} %copy-done.7), custom_call_target="tpu_custom_call" | custom-call | tf_op jit(solution)/shard_map/pallas_call | solution.py:193
  72.5 0.3 collective-permute-start
  72.8 1.4 collective-permute-done
  74.3 1.8 collective-permute-start.1
  76.1 1.5 collective-permute-start.2
  77.6 0.3 collective-permute-start.3
  77.8 0.0 all-gather.3.cloned.1.call-update
  77.9 1.1 collective-permute-done.1
  79.0 2.4 %collective-permute-done.2 = f32[8,2560]{1,0:T(8,128)S(1)} collective-permute-done((f32[8,2560]{1,0:T(8,128)S(1)}, f32[8,2560]{1,0:T(8,128)S(1)}, u32[]{:S(2)}, u32[]{:S(2)}) %collective-permute-start.2) | collective-permute-done | bytes 81952 | tf_op jit(solution)/shard_map/ppermute | solution.py:204
  81.3 1.6 collective-permute-done.3
  83.0 1.5 collective-permute-start.4
  84.5 2.5 %collective-permute-start.5 = (f32[8,2560]{1,0:T(8,128)S(1)}, f32[8,2560]{1,0:T(8,128)S(1)}, u32[]{:S(2)}, u32[]{:S(2)}) collective-permute-start(f32[8,2560]{1,0:T(8,128)S(1)} %add_add_fusion.1), channel_id=1, source_target_pairs={{0,4},{1,5},{2,6},{3,7},{4,0},{5,1},{6,2},{7,3},{8,12},{9,13},{10,... | collective-permute-start | bytes 245768 | tf_op jit(solution)/shard_map/ppermute | solution.py:204
  86.9 0.5 collective-permute-start.6
  87.4 0.1 copy.18
  87.5 0.1 convert_element_type.23
  87.6 0.1 collective-permute-done.4
  87.7 7.1 %collective-permute-done.5 = f32[8,2560]{1,0:T(8,128)S(1)} collective-permute-done((f32[8,2560]{1,0:T(8,128)S(1)}, f32[8,2560]{1,0:T(8,128)S(1)}, u32[]{:S(2)}, u32[]{:S(2)}) %collective-permute-start.5) | collective-permute-done | bytes 81952 | tf_op jit(solution)/shard_map/ppermute | solution.py:204
  94.8 0.0 collective-permute-done.6
  94.9 0.7 collective-permute-start.7
  95.6 0.2 collective-permute-start.8
  95.8 2.6 %collective-permute-start.9 = (f32[8,2560]{1,0:T(8,128)S(1)}, f32[8,2560]{1,0:T(8,128)S(1)}, u32[]{:S(2)}, u32[]{:S(2)}) collective-permute-start(f32[8,2560]{1,0:T(8,128)S(1)} %get-tuple-element.13), channel_id=1, source_target_pairs={{0,24},{1,25},{2,26},{3,27},{4,28},{5,29},{6,30},{7,31},{8,16},{9,... | collective-permute-start | bytes 245768 | tf_op jit(solution)/shard_map/ppermute | solution.py:204
  98.4 0.1 fusion.5.rows
  98.5 0.8 collective-permute-done.7
  99.4 0.6 collective-permute-done.8
  100.0 1.1 collective-permute-done.9
  101.1 0.1 collective-permute-start.10
  101.3 1.6 collective-permute-done.10
  102.9 1.5 shard_map.80.fields
  104.3 0.0 copy-start.3
  104.4 0.8 copy-done.3
  105.2 9.6 %shard_map.81 = f32[1024,128]{1,0:T(8,128)} custom-call(bf16[128,2560]{1,0:T(8,128)(2,1)S(1)} %shard_map.80.fields, f32[2560,8192]{1,0:T(8,128)} %refs_9_.3, f32[2560,8192]{1,0:T(8,128)} %refs_9_.3, f32[2560,8192]{1,0:T(8,128)} %refs_9_.3, f32[2560,8192]{1,0:T(8,128)} %refs_9_.3, f32[2560,8192]{1,0:T(8,128)} %refs_9_.3, f32[2560,8192]{1,0:T(8,128)} %refs_9_.3, ...), custom_call_target="tpu_custom_call" | custom-call | flops 2013265920 | bytes 20971520 | tf_op jit(solution)/shard_map/pallas_call | solution.py:302
  114.8 11.0 %all-to-all-start.1 = ((f32[32,32,128]{2,1,0:T(8,128)}), f32[32,32,128]{2,1,0:T(8,128)}, u32[]{:S(2)}, u32[]{:S(2)}) async-start(f32[32,32,128]{2,1,0:T(8,128)} %bitcast.7), calls=%async_computation.1 | async-start | bytes 1048576 | tf_op jit(solution)/shard_map/all_to_all | solution.py:421
  125.8 24.3 %shard_map.82 = f32[3072,128]{1,0:T(8,128)} custom-call(bf16[128,2560]{1,0:T(8,128)(2,1)S(1)} %shard_map.80.fields, f32[2560,8192]{1,0:T(8,128)} %refs_9_.3, f32[2560,8192]{1,0:T(8,128)} %refs_9_.3, f32[2560,8192]{1,0:T(8,128)} %refs_9_.3, f32[2560,8192]{1,0:T(8,128)} %refs_9_.3, f32[2560,8192]{1,0:T(8,128)} %refs_9_.3, f32[2560,8192]{1,0:T(8,128)} %refs_9_.3, ...), custom_call_target="tpu_custom_call" | custom-call | flops 6039797760 | bytes 62914560 | tf_op jit(solution)/shard_map/pallas_call | solution.py:302
  150.1 0.0 all-to-all-done.1.refs_0_
  150.1 6.0 %all-to-all-start.2 = ((f32[32,96,128]{2,1,0:T(8,128)}), f32[32,96,128]{2,1,0:T(8,128)S(1)}, u32[]{:S(2)}, u32[]{:S(2)}) async-start(f32[32,96,128]{2,1,0:T(8,128)} %bitcast.8), calls=%async_computation.2 | async-start | bytes 3145728 | tf_op jit(solution)/shard_map/all_to_all | solution.py:421
  156.2 0.1 pad_add_fusion.index
  156.3 1.7 gather_fusion.2
  158.0 0.0 all-gather.3.cloned.1.call-done
  158.0 0.9 slice.20
  159.0 0.8 slice_reduce_fusion
  159.7 0.1 reshape_squeeze.3
  159.8 0.6 gather_fusion.1
  160.4 0.6 gather_fusion
  161.0 0.2 fusion.19
  161.2 0.5 select_add_fusion
  161.8 33.0 %all-to-all-done.2.refs_1_ = f32[32,96,128]{2,1,0:T(8,128)S(1)} async-done(((f32[32,96,128]{2,1,0:T(8,128)}), f32[32,96,128]{2,1,0:T(8,128)S(1)}, u32[]{:S(2)}, u32[]{:S(2)}) %all-to-all-start.2) | async-done | bytes 1572896 | tf_op jit(solution)/shard_map/all_to_all | solution.py:421
  194.8 1.6 copy-done.2
  196.4 5.4 %shard_map.83 = f32[2,64,512]{2,1,0:T(8,128)} custom-call(s32[4]{0:T(128)S(1)} %pad_add_fusion.index, f32[8,560,128]{2,1,0:T(8,128)S(1)} %bitcast.12, f32[32,32,128]{2,1,0:T(8,128)} %all-to-all-done.1.refs_0_, f32[32,96,128]{2,1,0:T(8,128)S(1)} %all-to-all-done.2.refs_1_), custom_call_target="tpu_custom_call" | custom-call | tf_op jit(solution)/shard_map/pallas_call | solution.py:375
  (25 shorter events, 0.3 us)
Async XLA Ops:
  7.2 1.0 copy-start.4
  8.1 0.9 copy-start.5
  9.0 0.7 copy-start.6
  9.7 0.7 copy-start.8
  10.4 0.7 copy-start.10
  19.4 44.0 %all-to-all-start = ((f32[32,24,128]{2,1,0:T(8,128)}), f32[32,24,128]{2,1,0:T(8,128)S(1)}, u32[]{:S(2)}, u32[]{:S(2)}) async-start(f32[32,24,128]{2,1,0:T(8,128)} %get-tuple-element.6), calls=%async_computation | async-start | bytes 786432 | tf_op jit(solution)/shard_map/all_to_all | solution.py:404
  26.7 131.3 %all-gather.3.cloned.1.call-start = ((), (), s32[]{:S(2)}) async-start(), calls=%async_computation.3 | async-start | bytes 2580480 | tf_op jit(solution)/shard_map/all_gather | solution.py:405
  26.9 36.5 %copy-start.7 = (f32[2,2560]{1,0:T(2,128)S(1)}, f32[2,2560]{1,0:T(2,128)}, u32[]{:S(2)}) copy-start(f32[2,2560]{1,0:T(2,128)} %noise.3) | copy-start | bytes 61444
  59.3 4.0 %copy-start = (f32[2560,1024]{1,0:T(8,128)}, f32[2560,1024]{1,0:T(8,128)S(1)}, u32[]{:S(2)}) copy-start(f32[2560,1024]{1,0:T(8,128)S(1)} %shard_map.78.contracted) | copy-start | bytes 31457284
  63.4 4.0 %copy-start.1 = (f32[2560,1024]{1,0:T(8,128)S(1)}, f32[2560,1024]{1,0:T(8,128)}, u32[]{:S(2)}) copy-start(f32[2560,1024]{1,0:T(8,128)} %copy-done) | copy-start | bytes 31457284
  72.5 1.7 collective-permute-start
  74.3 4.7 %collective-permute-start.1 = (f32[8,2560]{1,0:T(8,128)S(1)}, f32[8,2560]{1,0:T(8,128)S(1)}, u32[]{:S(2)}, u32[]{:S(2)}) collective-permute-start(f32[8,2560]{1,0:T(8,128)S(1)} %get-tuple-element.16), channel_id=1, source_target_pairs={{0,8},{1,9},{2,10},{3,11},{4,12},{5,13},{6,14},{7,15},{8,0},{9,1},... | collective-permute-start | bytes 245768 | tf_op jit(solution)/shard_map/ppermute | solution.py:204
  76.1 5.2 %collective-permute-start.2 = (f32[8,2560]{1,0:T(8,128)S(1)}, f32[8,2560]{1,0:T(8,128)S(1)}, u32[]{:S(2)}, u32[]{:S(2)}) collective-permute-start(f32[8,2560]{1,0:T(8,128)S(1)} %get-tuple-element.18), channel_id=1, source_target_pairs={{0,16},{1,17},{2,18},{3,19},{4,20},{5,21},{6,22},{7,23},{8,24},{9,... | collective-permute-start | bytes 245768 | tf_op jit(solution)/shard_map/ppermute | solution.py:204
  77.6 5.3 %collective-permute-start.3 = (f32[8,2560]{1,0:T(8,128)S(1)}, f32[8,2560]{1,0:T(8,128)S(1)}, u32[]{:S(2)}, u32[]{:S(2)}) collective-permute-start(f32[8,2560]{1,0:T(8,128)S(1)} %get-tuple-element.17), channel_id=1, source_target_pairs={{0,24},{1,25},{2,26},{3,27},{4,28},{5,29},{6,30},{7,31},{8,16},{9,... | collective-permute-start | bytes 245768 | tf_op jit(solution)/shard_map/ppermute | solution.py:204
  83.0 4.8 %collective-permute-start.4 = (f32[8,2560]{1,0:T(8,128)S(1)}, f32[8,2560]{1,0:T(8,128)S(1)}, u32[]{:S(2)}, u32[]{:S(2)}) collective-permute-start(f32[8,2560]{1,0:T(8,128)S(1)} %add_add_fusion.1), channel_id=1, source_target_pairs={{0,2},{1,3},{2,0},{3,1},{4,6},{5,7},{6,4},{7,5},{8,10},{9,11},{10,... | collective-permute-start | bytes 245768 | tf_op jit(solution)/shard_map/ppermute | solution.py:204
  84.5 10.4 %collective-permute-start.5 = (f32[8,2560]{1,0:T(8,128)S(1)}, f32[8,2560]{1,0:T(8,128)S(1)}, u32[]{:S(2)}, u32[]{:S(2)}) collective-permute-start(f32[8,2560]{1,0:T(8,128)S(1)} %add_add_fusion.1), channel_id=1, source_target_pairs={{0,4},{1,5},{2,6},{3,7},{4,0},{5,1},{6,2},{7,3},{8,12},{9,13},{10,... | collective-permute-start | bytes 245768 | tf_op jit(solution)/shard_map/ppermute | solution.py:204
  86.9 7.9 %collective-permute-start.6 = (f32[8,2560]{1,0:T(8,128)S(1)}, f32[8,2560]{1,0:T(8,128)S(1)}, u32[]{:S(2)}, u32[]{:S(2)}) collective-permute-start(f32[8,2560]{1,0:T(8,128)S(1)} %add_add_fusion.1), channel_id=1, source_target_pairs={{0,6},{1,7},{2,4},{3,5},{4,2},{5,3},{6,0},{7,1},{8,14},{9,15},{10,... | collective-permute-start | bytes 245768 | tf_op jit(solution)/shard_map/ppermute | solution.py:204
  94.9 4.5 %collective-permute-start.7 = (f32[8,2560]{1,0:T(8,128)S(1)}, f32[8,2560]{1,0:T(8,128)S(1)}, u32[]{:S(2)}, u32[]{:S(2)}) collective-permute-start(f32[8,2560]{1,0:T(8,128)S(1)} %get-tuple-element.13), channel_id=1, source_target_pairs={{0,8},{1,9},{2,10},{3,11},{4,12},{5,13},{6,14},{7,15},{8,0},{9,1},... | collective-permute-start | bytes 245768 | tf_op jit(solution)/shard_map/ppermute | solution.py:204
  95.6 4.4 %collective-permute-start.8 = (f32[8,2560]{1,0:T(8,128)S(1)}, f32[8,2560]{1,0:T(8,128)S(1)}, u32[]{:S(2)}, u32[]{:S(2)}) collective-permute-start(f32[8,2560]{1,0:T(8,128)S(1)} %get-tuple-element.13), channel_id=1, source_target_pairs={{0,16},{1,17},{2,18},{3,19},{4,20},{5,21},{6,22},{7,23},{8,24},{9,... | collective-permute-start | bytes 245768 | tf_op jit(solution)/shard_map/ppermute | solution.py:204
  95.8 5.3 %collective-permute-start.9 = (f32[8,2560]{1,0:T(8,128)S(1)}, f32[8,2560]{1,0:T(8,128)S(1)}, u32[]{:S(2)}, u32[]{:S(2)}) collective-permute-start(f32[8,2560]{1,0:T(8,128)S(1)} %get-tuple-element.13), channel_id=1, source_target_pairs={{0,24},{1,25},{2,26},{3,27},{4,28},{5,29},{6,30},{7,31},{8,16},{9,... | collective-permute-start | bytes 245768 | tf_op jit(solution)/shard_map/ppermute | solution.py:204
  101.1 1.7 collective-permute-start.10
  104.3 0.8 copy-start.3
  114.8 35.4 %all-to-all-start.1 = ((f32[32,32,128]{2,1,0:T(8,128)}), f32[32,32,128]{2,1,0:T(8,128)}, u32[]{:S(2)}, u32[]{:S(2)}) async-start(f32[32,32,128]{2,1,0:T(8,128)} %bitcast.7), calls=%async_computation.1 | async-start | bytes 1048576 | tf_op jit(solution)/shard_map/all_to_all | solution.py:421
  150.1 6.0 %copy-start.9 = (s32[2]{0:T(128)S(1)}, s32[2]{0:T(128)}, u32[]{:S(2)}) copy-start(s32[2]{0:T(128)} %parent.1) | copy-start | bytes 28
  150.1 44.6 %all-to-all-start.2 = ((f32[32,96,128]{2,1,0:T(8,128)}), f32[32,96,128]{2,1,0:T(8,128)S(1)}, u32[]{:S(2)}, u32[]{:S(2)}) async-start(f32[32,96,128]{2,1,0:T(8,128)} %bitcast.8), calls=%async_computation.2 | async-start | bytes 3145728 | tf_op jit(solution)/shard_map/all_to_all | solution.py:421
  194.8 1.6 copy-start.2
Sparse Core Ops, SparseCore 0:
  78.0 35.2 all-gather.2

commit v3 on v2

--- a/solution.py
+++ b/solution.py
@@ -42,7 +42,7 @@
     return high, low
 
 
-def rotate_kernel(devices, parent, weight, trial, walkers, noise, sent, pack, pair):
+def rotate_kernel(devices, parent, trial, walkers, sent, pair):
     own, occupied, orbitals = walkers.shape
     half = orbitals // devices // 2
     rows = jax.lax.broadcasted_iota(jnp.int32, (occupied, 1), 0)
@@ -63,7 +63,6 @@
             state[s] = jnp.where(rows == k, scaled, m - m[:, k : k + 1] * scaled)
     lane = jax.lax.broadcasted_iota(jnp.int32, (1, LANES), 1)
     packed = jnp.concatenate([walkers[s] for s in range(own)], axis=0).T
-    pack[:orbitals, :] = packed
     empty = jnp.zeros((occupied, occupied), F32)
     inverse = jnp.concatenate(
         [
@@ -73,28 +72,22 @@
         axis=0,
     )
     rotated = jnp.dot(packed, inverse, precision=PRECISE, preferred_element_type=F32)
-    blocks = rotated.reshape(devices, 2, half, LANES)
-    first, second = blocks[:, 0], blocks[:, 1]
-    sent[:, :half, :] = jnp.where(lane < occupied, first, pltpu.roll(second, occupied, 2))
-    sent[:, half : 2 * half, :] = jnp.where(lane < occupied, pltpu.roll(first, occupied, 2), second)
+    for at, value in ((0, rotated), (own * half, packed)):
+        blocks = value.reshape(devices, 2, half, LANES)
+        first, second = blocks[:, 0], blocks[:, 1]
+        sent[:, at : at + half, :] = jnp.where(lane < occupied, first, pltpu.roll(second, occupied, 2))
+        sent[:, at + half : at + 2 * half, :] = jnp.where(lane < occupied, pltpu.roll(first, occupied, 2), second)
     extra = jnp.zeros((SUBLANES, LANES), F32)
-    levels = jnp.zeros((SUBLANES, LANES), F32)
-    width = noise.shape[1] // LANES
     for s in range(own):
         extra = jnp.where(lane == s, parent[s].astype(F32), extra)
-        levels = jnp.where(lane == s, weight[s], levels)
-        for t in range(width):
-            at = orbitals + s * width + t
-            pack[at : at + 1, :] = noise[s : s + 1, t * LANES : (t + 1) * LANES]
-    tail = sent.shape[1] - own * half
-    sent[:, own * half :, :] = jnp.broadcast_to(extra[None, :tail], (devices, tail, LANES))
-    pack[pack.shape[0] - SUBLANES :, :] = levels
+    tail = sent.shape[1] - 2 * own * half
+    sent[:, 2 * own * half :, :] = jnp.broadcast_to(extra[None, :tail], (devices, tail, LANES))
     value = jnp.concatenate([trial[...]] * 2, axis=0).T
     high, low = split(value)
     pair[...] = jnp.where(lane < occupied, high, low)
 
 
-def rotate_plain(devices, parent, weight, trial, walkers, noise, sent_rows, pack_rows):
+def rotate_plain(devices, parent, trial, walkers, sent_rows):
     own, occupied, orbitals = walkers.shape
     half = orbitals // devices // 2
     crossed = jnp.einsum("wkm,nm->wkn", walkers, trial, precision=PRECISE)
@@ -102,36 +95,35 @@
     factor = jnp.linalg.cholesky(normal)
     inverse = jax.vmap(lambda f, c: jax.scipy.linalg.cho_solve((f, True), c))(factor, crossed)
     rotated = jnp.einsum("wkm,wkn->wmn", walkers, inverse, precision=PRECISE)
-    sent = rotated.reshape(own, devices, 2, half, occupied).transpose(1, 0, 3, 2, 4)
-    sent = sent.reshape(devices, own * half, 2 * occupied)
-    extra = jnp.zeros((sent_rows - own * half, LANES), F32).at[0, :own].set(parent.astype(F32))
+    sent = jnp.concatenate([rotated, walkers.transpose(0, 2, 1)], axis=0)
+    sent = sent.reshape(2 * own, devices, 2, half, occupied).transpose(1, 0, 3, 2, 4)
+    sent = sent.reshape(devices, 2 * own * half, 2 * occupied)
+    extra = jnp.zeros((sent_rows - 2 * own * half, LANES), F32).at[0, :own].set(parent.astype(F32))
     sent = jnp.concatenate([sent, jnp.broadcast_to(extra[None], (devices,) + extra.shape)], axis=1)
-    levels = jnp.zeros((SUBLANES, LANES), F32).at[0, :own].set(weight)
-    pack = jnp.concatenate(
-        [walkers.transpose(2, 0, 1).reshape(orbitals, own * occupied), noise.reshape(-1, LANES), levels], axis=0
-    )
-    return sent, pack, jnp.concatenate(split(trial.T), axis=1)
-
-
-def rotate(devices, parent, weight, trial, walkers, noise):
+    return sent, jnp.concatenate(split(trial.T), axis=1)
+
+
+def eights(rows):
+    return -(-rows // SUBLANES) * SUBLANES
+
+
+def rotate(devices, parent, trial, walkers):
     own, occupied, orbitals = walkers.shape
     half = orbitals // devices // 2
-    sent_rows = -(-(own * half + 1) // SUBLANES) * SUBLANES
-    pack_rows = orbitals + noise.size // LANES + SUBLANES
+    sent_rows = eights(2 * own * half + 1)
     if half % SUBLANES or own != 2 or own * occupied != LANES:
-        return rotate_plain(devices, parent, weight, trial, walkers, noise, sent_rows, pack_rows)
-    smem = pl.BlockSpec(memory_space=pltpu.SMEM)
+        return rotate_plain(devices, parent, trial, walkers, sent_rows)
     return pl.pallas_call(
         functools.partial(rotate_kernel, devices),
+        grid=(1,),
         out_shape=(
             jax.ShapeDtypeStruct((devices, sent_rows, LANES), F32),
-            jax.ShapeDtypeStruct((pack_rows, LANES), F32),
             jax.ShapeDtypeStruct((orbitals, 2 * occupied), BF16),
         ),
-        in_specs=[smem, smem] + [pl.BlockSpec(memory_space=pltpu.VMEM)] * 3,
-        out_specs=(pl.BlockSpec(memory_space=pltpu.VMEM),) * 3,
+        in_specs=[pl.BlockSpec(memory_space=pltpu.SMEM), whole(trial.shape), whole(walkers.shape)],
+        out_specs=(whole((devices, sent_rows, LANES)), whole((orbitals, 2 * occupied))),
         compiler_params=params(16),
-    )(parent, weight, trial, walkers, noise)
+    )(parent, trial, walkers)
 
 
 def contract_kernel(pair, chol, out):
@@ -162,41 +154,52 @@
         out_shape=jax.ShapeDtypeStruct((vectors, columns), F32),
         in_specs=[whole(pair.shape), pl.BlockSpec((block, pairs), lambda g: (g, 0))],
         out_specs=pl.BlockSpec((block, columns), lambda g: (g, 0)),
-        compiler_params=params(32),
+        compiler_params=params(48),
         cost_estimate=pl.CostEstimate(
             flops=2 * vectors * pairs * occupied * 3, bytes_accessed=4 * vectors * (pairs + columns), transcendentals=0
         ),
     )(pair, chol)
 
 
-def bias_kernel(own, half, place, rotated, contracted, noise, out, high, low):
+def bias_kernel(own, half, place, rotated, contracted, noise, out, stacked):
     devices = rotated.shape[0]
-    for i in range(half):
-        for s in range(own):
-            part_high, part_low = split(rotated[:, s * half + i, :])
-            high[s * devices : (s + 1) * devices, i * LANES : (i + 1) * LANES] = part_high
-            low[s * devices : (s + 1) * devices, i * LANES : (i + 1) * LANES] = part_low
-    rows = jax.lax.broadcasted_iota(jnp.int32, (out.shape[0], 1), 0)
-    block = 512
-    for g in range(0, out.shape[1], block):
-        b_high, b_low = split(contracted[g : g + block, :])
-        bias = dot_nt(high[...], b_high) + dot_nt(low[...], b_high) + dot_nt(high[...], b_low)
-        value = -TIME_ROOT * bias
-        for s in range(own):
-            value += jnp.where(rows == s * devices + place[0], noise[s : s + 1, g : g + block], 0.0)
-        out[:, g : g + block] = value
+    slots = own * devices
+
+    @pl.when(pl.program_id(0) == 0)
+    def _():
+        for i in range(half):
+            for s in range(own):
+                high, low = split(rotated[:, s * half + i, :])
+                at = s * devices
+                stacked[at : at + devices, i * LANES : (i + 1) * LANES] = high
+                stacked[slots + at : slots + at + devices, i * LANES : (i + 1) * LANES] = low
+
+    b_high, b_low = split(contracted[...])
+    both = dot_nt(stacked[...], b_high) + dot_nt(stacked[...], b_low)
+    value = -TIME_ROOT * (both[:slots] + both[slots:])
+    rows = jax.lax.broadcasted_iota(jnp.int32, (slots, 1), 0)
+    for s in range(own):
+        value += jnp.where(rows == s * devices + place[0], noise[s : s + 1, :], 0.0)
+    out[...] = value
 
 
 def partial_fields(own, half, place, rotated, contracted, noise):
     vectors, columns = contracted.shape
     devices = rotated.shape[0]
+    block = 512
     return pl.pallas_call(
         functools.partial(bias_kernel, own, half),
+        grid=(vectors // block,),
         out_shape=jax.ShapeDtypeStruct((own * devices, vectors), F32),
-        in_specs=[pl.BlockSpec(memory_space=pltpu.SMEM)] + [pl.BlockSpec(memory_space=pltpu.VMEM)] * 3,
-        out_specs=pl.BlockSpec(memory_space=pltpu.VMEM),
-        scratch_shapes=[pltpu.VMEM((own * devices, columns), BF16)] * 2,
-        compiler_params=params(28),
+        in_specs=[
+            pl.BlockSpec(memory_space=pltpu.SMEM),
+            whole(rotated.shape),
+            pl.BlockSpec((block, columns), lambda g: (g, 0)),
+            pl.BlockSpec((own, block), lambda g: (0, g)),
+        ],
+        out_specs=pl.BlockSpec((own * devices, block), lambda g: (0, g)),
+        scratch_shapes=[pltpu.VMEM((2 * own * devices, columns), BF16)],
+        compiler_params=params(48),
     )(place, rotated, contracted, noise)
 
 
@@ -270,8 +273,35 @@
     )(rows.reshape(slots, 1), fields)
 
 
-def potential_kernel(own, parts, fields, *refs):
-    chols, out = refs[:parts], refs[parts]
+def carry_kernel(own, half, rows, received, out):
+    devices = received.shape[0]
+    slots = own * devices
+    lane = jax.lax.broadcasted_iota(jnp.int32, (slots, slots), 1)
+    pick = jnp.where(lane == rows[...], 1.0, 0.0).astype(BF16)
+    for i in range(half):
+        value = jnp.concatenate([received[:, (own + s) * half + i, :] for s in range(own)], axis=0)
+        first, rest = split(value)
+        second, third = split(value - first.astype(F32))
+        picked = dot(pick, first) + dot(pick, second) + dot(pick, third)
+        for s in range(own):
+            out[s * half + i] = picked[s * devices : (s + 1) * devices]
+
+
+def carry(own, half, rows, received):
+    devices = received.shape[0]
+    shape = (own * half, devices, LANES)
+    return pl.pallas_call(
+        functools.partial(carry_kernel, own, half),
+        grid=(1,),
+        out_shape=jax.ShapeDtypeStruct(shape, F32),
+        in_specs=[whole((own * devices, 1)), whole(received.shape)],
+        out_specs=whole(shape),
+        compiler_params=params(16),
+    )(rows.reshape(-1, 1), received)
+
+
+def potential_kernel(own, parts, base, fields, *refs):
+    chols, out = refs[:parts], refs[-1]
     slots = fields.shape[0] // 2
     devices = slots // own
     unit = SUBLANES // own
@@ -291,20 +321,45 @@
         for s in range(own):
             at = pl.ds(start + t * SUBLANES + s * unit, devices, stride=stride)
             out[at, :] = total[s * devices : (s + 1) * devices, t * LANES : (t + 1) * LANES]
-
-
-def potential_tiles(own, fields, chol, orbitals, first, count):
+    if len(refs) == parts + 1:
+        return
+    orbital_rows, summed, noise, places, levels = refs[parts:-1]
+
+    @pl.when(here == 0)
+    def _():
+        lane = jax.lax.broadcasted_iota(jnp.int32, (1, LANES), 1)
+        line = jnp.zeros((1, LANES), F32)
+        for s in range(own):
+            shift = noise[s : s + 1, :] - summed[pl.ds(places[s], 1), :]
+            terms = 0.5 * shift * shift - noise[s : s + 1, :] * shift
+            line = jnp.where(lane == s, levels[s] + jnp.sum(terms, axis=1, keepdims=True), line)
+        taken = orbital_rows.shape[0]
+        for r in range(taken):
+            out[pl.ds(base + r, devices, stride=stride), :] = orbital_rows[r]
+        for r in range(taken, stride - base):
+            out[pl.ds(base + r, devices, stride=stride), :] = jnp.broadcast_to(line, (devices, LANES))
+
+
+def potential_tiles(own, fields, chol, orbitals, first, count, along):
     vectors = chol.shape[0]
     slots = fields.shape[0] // 2
     step = 256
     parts = vectors // step
-    rows = slots * count * orbitals // LANES
-    return pl.pallas_call(
-        functools.partial(potential_kernel, own, parts),
+    devices = slots // own
+    base = own * count * orbitals // LANES
+    rows = devices * base
+    smem = pl.BlockSpec(memory_space=pltpu.SMEM)
+    more = []
+    if along:
+        rows += devices * eights(along[0].shape[0] + 1)
+        more = [whole(a.shape) for a in along[:3]] + [smem, smem]
+    return pl.pallas_call(
+        functools.partial(potential_kernel, own, parts, base),
         grid=(count,),
         out_shape=jax.ShapeDtypeStruct((rows, LANES), F32),
         in_specs=[whole(fields.shape)]
-        + [pl.BlockSpec((step, orbitals), lambda i, p=p: (p, first + i)) for p in range(parts)],
+        + [pl.BlockSpec((step, orbitals), lambda i, p=p: (p, first + i)) for p in range(parts)]
+        + more,
         out_specs=whole((rows, LANES)),
         compiler_params=params(32),
         cost_estimate=pl.CostEstimate(
@@ -312,40 +367,37 @@
             bytes_accessed=4 * vectors * orbitals * count,
             transcendentals=0,
         ),
-    )(fields, *[chol] * parts)
-
-
-def taylor_kernel(own, chunks, index, gathered, *refs):
+    )(fields, *[chol] * parts, *along)
+
+
+def taylor_kernel(own, chunks, base, *refs):
     tiles = refs[:chunks]
-    out, high, low, term, starts, sems = refs[chunks:]
+    begin = refs[chunks:-4]
+    out, high, low, term = refs[-4:]
     orbitals, width = term.shape
     occupied = width // own
     pieces = orbitals // LANES
     devices = tiles[0].shape[0]
+    half = orbitals // devices // 2
     unit = SUBLANES // own
-    copies = [
-        pltpu.make_async_copy(gathered.at[index[s], pl.ds(0, orbitals)], starts.at[s], sems.at[s]) for s in range(own)
-    ]
-    for copy in copies:
-        copy.start()
     lane = jax.lax.broadcasted_iota(jnp.int32, (1, width), 1) // occupied
     sub = jax.lax.broadcasted_iota(jnp.int32, (SUBLANES, 1), 0) // unit
     for t in range(pieces):
-        parts = [tile[...].reshape(devices, -1, pieces, SUBLANES, LANES)[:, :, t] for tile in tiles]
+        parts = []
+        for c, tile in enumerate(tiles):
+            value = tile[:, :base, :] if c == 0 else tile[...]
+            parts.append(value.reshape(devices, -1, pieces, SUBLANES, LANES)[:, :, t])
         value_high, value_low = split(jnp.concatenate(parts, axis=1).reshape(-1, LANES))
         high[:, t * LANES : (t + 1) * LANES] = value_high
         low[:, t * LANES : (t + 1) * LANES] = value_low
-    for copy in copies:
-        copy.wait()
-    total = jnp.zeros((orbitals, width), F32)
-    for s in range(own):
-        source = starts[s]
-        inside = index[own + s]
-        moved = source
-        for shift in range(1, own):
-            rolled = pltpu.roll(source, shift * occupied, 1)
-            moved = jnp.where((inside + shift) % own == s, rolled, moved)
-        total = jnp.where(lane == s, moved, total)
+    if begin:
+        total = begin[0][...]
+    else:
+        left = tiles[0][:, base : base + half, :]
+        right = tiles[0][:, base + half : base + 2 * half, :]
+        upper = jnp.where(lane == 0, left, pltpu.roll(right, occupied, 2))
+        lower = jnp.where(lane == 0, pltpu.roll(left, occupied, 2), right)
+        total = jnp.stack([upper, lower], axis=1).reshape(orbitals, width)
     term[...] = total
     for order in range(1, TERMS):
         term_high, term_low = split(term[...])
@@ -367,25 +419,28 @@
         out[s] = flipped[s * occupied : (s + 1) * occupied, :]
 
 
-def taylor(index, gathered, tiles, own, orbitals, occupied):
+def taylor(tiles, base, own, orbitals, occupied):
     width = own * occupied
     chunks = len(tiles)
-    rows = sum(t.shape[0] * t.shape[1] for t in tiles) // (orbitals // LANES)
+    devices = tiles[0].shape[0]
+    half = orbitals // devices // 2
+    begin = []
+    if half % SUBLANES or own != 2:
+        start = tiles[0][:, base : base + own * half].reshape(devices, own, half, 2, occupied)
+        begin = [start.transpose(0, 3, 2, 1, 4).reshape(orbitals, width)]
     vmem = pl.BlockSpec(memory_space=pltpu.VMEM)
     return pl.pallas_call(
-        functools.partial(taylor_kernel, own, chunks),
+        functools.partial(taylor_kernel, own, chunks, base),
         out_shape=jax.ShapeDtypeStruct((own, occupied, orbitals), F32),
-        in_specs=[pl.BlockSpec(memory_space=pltpu.SMEM), pl.BlockSpec(memory_space=pl.ANY)] + [vmem] * chunks,
+        in_specs=[vmem] * (chunks + len(begin)),
         out_specs=vmem,
         scratch_shapes=[
-            pltpu.VMEM((rows, orbitals), BF16),
-            pltpu.VMEM((rows, orbitals), BF16),
+            pltpu.VMEM((own * orbitals, orbitals), BF16),
+            pltpu.VMEM((own * orbitals, orbitals), BF16),
             pltpu.VMEM((orbitals, width), F32),
-            pltpu.VMEM((own, orbitals, width), F32),
-            pltpu.SemaphoreType.DMA((own,)),
         ],
         compiler_params=params(24),
-    )(index, gathered, *tiles)
+    )(*tiles, *begin)
 
 
 def per_device(trial, walkers, chol, field_noise, log_weight, parent):
@@ -398,41 +453,30 @@
     half = rows_here // 2
     place = lax.axis_index(BOTH)
 
-    sent, pack, pair = rotate(
-        devices, parent, log_weight, trial.T, walkers.transpose(0, 2, 1), field_noise
-    )
+    sent, pair = rotate(devices, parent, trial.T, walkers.transpose(0, 2, 1))
     rotated = lax.all_to_all(sent, BOTH, split_axis=0, concat_axis=0, tiled=True)
-    gathered = lax.all_gather(pack, "chol", axis=0, tiled=False)
     contracted = contract(pair, chol)
     mine = partial_fields(own, half, place.reshape(1), rotated, contracted, field_noise)
     fields = sum_everywhere(mine, walk_size, chol_size)
 
-    parents = rotated[:, own * half, :own].T.reshape(own * devices).astype(jnp.int32)
-    parent_rows = row_of(parents, own, walk_size, chol_size)
-    scaled = select(parent_rows, fields)
+    parents = rotated[:, 2 * own * half, :own].T.reshape(own * devices).astype(jnp.int32)
+    orbital_rows = carry(own, half, (parents % own) * devices + parents // own, rotated)
+    scaled = select(row_of(parents, own, walk_size, chol_size), fields)
+    places = row_of(place * own + jnp.arange(own, dtype=jnp.int32), own, walk_size, chol_size)
 
     unit = SUBLANES // own
     units = rows_here // unit
     cuts = [0] + ([FIRST_UNITS] if units > FIRST_UNITS else []) + [units]
     tiles = []
     for begin, end in zip(cuts[:-1], cuts[1:]):
-        chunk = potential_tiles(own, scaled, chol, orbitals, begin * unit, (end - begin) * unit)
+        along = () if begin else (orbital_rows, fields, field_noise, places, log_weight)
+        chunk = potential_tiles(own, scaled, chol, orbitals, begin * unit, (end - begin) * unit, along)
         chunk = chunk.reshape(devices, -1, LANES)
         tiles.append(lax.all_to_all(chunk, BOTH, split_axis=0, concat_axis=0, tiled=True))
 
-    local = parent - lax.axis_index("walk") * (own * chol_size)
-    source, inside = local // own, local % own
-    new_walkers = taylor(
-        jnp.concatenate([source, inside]), gathered, tiles, own, orbitals, occupied
-    ).transpose(0, 2, 1)
-
-    width = vectors // LANES
-    notes = gathered[:, orbitals : orbitals + own * width, :].reshape(own * chol_size, vectors)
-    parent_noise = jnp.take(notes, local, axis=0)
-    parent_level = jnp.take(gathered[:, -SUBLANES, :own].reshape(own * chol_size), local, axis=0)
-    parent_fields = jnp.take(fields, row_of(parent, own, walk_size, chol_size), axis=0)
-    shift = parent_noise - parent_fields
-    new_log_weight = parent_level + jnp.sum(0.5 * shift * shift - parent_noise * shift, axis=1)
+    base = own * cuts[1] * unit * orbitals // LANES
+    new_walkers = taylor(tiles, base, own, orbitals, occupied).transpose(0, 2, 1)
+    new_log_weight = tiles[0][parent // own, base + own * half, parent % own]
     return (new_walkers, new_log_weight)
 
 

time: 210 us -> 181 us (0.86)
  local copies, waits for them, and re-layouts: 19.3 us -> 4.71 us
  between operations: 14.3 us -> 0.83 us
  starting transfers between devices: 36.4 us -> 28.1 us
  Pallas kernels: 86.6 us -> 92.9 us
  waiting for transfers between devices: 50.9 us -> 53.7 us
    unnamed x25 -> x15, local copies, waits for them, and re-layouts: 14.4 us -> 2.54 us
    all_to_all x2, starting transfers between devices: 17 us -> 8.93 us  [per_device(): lax.all_to_all(chunk, BOTH, split_axis=0, concat_axis=0, tiled=True)]
    all_to_all x2, waiting for transfers between devices: 33 us -> 37.2 us  [per_device(): lax.all_to_all(chunk, BOTH, split_axis=0, concat_axis=0, tiled=True)]
    pallas_call x1, Pallas kernels: 32.4 us -> 35.8 us  [contract(): pl.pallas_call(contract_kernel, grid=(vectors // block,), out_shape=jax.S...]
    pallas_call x5 -> x6, Pallas kernels: 52.7 us -> 55.6 us  [the longest x2 34 us: potential_tiles(): pl.pallas_call(functools.partial(potential_kernel, own, parts, base), gri...]
  transfers between devices with their start and end apart: 15 -> 14, of which waited for: 11 -> 13; matrix products, arithmetic and copies ran while one was open for 3% -> 1% of each run, Pallas kernels for 32% -> 34%
where the time goes in v3:
time: 181 us; the launch traced here: 180 us
  Pallas kernels  92.9 us (51%)
  waiting for transfers between devices  53.7 us (30%)
  starting transfers between devices  28.1 us (16%)
  local copies, waits for them, and re-layouts  4.71 us (3%)
    all_to_all x2, waiting for transfers between devices, per_device(): lax.all_to_all(chunk, BOTH, split_axis=0, concat_axis=0, tiled=True)  37.2 us
    pallas_call x1, Pallas kernels, contract(): pl.pallas_call(contract_kernel, grid=(vectors // block,), out_shape=jax.S...  35.8 us
    pallas_call x2, Pallas kernels, potential_tiles(): pl.pallas_call(functools.partial(potential_kernel, own, parts, base), gri...  34 us
    ppermute x11, waiting for transfers between devices, send(): lax.ppermute(x, BOTH, [(i, target(i)) for i in range(walk_size * chol_siz...  16.5 us
    ppermute x11, starting transfers between devices, send(): lax.ppermute(x, BOTH, [(i, target(i)) for i in range(walk_size * chol_siz...  11.9 us
    all_to_all x2, starting transfers between devices, per_device(): lax.all_to_all(chunk, BOTH, split_axis=0, concat_axis=0, tiled=True)  8.93 us
    pallas_call x1, Pallas kernels, rotate(): pl.pallas_call(functools.partial(rotate_kernel, devices), grid=(1,), out_...  8.3 us
    pallas_call x1, Pallas kernels, partial_fields(): pl.pallas_call(functools.partial(bias_kernel, own, half), grid=(vectors /...  8 us
  transfers between devices with their start and end apart: 14, of which 13 were waited for; matrix products, arithmetic and copies ran while one was open for 1% of the time, Pallas kernels for 34%

profile of v3, /device:TPU:0, one launch (start us, length us, event | category | flops | bytes accessed | tf_op | source)
XLA Modules:
  0.0 180.5 jit_solution(8405669631392702930)
XLA Ops:
  0.6 0.0 copy-start
  0.6 0.9 copy-done
  1.6 0.0 copy-start.1
  1.6 0.9 copy-done.1
  2.5 0.0 copy-start.3
  2.5 0.7 copy-done.3
  3.1 8.3 %shard_map.77 = (f32[32,40,128]{2,1,0:T(8,128)}, bf16[512,128]{1,0:T(8,128)(2,1)S(1)}) custom-call(s32[2]{0:T(128)S(1)} %copy-done.3, f32[64,512]{1,0:T(8,128)S(1)} %bitcast.10, f32[2,64,512]{2,1,0:T(8,128)S(1)} %bitcast.9), custom_call_target="tpu_custom_call" | custom-call | tf_op jit(solution)/shard_map/pallas_call | solution.py:116
  11.4 7.3 %all-to-all-start = ((f32[32,40,128]{2,1,0:T(8,128)}), f32[32,40,128]{2,1,0:T(8,128)S(1)}, u32[]{:S(2)}, u32[]{:S(2)}) async-start(f32[32,40,128]{2,1,0:T(8,128)} %get-tuple-element.4), calls=%async_computation | async-start | bytes 1310720 | tf_op jit(solution)/shard_map/all_to_all | solution.py:457
  18.8 0.0 copy-start.2
  18.8 35.8 %shard_map.78.contracted = f32[2560,1024]{1,0:T(8,128)} custom-call(bf16[512,128]{1,0:T(8,128)(2,1)S(1)} %get-tuple-element.5.pair, f32[2560,8192]{1,0:T(8,128)} %refs_9_.3), custom_call_target="tpu_custom_call" | custom-call | flops 8053063680 | bytes 94371840 | tf_op jit(solution)/shard_map/pallas_call | solution.py:151
  54.6 0.0 copy-start.5
  54.6 0.0 all-to-all-done.rotated.received
  54.6 0.0 copy-done.2
  54.6 8.0 %shard_map.79 = f32[64,2560]{1,0:T(8,128)S(1)} custom-call(s32[1]{0:T(128)} %bitcast.5.place, f32[32,40,128]{2,1,0:T(8,128)S(1)} %all-to-all-done.rotated.received, f32[2560,1024]{1,0:T(8,128)} %shard_map.78.contracted, f32[2,2560]{1,0:T(2,128)S(1)} %copy-done.2), custom_call_target="tpu_custom_call" | custom-call | tf_op jit(solution)/shard_map/pallas_call | solution.py:190
  62.7 0.3 collective-permute-start
  62.9 1.4 collective-permute-done
  64.4 1.8 %collective-permute-start.1 = (f32[8,2560]{1,0:T(8,128)S(1)}, f32[8,2560]{1,0:T(8,128)S(1)}, u32[]{:S(2)}, u32[]{:S(2)}) collective-permute-start(f32[8,2560]{1,0:T(8,128)S(1)} %get-tuple-element.10), channel_id=1, source_target_pairs={{0,8},{1,9},{2,10},{3,11},{4,12},{5,13},{6,14},{7,15},{8,0},{9,1},... | collective-permute-start | bytes 245768 | tf_op jit(solution)/shard_map/ppermute | solution.py:207
  66.3 1.4 collective-permute-start.2
  67.7 0.3 collective-permute-start.3
  68.0 1.0 collective-permute-done.1
  69.0 1.9 %collective-permute-done.2 = f32[8,2560]{1,0:T(8,128)S(1)} collective-permute-done((f32[8,2560]{1,0:T(8,128)S(1)}, f32[8,2560]{1,0:T(8,128)S(1)}, u32[]{:S(2)}, u32[]{:S(2)}) %collective-permute-start.2) | collective-permute-done | bytes 81952 | tf_op jit(solution)/shard_map/ppermute | solution.py:207
  71.0 2.0 %collective-permute-done.3 = f32[8,2560]{1,0:T(8,128)S(1)} collective-permute-done((f32[8,2560]{1,0:T(8,128)S(1)}, f32[8,2560]{1,0:T(8,128)S(1)}, u32[]{:S(2)}, u32[]{:S(2)}) %collective-permute-start.3) | collective-permute-done | bytes 81952 | tf_op jit(solution)/shard_map/ppermute | solution.py:207
  73.0 1.5 collective-permute-start.4
  74.6 2.5 %collective-permute-start.5 = (f32[8,2560]{1,0:T(8,128)S(1)}, f32[8,2560]{1,0:T(8,128)S(1)}, u32[]{:S(2)}, u32[]{:S(2)}) collective-permute-start(f32[8,2560]{1,0:T(8,128)S(1)} %add_add_fusion.1), channel_id=1, source_target_pairs={{0,4},{1,5},{2,6},{3,7},{4,0},{5,1},{6,2},{7,3},{8,12},{9,13},{10,... | collective-permute-start | bytes 245768 | tf_op jit(solution)/shard_map/ppermute | solution.py:207
  77.1 0.4 collective-permute-start.6
  77.5 0.1 copy.18
  77.6 0.1 convert_element_type.27
  77.7 0.2 collective-permute-done.4
  77.9 3.8 %collective-permute-done.5 = f32[8,2560]{1,0:T(8,128)S(1)} collective-permute-done((f32[8,2560]{1,0:T(8,128)S(1)}, f32[8,2560]{1,0:T(8,128)S(1)}, u32[]{:S(2)}, u32[]{:S(2)}) %collective-permute-start.5) | collective-permute-done | bytes 81952 | tf_op jit(solution)/shard_map/ppermute | solution.py:207
  81.7 1.8 collective-permute-done.6
  83.4 0.6 collective-permute-start.7
  84.1 0.9 collective-permute-start.8
  84.9 2.1 %collective-permute-start.9 = (f32[8,2560]{1,0:T(8,128)S(1)}, f32[8,2560]{1,0:T(8,128)S(1)}, u32[]{:S(2)}, u32[]{:S(2)}) collective-permute-start(f32[8,2560]{1,0:T(8,128)S(1)} %get-tuple-element.7), channel_id=1, source_target_pairs={{0,24},{1,25},{2,26},{3,27},{4,28},{5,29},{6,30},{7,31},{8,16},{9,... | collective-permute-start | bytes 245768 | tf_op jit(solution)/shard_map/ppermute | solution.py:207
  87.0 0.1 fusion.5
  87.1 0.3 shard_map.81.refs_10_
  87.5 0.5 collective-permute-done.7
  88.0 0.6 collective-permute-done.8
  88.5 1.8 collective-permute-done.9
  90.3 0.1 collective-permute-start.10
  90.4 1.6 collective-permute-done.10
  92.0 1.5 shard_map.80.fields
  93.5 0.0 copy-done.5
  93.5 9.7 %shard_map.82 = f32[1792,128]{1,0:T(8,128)} custom-call(bf16[128,2560]{1,0:T(8,128)(2,1)S(1)} %shard_map.80.fields, f32[2560,8192]{1,0:T(8,128)} %refs_9_.3, f32[2560,8192]{1,0:T(8,128)} %refs_9_.3, f32[2560,8192]{1,0:T(8,128)} %refs_9_.3, f32[2560,8192]{1,0:T(8,128)} %refs_9_.3, f32[2560,8192]{1,0:T(8,128)} %refs_9_.3, f32[2560,8192]{1,0:T(8,128)} %refs_9_.3, ...), custom_call_target="tpu_custom_call" | custom-call | flops 2013265920 | bytes 20971520 | tf_op jit(solution)/shard_map/pallas_call | solution.py:356
  103.2 3.4 %all-to-all-start.1 = ((f32[32,56,128]{2,1,0:T(8,128)}), f32[32,56,128]{2,1,0:T(8,128)}, u32[]{:S(2)}, u32[]{:S(2)}) async-start(f32[32,56,128]{2,1,0:T(8,128)} %bitcast.6), calls=%async_computation.1 | async-start | bytes 1835008 | tf_op jit(solution)/shard_map/all_to_all | solution.py:475
  106.5 0.0 copy-start.4
  106.5 24.4 %shard_map.83 = f32[3072,128]{1,0:T(8,128)} custom-call(bf16[128,2560]{1,0:T(8,128)(2,1)S(1)} %shard_map.80.fields, f32[2560,8192]{1,0:T(8,128)} %refs_9_.3, f32[2560,8192]{1,0:T(8,128)} %refs_9_.3, f32[2560,8192]{1,0:T(8,128)} %refs_9_.3, f32[2560,8192]{1,0:T(8,128)} %refs_9_.3, f32[2560,8192]{1,0:T(8,128)} %refs_9_.3, f32[2560,8192]{1,0:T(8,128)} %refs_9_.3, ...), custom_call_target="tpu_custom_call" | custom-call | flops 6039797760 | bytes 62914560 | tf_op jit(solution)/shard_map/pallas_call | solution.py:356
  130.9 0.4 all-to-all-done.1.refs_0_
  131.3 5.6 %all-to-all-start.2 = ((f32[32,96,128]{2,1,0:T(8,128)}), f32[32,96,128]{2,1,0:T(8,128)S(1)}, u32[]{:S(2)}, u32[]{:S(2)}) async-start(f32[32,96,128]{2,1,0:T(8,128)} %bitcast.7), calls=%async_computation.2 | async-start | bytes 3145728 | tf_op jit(solution)/shard_map/all_to_all | solution.py:475
  136.9 0.0 copy-done.4
  136.9 1.9 %gather_fusion = f32[2]{0:T(128)} fusion(f32[32,56,128]{2,1,0:T(8,128)} %all-to-all-done.1.refs_0_, s32[2]{0:T(128)S(1)} %fusion.24), kind=kCustom, calls=%fused_computation | custom fusion | bytes 40 | tf_op jit(solution)/shard_map/gather | solution.py:479
  138.8 36.8 %all-to-all-done.2.refs_1_ = f32[32,96,128]{2,1,0:T(8,128)S(1)} async-done(((f32[32,96,128]{2,1,0:T(8,128)}), f32[32,96,128]{2,1,0:T(8,128)S(1)}, u32[]{:S(2)}, u32[]{:S(2)}) %all-to-all-start.2) | async-done | bytes 1572896 | tf_op jit(solution)/shard_map/all_to_all | solution.py:475
  175.6 4.9 %shard_map.84 = f32[2,64,512]{2,1,0:T(8,128)} custom-call(f32[32,56,128]{2,1,0:T(8,128)} %all-to-all-done.1.refs_0_, f32[32,96,128]{2,1,0:T(8,128)S(1)} %all-to-all-done.2.refs_1_), custom_call_target="tpu_custom_call" | custom-call | tf_op jit(solution)/shard_map/pallas_call | solution.py:432
  (13 shorter events, 0.3 us)
Async XLA Ops:
  0.6 1.0 copy-start
  1.6 0.9 copy-start.1
  2.5 0.7 copy-start.3
  11.4 43.2 %all-to-all-start = ((f32[32,40,128]{2,1,0:T(8,128)}), f32[32,40,128]{2,1,0:T(8,128)S(1)}, u32[]{:S(2)}, u32[]{:S(2)}) async-start(f32[32,40,128]{2,1,0:T(8,128)} %get-tuple-element.4), calls=%async_computation | async-start | bytes 1310720 | tf_op jit(solution)/shard_map/all_to_all | solution.py:457
  18.8 35.8 %copy-start.2 = (f32[2,2560]{1,0:T(2,128)S(1)}, f32[2,2560]{1,0:T(2,128)}, u32[]{:S(2)}) copy-start(f32[2,2560]{1,0:T(2,128)} %refs_12_.1) | copy-start | bytes 61444
  54.6 38.9 %copy-start.5 = (f32[2]{0:T(128)S(1)}, f32[2]{0:T(128)}, u32[]{:S(2)}) copy-start(f32[2]{0:T(128)} %refs_14_.1) | copy-start | bytes 28
  62.7 1.7 collective-permute-start
  64.4 4.6 %collective-permute-start.1 = (f32[8,2560]{1,0:T(8,128)S(1)}, f32[8,2560]{1,0:T(8,128)S(1)}, u32[]{:S(2)}, u32[]{:S(2)}) collective-permute-start(f32[8,2560]{1,0:T(8,128)S(1)} %get-tuple-element.10), channel_id=1, source_target_pairs={{0,8},{1,9},{2,10},{3,11},{4,12},{5,13},{6,14},{7,15},{8,0},{9,1},... | collective-permute-start | bytes 245768 | tf_op jit(solution)/shard_map/ppermute | solution.py:207
  66.3 4.7 %collective-permute-start.2 = (f32[8,2560]{1,0:T(8,128)S(1)}, f32[8,2560]{1,0:T(8,128)S(1)}, u32[]{:S(2)}, u32[]{:S(2)}) collective-permute-start(f32[8,2560]{1,0:T(8,128)S(1)} %get-tuple-element.12), channel_id=1, source_target_pairs={{0,16},{1,17},{2,18},{3,19},{4,20},{5,21},{6,22},{7,23},{8,24},{9,... | collective-permute-start | bytes 245768 | tf_op jit(solution)/shard_map/ppermute | solution.py:207
  67.7 5.3 %collective-permute-start.3 = (f32[8,2560]{1,0:T(8,128)S(1)}, f32[8,2560]{1,0:T(8,128)S(1)}, u32[]{:S(2)}, u32[]{:S(2)}) collective-permute-start(f32[8,2560]{1,0:T(8,128)S(1)} %get-tuple-element.11), channel_id=1, source_target_pairs={{0,24},{1,25},{2,26},{3,27},{4,28},{5,29},{6,30},{7,31},{8,16},{9,... | collective-permute-start | bytes 245768 | tf_op jit(solution)/shard_map/ppermute | solution.py:207
  73.0 4.8 %collective-permute-start.4 = (f32[8,2560]{1,0:T(8,128)S(1)}, f32[8,2560]{1,0:T(8,128)S(1)}, u32[]{:S(2)}, u32[]{:S(2)}) collective-permute-start(f32[8,2560]{1,0:T(8,128)S(1)} %add_add_fusion.1), channel_id=1, source_target_pairs={{0,2},{1,3},{2,0},{3,1},{4,6},{5,7},{6,4},{7,5},{8,10},{9,11},{10,... | collective-permute-start | bytes 245768 | tf_op jit(solution)/shard_map/ppermute | solution.py:207
  74.6 7.1 %collective-permute-start.5 = (f32[8,2560]{1,0:T(8,128)S(1)}, f32[8,2560]{1,0:T(8,128)S(1)}, u32[]{:S(2)}, u32[]{:S(2)}) collective-permute-start(f32[8,2560]{1,0:T(8,128)S(1)} %add_add_fusion.1), channel_id=1, source_target_pairs={{0,4},{1,5},{2,6},{3,7},{4,0},{5,1},{6,2},{7,3},{8,12},{9,13},{10,... | collective-permute-start | bytes 245768 | tf_op jit(solution)/shard_map/ppermute | solution.py:207
  77.1 6.3 %collective-permute-start.6 = (f32[8,2560]{1,0:T(8,128)S(1)}, f32[8,2560]{1,0:T(8,128)S(1)}, u32[]{:S(2)}, u32[]{:S(2)}) collective-permute-start(f32[8,2560]{1,0:T(8,128)S(1)} %add_add_fusion.1), channel_id=1, source_target_pairs={{0,6},{1,7},{2,4},{3,5},{4,2},{5,3},{6,0},{7,1},{8,14},{9,15},{10,... | collective-permute-start | bytes 245768 | tf_op jit(solution)/shard_map/ppermute | solution.py:207
  83.4 4.5 %collective-permute-start.7 = (f32[8,2560]{1,0:T(8,128)S(1)}, f32[8,2560]{1,0:T(8,128)S(1)}, u32[]{:S(2)}, u32[]{:S(2)}) collective-permute-start(f32[8,2560]{1,0:T(8,128)S(1)} %get-tuple-element.7), channel_id=1, source_target_pairs={{0,8},{1,9},{2,10},{3,11},{4,12},{5,13},{6,14},{7,15},{8,0},{9,1},... | collective-permute-start | bytes 245768 | tf_op jit(solution)/shard_map/ppermute | solution.py:207
  84.1 4.4 %collective-permute-start.8 = (f32[8,2560]{1,0:T(8,128)S(1)}, f32[8,2560]{1,0:T(8,128)S(1)}, u32[]{:S(2)}, u32[]{:S(2)}) collective-permute-start(f32[8,2560]{1,0:T(8,128)S(1)} %get-tuple-element.7), channel_id=1, source_target_pairs={{0,16},{1,17},{2,18},{3,19},{4,20},{5,21},{6,22},{7,23},{8,24},{9,... | collective-permute-start | bytes 245768 | tf_op jit(solution)/shard_map/ppermute | solution.py:207
  84.9 5.3 %collective-permute-start.9 = (f32[8,2560]{1,0:T(8,128)S(1)}, f32[8,2560]{1,0:T(8,128)S(1)}, u32[]{:S(2)}, u32[]{:S(2)}) collective-permute-start(f32[8,2560]{1,0:T(8,128)S(1)} %get-tuple-element.7), channel_id=1, source_target_pairs={{0,24},{1,25},{2,26},{3,27},{4,28},{5,29},{6,30},{7,31},{8,16},{9,... | collective-permute-start | bytes 245768 | tf_op jit(solution)/shard_map/ppermute | solution.py:207
  90.3 1.7 collective-permute-start.10
  103.2 28.1 %all-to-all-start.1 = ((f32[32,56,128]{2,1,0:T(8,128)}), f32[32,56,128]{2,1,0:T(8,128)}, u32[]{:S(2)}, u32[]{:S(2)}) async-start(f32[32,56,128]{2,1,0:T(8,128)} %bitcast.6), calls=%async_computation.1 | async-start | bytes 1835008 | tf_op jit(solution)/shard_map/all_to_all | solution.py:475
  106.5 30.3 %copy-start.4 = (s32[2]{0:T(128)S(1)}, s32[2]{0:T(128)}, u32[]{:S(2)}) copy-start(s32[2]{0:T(128)} %parent.1) | copy-start | bytes 28
  131.3 44.3 %all-to-all-start.2 = ((f32[32,96,128]{2,1,0:T(8,128)}), f32[32,96,128]{2,1,0:T(8,128)S(1)}, u32[]{:S(2)}, u32[]{:S(2)}) async-start(f32[32,96,128]{2,1,0:T(8,128)} %bitcast.7), calls=%async_computation.2 | async-start | bytes 3145728 | tf_op jit(solution)/shard_map/all_to_all | solution.py:475

commit v4 on v3

--- a/solution.py
+++ b/solution.py
@@ -17,6 +17,8 @@
 BF16 = jnp.bfloat16
 MIB = 1024 * 1024
 FIRST_UNITS = 1
+HEAD = 512
+PIECE = 128
 
 
 def params(mib):
@@ -42,9 +44,29 @@
     return high, low
 
 
-def rotate_kernel(devices, parent, trial, walkers, sent, pair):
+def rotate_kernel(devices, parent, trial_in, walkers_in, chol, sent, pair, contracted, trial, walkers, loaded, done, sems):
     own, occupied, orbitals = walkers.shape
     half = orbitals // devices // 2
+    count = loaded.shape[0] // PIECE
+    small = [
+        pltpu.make_async_copy(walkers_in, walkers, sems.at[0]),
+        pltpu.make_async_copy(trial_in, trial, sems.at[1]),
+    ]
+    reads, writes = [], []
+    for p in range(count):
+        at = pl.ds(p * PIECE, PIECE)
+        reads.append(pltpu.make_async_copy(chol.at[at], loaded.at[at], sems.at[2 + p]))
+        writes.append(pltpu.make_async_copy(done.at[at], contracted.at[at], sems.at[2 + count + p]))
+    for copy in small + reads:
+        copy.start()
+    for copy in small:
+        copy.wait()
+    lane = jax.lax.broadcasted_iota(jnp.int32, (1, LANES), 1)
+    both_parts = jnp.concatenate([trial[...]] * 2, axis=0).T
+    high, low = split(both_parts)
+    both_parts = jnp.where(lane < occupied, high, low)
+    pair[...] = both_parts
+    alone = jnp.where(lane < occupied, both_parts, jnp.zeros_like(both_parts))
     rows = jax.lax.broadcasted_iota(jnp.int32, (occupied, 1), 0)
     state = []
     for s in range(own):
@@ -55,13 +77,26 @@
             crossed, crossed, (((1,), (1,)), ((), ())), precision=PRECISE, preferred_element_type=F32
         )
         state.append(jnp.concatenate([normal, crossed], axis=1))
-    for k in range(occupied):
+
+    def eliminate(k):
         for s in range(own):
             m = state[s]
             pivot = m[k : k + 1, :]
             scaled = pivot / m[k : k + 1, k : k + 1]
             state[s] = jnp.where(rows == k, scaled, m - m[:, k : k + 1] * scaled)
-    lane = jax.lax.broadcasted_iota(jnp.int32, (1, LANES), 1)
+
+    pivots = 0
+    for p in range(count):
+        reads[p].wait()
+        at = slice(p * PIECE, (p + 1) * PIECE)
+        for i in range(half):
+            ends = [contract_row(loaded[at, r * orbitals : (r + 1) * orbitals], both_parts, alone) for r in (i, i + half)]
+            done[at, i * LANES : (i + 1) * LANES] = jnp.where(lane < occupied, ends[0], ends[1])
+            upto = occupied * (p * half + i + 1) // (count * half)
+            for k in range(pivots, upto):
+                eliminate(k)
+            pivots = upto
+        writes[p].start()
     packed = jnp.concatenate([walkers[s] for s in range(own)], axis=0).T
     empty = jnp.zeros((occupied, occupied), F32)
     inverse = jnp.concatenate(
@@ -82,9 +117,8 @@
         extra = jnp.where(lane == s, parent[s].astype(F32), extra)
     tail = sent.shape[1] - 2 * own * half
     sent[:, 2 * own * half :, :] = jnp.broadcast_to(extra[None, :tail], (devices, tail, LANES))
-    value = jnp.concatenate([trial[...]] * 2, axis=0).T
-    high, low = split(value)
-    pair[...] = jnp.where(lane < occupied, high, low)
+    for copy in writes:
+        copy.wait()
 
 
 def rotate_plain(devices, parent, trial, walkers, sent_rows):
@@ -107,58 +141,76 @@
     return -(-rows // SUBLANES) * SUBLANES
 
 
-def rotate(devices, parent, trial, walkers):
+def rotate(devices, parent, trial, walkers, chol):
     own, occupied, orbitals = walkers.shape
+    vectors = chol.shape[0]
+    columns = chol.shape[1] // orbitals * occupied
     half = orbitals // devices // 2
     sent_rows = eights(2 * own * half + 1)
     if half % SUBLANES or own != 2 or own * occupied != LANES:
-        return rotate_plain(devices, parent, trial, walkers, sent_rows)
+        return rotate_plain(devices, parent, trial, walkers, sent_rows) + (None,)
+    anywhere = pl.BlockSpec(memory_space=pl.ANY)
     return pl.pallas_call(
         functools.partial(rotate_kernel, devices),
         grid=(1,),
         out_shape=(
             jax.ShapeDtypeStruct((devices, sent_rows, LANES), F32),
             jax.ShapeDtypeStruct((orbitals, 2 * occupied), BF16),
+            jax.ShapeDtypeStruct((vectors, columns), F32),
         ),
-        in_specs=[pl.BlockSpec(memory_space=pltpu.SMEM), whole(trial.shape), whole(walkers.shape)],
-        out_specs=(whole((devices, sent_rows, LANES)), whole((orbitals, 2 * occupied))),
-        compiler_params=params(16),
-    )(parent, trial, walkers)
-
-
-def contract_kernel(pair, chol, out):
+        in_specs=[pl.BlockSpec(memory_space=pltpu.SMEM), anywhere, anywhere, anywhere],
+        out_specs=(whole((devices, sent_rows, LANES)), whole((orbitals, 2 * occupied)), anywhere),
+        scratch_shapes=[
+            pltpu.VMEM(trial.shape, F32),
+            pltpu.VMEM(walkers.shape, F32),
+            pltpu.VMEM((HEAD, chol.shape[1]), F32),
+            pltpu.VMEM((HEAD, columns), F32),
+            pltpu.SemaphoreType.DMA((2 + 2 * (HEAD // PIECE),)),
+        ],
+        compiler_params=params(60),
+    )(parent, trial, walkers, chol)
+
+
+def contract_row(part, both_parts, alone):
+    chol_high, chol_low = split(part)
+    both = dot(chol_high, both_parts) + dot(chol_low, alone)
+    return both + pltpu.roll(both, both.shape[1] // 2, 1)
+
+
+def contract_kernel(pair, chol, *refs):
+    out = refs[-1]
     orbitals = pair.shape[0]
     occupied = pair.shape[1] // 2
     half = chol.shape[1] // orbitals // 2
     lane = jax.lax.broadcasted_iota(jnp.int32, (1, 2 * occupied), 1)
     both_parts = pair[...]
     alone = jnp.where(lane < occupied, both_parts, jnp.zeros_like(both_parts))
-
-    def one(i):
-        chol_high, chol_low = split(chol[:, i * orbitals : (i + 1) * orbitals])
-        both = dot(chol_high, both_parts) + dot(chol_low, alone)
-        return both + pltpu.roll(both, occupied, 1)
-
     for i in range(half):
-        out[:, i * 2 * occupied : (i + 1) * 2 * occupied] = jnp.where(lane < occupied, one(i), one(i + half))
-
-
-def contract(pair, chol):
+        ends = [contract_row(chol[:, r * orbitals : (r + 1) * orbitals], both_parts, alone) for r in (i, i + half)]
+        out[:, i * 2 * occupied : (i + 1) * 2 * occupied] = jnp.where(lane < occupied, ends[0], ends[1])
+
+
+def contract(pair, chol, begun):
     vectors, pairs = chol.shape
     orbitals, occupied = pair.shape[0], pair.shape[1] // 2
     columns = pairs // orbitals * occupied
     block = 256
+    skip = 0 if begun is None else HEAD // block
+    more = [] if begun is None else [begun]
+    rest = vectors - skip * block
     return pl.pallas_call(
         contract_kernel,
-        grid=(vectors // block,),
+        grid=(rest // block,),
         out_shape=jax.ShapeDtypeStruct((vectors, columns), F32),
-        in_specs=[whole(pair.shape), pl.BlockSpec((block, pairs), lambda g: (g, 0))],
-        out_specs=pl.BlockSpec((block, columns), lambda g: (g, 0)),
+        in_specs=[whole(pair.shape), pl.BlockSpec((block, pairs), lambda g: (g + skip, 0))]
+        + [pl.BlockSpec(memory_space=pl.ANY)] * len(more),
+        out_specs=pl.BlockSpec((block, columns), lambda g: (g + skip, 0)),
+        input_output_aliases={2: 0} if more else {},
         compiler_params=params(48),
         cost_estimate=pl.CostEstimate(
-            flops=2 * vectors * pairs * occupied * 3, bytes_accessed=4 * vectors * (pairs + columns), transcendentals=0
+            flops=2 * rest * pairs * occupied * 3, bytes_accessed=4 * rest * (pairs + columns), transcendentals=0
         ),
-    )(pair, chol)
+    )(pair, chol, *more)
 
 
 def bias_kernel(own, half, place, rotated, contracted, noise, out, stacked):
@@ -453,9 +505,9 @@
     half = rows_here // 2
     place = lax.axis_index(BOTH)
 
-    sent, pair = rotate(devices, parent, trial.T, walkers.transpose(0, 2, 1))
+    sent, pair, begun = rotate(devices, parent, trial.T, walkers.transpose(0, 2, 1), chol)
     rotated = lax.all_to_all(sent, BOTH, split_axis=0, concat_axis=0, tiled=True)
-    contracted = contract(pair, chol)
+    contracted = contract(pair, chol, begun)
     mine = partial_fields(own, half, place.reshape(1), rotated, contracted, field_noise)
     fields = sum_everywhere(mine, walk_size, chol_size)
 

time: 181 us -> 176 us (0.972)
  Pallas kernels: 92.9 us -> 88.8 us
    pallas_call x1, Pallas kernels: 35.8 us -> 29.3 us  [contract(): pl.pallas_call(contract_kernel, grid=(rest // block,), out_shape=jax.Shap...]
    pallas_call x1, Pallas kernels: 8.3 us -> 10.8 us  [rotate(): pl.pallas_call(functools.partial(rotate_kernel, devices), grid=(1,), out_...]
  transfers between devices with their start and end apart: 14 -> 14, of which waited for: 13 -> 13; matrix products, arithmetic and copies ran while one was open for 1% -> 1% of each run, Pallas kernels for 34% -> 31%
where the time goes in v4:
time: 176 us; the launch traced here: 175 us
  Pallas kernels  88.8 us (50%)
  waiting for transfers between devices  53.9 us (31%)
  starting transfers between devices  28 us (16%)
  local copies, waits for them, and re-layouts  3.03 us (2%)
    all_to_all x2, waiting for transfers between devices, per_device(): lax.all_to_all(chunk, BOTH, split_axis=0, concat_axis=0, tiled=True)  37.4 us
    pallas_call x2, Pallas kernels, potential_tiles(): pl.pallas_call(functools.partial(potential_kernel, own, parts, base), gri...  34 us
    pallas_call x1, Pallas kernels, contract(): pl.pallas_call(contract_kernel, grid=(rest // block,), out_shape=jax.Shap...  29.3 us
    ppermute x11, waiting for transfers between devices, send(): lax.ppermute(x, BOTH, [(i, target(i)) for i in range(walk_size * chol_siz...  16.5 us
    ppermute x11, starting transfers between devices, send(): lax.ppermute(x, BOTH, [(i, target(i)) for i in range(walk_size * chol_siz...  11.8 us
    pallas_call x1, Pallas kernels, rotate(): pl.pallas_call(functools.partial(rotate_kernel, devices), grid=(1,), out_...  10.8 us
    all_to_all x2, starting transfers between devices, per_device(): lax.all_to_all(chunk, BOTH, split_axis=0, concat_axis=0, tiled=True)  8.73 us
    pallas_call x1, Pallas kernels, partial_fields(): pl.pallas_call(functools.partial(bias_kernel, own, half), grid=(vectors /...  8 us
  transfers between devices with their start and end apart: 14, of which 13 were waited for; matrix products, arithmetic and copies ran while one was open for 1% of the time, Pallas kernels for 31%

profile of v4, /device:TPU:0, one launch (start us, length us, event | category | flops | bytes accessed | tf_op | source)
XLA Modules:
  0.0 174.8 jit_solution(7699206414962902626)
XLA Ops:
  0.6 10.8 %shard_map.77 = (f32[32,40,128]{2,1,0:T(8,128)}, bf16[512,128]{1,0:T(8,128)(2,1)}, f32[2560,1024]{1,0:T(8,128)}) custom-call(s32[2]{0:T(128)} %parent.1, f32[64,512]{1,0:T(8,128)} %bitcast.11, f32[2,64,512]{2,1,0:T(8,128)} %bitcast.9, f32[2560,8192]{1,0:T(8,128)} %refs_9_.3), custom_call_target="tpu_custom_call" | custom-call | tf_op jit(solution)/shard_map/pallas_call | solution.py:153
  11.4 7.5 %all-to-all-start = ((f32[32,40,128]{2,1,0:T(8,128)}), f32[32,40,128]{2,1,0:T(8,128)S(1)}, u32[]{:S(2)}, u32[]{:S(2)}) async-start(f32[32,40,128]{2,1,0:T(8,128)} %get-tuple-element.5), calls=%async_computation | async-start | bytes 1310720 | tf_op jit(solution)/shard_map/all_to_all | solution.py:509
  18.9 0.0 copy-start
  18.9 0.9 copy-done
  19.8 0.0 copy-start.1
  19.8 29.3 %shard_map.78.contracted = f32[2560,1024]{1,0:T(8,128)} custom-call(bf16[512,128]{1,0:T(8,128)(2,1)S(1)} %copy-done, f32[2560,8192]{1,0:T(8,128)} %refs_9_.3, f32[2560,1024]{1,0:T(8,128)} %get-tuple-element.7.refs_0_), custom_call_target="tpu_custom_call", output_to_operand_aliasing={{}: (2, {})} | custom-call | flops 6442450944 | bytes 75497472 | tf_op jit(solution)/shard_map/pallas_call | solution.py:201
  49.1 0.0 copy-start.2
  49.1 0.0 all-to-all-done.rotated.received
  49.1 0.0 copy-done.1
  49.1 8.0 %shard_map.79 = f32[64,2560]{1,0:T(8,128)S(1)} custom-call(s32[1]{0:T(128)} %bitcast.5.place, f32[32,40,128]{2,1,0:T(8,128)S(1)} %all-to-all-done.rotated.received, f32[2560,1024]{1,0:T(8,128)} %shard_map.78.contracted, f32[2,2560]{1,0:T(2,128)S(1)} %copy-done.1), custom_call_target="tpu_custom_call" | custom-call | tf_op jit(solution)/shard_map/pallas_call | solution.py:242
  57.2 0.1 collective-permute-start
  57.3 1.5 collective-permute-done
  58.9 1.7 collective-permute-start.1
  60.6 1.4 collective-permute-start.2
  62.1 0.4 collective-permute-start.3
  62.5 1.0 collective-permute-done.1
  63.5 2.3 %collective-permute-done.2 = f32[8,2560]{1,0:T(8,128)S(1)} collective-permute-done((f32[8,2560]{1,0:T(8,128)S(1)}, f32[8,2560]{1,0:T(8,128)S(1)}, u32[]{:S(2)}, u32[]{:S(2)}) %collective-permute-start.2) | collective-permute-done | bytes 81952 | tf_op jit(solution)/shard_map/ppermute | solution.py:259
  65.8 1.6 collective-permute-done.3
  67.4 1.5 collective-permute-start.4
  69.0 2.4 %collective-permute-start.5 = (f32[8,2560]{1,0:T(8,128)S(1)}, f32[8,2560]{1,0:T(8,128)S(1)}, u32[]{:S(2)}, u32[]{:S(2)}) collective-permute-start(f32[8,2560]{1,0:T(8,128)S(1)} %add_add_fusion.1), channel_id=1, source_target_pairs={{0,4},{1,5},{2,6},{3,7},{4,0},{5,1},{6,2},{7,3},{8,12},{9,13},{10,... | collective-permute-start | bytes 245768 | tf_op jit(solution)/shard_map/ppermute | solution.py:259
  71.4 0.5 collective-permute-start.6
  71.9 0.1 copy.19
  72.0 0.1 convert_element_type.27
  72.1 0.2 collective-permute-done.4
  72.2 3.8 %collective-permute-done.5 = f32[8,2560]{1,0:T(8,128)S(1)} collective-permute-done((f32[8,2560]{1,0:T(8,128)S(1)}, f32[8,2560]{1,0:T(8,128)S(1)}, u32[]{:S(2)}, u32[]{:S(2)}) %collective-permute-start.5) | collective-permute-done | bytes 81952 | tf_op jit(solution)/shard_map/ppermute | solution.py:259
  76.1 1.7 collective-permute-done.6
  77.8 0.7 collective-permute-start.7
  78.4 0.9 collective-permute-start.8
  79.3 2.0 %collective-permute-start.9 = (f32[8,2560]{1,0:T(8,128)S(1)}, f32[8,2560]{1,0:T(8,128)S(1)}, u32[]{:S(2)}, u32[]{:S(2)}) collective-permute-start(f32[8,2560]{1,0:T(8,128)S(1)} %get-tuple-element.9), channel_id=1, source_target_pairs={{0,24},{1,25},{2,26},{3,27},{4,28},{5,29},{6,30},{7,31},{8,16},{9,... | collective-permute-start | bytes 245768 | tf_op jit(solution)/shard_map/ppermute | solution.py:259
  81.3 0.1 fusion.5
  81.4 0.3 shard_map.81.refs_10_
  81.8 0.5 collective-permute-done.7
  82.3 0.6 collective-permute-done.8
  82.9 1.8 %collective-permute-done.9 = f32[8,2560]{1,0:T(8,128)S(1)} collective-permute-done((f32[8,2560]{1,0:T(8,128)S(1)}, f32[8,2560]{1,0:T(8,128)S(1)}, u32[]{:S(2)}, u32[]{:S(2)}) %collective-permute-start.9) | collective-permute-done | bytes 81952 | tf_op jit(solution)/shard_map/ppermute | solution.py:259
  84.6 0.1 collective-permute-start.10
  84.8 1.6 collective-permute-done.10
  86.4 1.5 shard_map.80.fields
  87.8 0.0 copy-done.2
  87.9 9.7 %shard_map.82 = f32[1792,128]{1,0:T(8,128)} custom-call(bf16[128,2560]{1,0:T(8,128)(2,1)S(1)} %shard_map.80.fields, f32[2560,8192]{1,0:T(8,128)} %refs_9_.3, f32[2560,8192]{1,0:T(8,128)} %refs_9_.3, f32[2560,8192]{1,0:T(8,128)} %refs_9_.3, f32[2560,8192]{1,0:T(8,128)} %refs_9_.3, f32[2560,8192]{1,0:T(8,128)} %refs_9_.3, f32[2560,8192]{1,0:T(8,128)} %refs_9_.3, ...), custom_call_target="tpu_custom_call" | custom-call | flops 2013265920 | bytes 20971520 | tf_op jit(solution)/shard_map/pallas_call | solution.py:408
  97.5 3.4 %all-to-all-start.1 = ((f32[32,56,128]{2,1,0:T(8,128)}), f32[32,56,128]{2,1,0:T(8,128)}, u32[]{:S(2)}, u32[]{:S(2)}) async-start(f32[32,56,128]{2,1,0:T(8,128)} %bitcast.6), calls=%async_computation.1 | async-start | bytes 1835008 | tf_op jit(solution)/shard_map/all_to_all | solution.py:527
  100.9 0.0 copy-start.3
  100.9 24.3 %shard_map.83 = f32[3072,128]{1,0:T(8,128)} custom-call(bf16[128,2560]{1,0:T(8,128)(2,1)S(1)} %shard_map.80.fields, f32[2560,8192]{1,0:T(8,128)} %refs_9_.3, f32[2560,8192]{1,0:T(8,128)} %refs_9_.3, f32[2560,8192]{1,0:T(8,128)} %refs_9_.3, f32[2560,8192]{1,0:T(8,128)} %refs_9_.3, f32[2560,8192]{1,0:T(8,128)} %refs_9_.3, f32[2560,8192]{1,0:T(8,128)} %refs_9_.3, ...), custom_call_target="tpu_custom_call" | custom-call | flops 6039797760 | bytes 62914560 | tf_op jit(solution)/shard_map/pallas_call | solution.py:408
  125.2 0.4 all-to-all-done.1.refs_0_
  125.7 5.4 %all-to-all-start.2 = ((f32[32,96,128]{2,1,0:T(8,128)}), f32[32,96,128]{2,1,0:T(8,128)S(1)}, u32[]{:S(2)}, u32[]{:S(2)}) async-start(f32[32,96,128]{2,1,0:T(8,128)} %bitcast.7), calls=%async_computation.2 | async-start | bytes 3145728 | tf_op jit(solution)/shard_map/all_to_all | solution.py:527
  131.0 0.0 copy-done.3
  131.1 1.8 %gather_fusion = f32[2]{0:T(128)} fusion(f32[32,56,128]{2,1,0:T(8,128)} %all-to-all-done.1.refs_0_, s32[2]{0:T(128)S(1)} %fusion.24), kind=kCustom, calls=%fused_computation | custom fusion | bytes 40 | tf_op jit(solution)/shard_map/gather | solution.py:531
  132.9 37.0 %all-to-all-done.2.refs_1_ = f32[32,96,128]{2,1,0:T(8,128)S(1)} async-done(((f32[32,96,128]{2,1,0:T(8,128)}), f32[32,96,128]{2,1,0:T(8,128)S(1)}, u32[]{:S(2)}, u32[]{:S(2)}) %all-to-all-start.2) | async-done | bytes 1572896 | tf_op jit(solution)/shard_map/all_to_all | solution.py:527
  169.9 4.9 %shard_map.84 = f32[2,64,512]{2,1,0:T(8,128)} custom-call(f32[32,56,128]{2,1,0:T(8,128)} %all-to-all-done.1.refs_0_, f32[32,96,128]{2,1,0:T(8,128)S(1)} %all-to-all-done.2.refs_1_), custom_call_target="tpu_custom_call" | custom-call | tf_op jit(solution)/shard_map/pallas_call | solution.py:484
  (13 shorter events, 0.3 us)
Async XLA Ops:
  11.4 37.7 %all-to-all-start = ((f32[32,40,128]{2,1,0:T(8,128)}), f32[32,40,128]{2,1,0:T(8,128)S(1)}, u32[]{:S(2)}, u32[]{:S(2)}) async-start(f32[32,40,128]{2,1,0:T(8,128)} %get-tuple-element.5), calls=%async_computation | async-start | bytes 1310720 | tf_op jit(solution)/shard_map/all_to_all | solution.py:509
  18.9 0.9 copy-start
  19.8 29.3 %copy-start.1 = (f32[2,2560]{1,0:T(2,128)S(1)}, f32[2,2560]{1,0:T(2,128)}, u32[]{:S(2)}) copy-start(f32[2,2560]{1,0:T(2,128)} %refs_12_.1) | copy-start | bytes 61444
  49.1 38.7 %copy-start.2 = (f32[2]{0:T(128)S(1)}, f32[2]{0:T(128)}, u32[]{:S(2)}) copy-start(f32[2]{0:T(128)} %refs_14_.1) | copy-start | bytes 28
  57.2 1.7 collective-permute-start
  58.9 4.6 %collective-permute-start.1 = (f32[8,2560]{1,0:T(8,128)S(1)}, f32[8,2560]{1,0:T(8,128)S(1)}, u32[]{:S(2)}, u32[]{:S(2)}) collective-permute-start(f32[8,2560]{1,0:T(8,128)S(1)} %get-tuple-element.12), channel_id=1, source_target_pairs={{0,8},{1,9},{2,10},{3,11},{4,12},{5,13},{6,14},{7,15},{8,0},{9,1},... | collective-permute-start | bytes 245768 | tf_op jit(solution)/shard_map/ppermute | solution.py:259
  60.6 5.2 %collective-permute-start.2 = (f32[8,2560]{1,0:T(8,128)S(1)}, f32[8,2560]{1,0:T(8,128)S(1)}, u32[]{:S(2)}, u32[]{:S(2)}) collective-permute-start(f32[8,2560]{1,0:T(8,128)S(1)} %get-tuple-element.14), channel_id=1, source_target_pairs={{0,16},{1,17},{2,18},{3,19},{4,20},{5,21},{6,22},{7,23},{8,24},{9,... | collective-permute-start | bytes 245768 | tf_op jit(solution)/shard_map/ppermute | solution.py:259
  62.1 5.3 %collective-permute-start.3 = (f32[8,2560]{1,0:T(8,128)S(1)}, f32[8,2560]{1,0:T(8,128)S(1)}, u32[]{:S(2)}, u32[]{:S(2)}) collective-permute-start(f32[8,2560]{1,0:T(8,128)S(1)} %get-tuple-element.13), channel_id=1, source_target_pairs={{0,24},{1,25},{2,26},{3,27},{4,28},{5,29},{6,30},{7,31},{8,16},{9,... | collective-permute-start | bytes 245768 | tf_op jit(solution)/shard_map/ppermute | solution.py:259
  67.4 4.8 %collective-permute-start.4 = (f32[8,2560]{1,0:T(8,128)S(1)}, f32[8,2560]{1,0:T(8,128)S(1)}, u32[]{:S(2)}, u32[]{:S(2)}) collective-permute-start(f32[8,2560]{1,0:T(8,128)S(1)} %add_add_fusion.1), channel_id=1, source_target_pairs={{0,2},{1,3},{2,0},{3,1},{4,6},{5,7},{6,4},{7,5},{8,10},{9,11},{10,... | collective-permute-start | bytes 245768 | tf_op jit(solution)/shard_map/ppermute | solution.py:259
  69.0 7.1 %collective-permute-start.5 = (f32[8,2560]{1,0:T(8,128)S(1)}, f32[8,2560]{1,0:T(8,128)S(1)}, u32[]{:S(2)}, u32[]{:S(2)}) collective-permute-start(f32[8,2560]{1,0:T(8,128)S(1)} %add_add_fusion.1), channel_id=1, source_target_pairs={{0,4},{1,5},{2,6},{3,7},{4,0},{5,1},{6,2},{7,3},{8,12},{9,13},{10,... | collective-permute-start | bytes 245768 | tf_op jit(solution)/shard_map/ppermute | solution.py:259
  71.4 6.3 %collective-permute-start.6 = (f32[8,2560]{1,0:T(8,128)S(1)}, f32[8,2560]{1,0:T(8,128)S(1)}, u32[]{:S(2)}, u32[]{:S(2)}) collective-permute-start(f32[8,2560]{1,0:T(8,128)S(1)} %add_add_fusion.1), channel_id=1, source_target_pairs={{0,6},{1,7},{2,4},{3,5},{4,2},{5,3},{6,0},{7,1},{8,14},{9,15},{10,... | collective-permute-start | bytes 245768 | tf_op jit(solution)/shard_map/ppermute | solution.py:259
  77.8 4.5 %collective-permute-start.7 = (f32[8,2560]{1,0:T(8,128)S(1)}, f32[8,2560]{1,0:T(8,128)S(1)}, u32[]{:S(2)}, u32[]{:S(2)}) collective-permute-start(f32[8,2560]{1,0:T(8,128)S(1)} %get-tuple-element.9), channel_id=1, source_target_pairs={{0,8},{1,9},{2,10},{3,11},{4,12},{5,13},{6,14},{7,15},{8,0},{9,1},... | collective-permute-start | bytes 245768 | tf_op jit(solution)/shard_map/ppermute | solution.py:259
  78.4 4.4 %collective-permute-start.8 = (f32[8,2560]{1,0:T(8,128)S(1)}, f32[8,2560]{1,0:T(8,128)S(1)}, u32[]{:S(2)}, u32[]{:S(2)}) collective-permute-start(f32[8,2560]{1,0:T(8,128)S(1)} %get-tuple-element.9), channel_id=1, source_target_pairs={{0,16},{1,17},{2,18},{3,19},{4,20},{5,21},{6,22},{7,23},{8,24},{9,... | collective-permute-start | bytes 245768 | tf_op jit(solution)/shard_map/ppermute | solution.py:259
  79.3 5.3 %collective-permute-start.9 = (f32[8,2560]{1,0:T(8,128)S(1)}, f32[8,2560]{1,0:T(8,128)S(1)}, u32[]{:S(2)}, u32[]{:S(2)}) collective-permute-start(f32[8,2560]{1,0:T(8,128)S(1)} %get-tuple-element.9), channel_id=1, source_target_pairs={{0,24},{1,25},{2,26},{3,27},{4,28},{5,29},{6,30},{7,31},{8,16},{9,... | collective-permute-start | bytes 245768 | tf_op jit(solution)/shard_map/ppermute | solution.py:259
  84.6 1.7 collective-permute-start.10
  97.5 28.2 %all-to-all-start.1 = ((f32[32,56,128]{2,1,0:T(8,128)}), f32[32,56,128]{2,1,0:T(8,128)}, u32[]{:S(2)}, u32[]{:S(2)}) async-start(f32[32,56,128]{2,1,0:T(8,128)} %bitcast.6), calls=%async_computation.1 | async-start | bytes 1835008 | tf_op jit(solution)/shard_map/all_to_all | solution.py:527
  100.9 30.1 %copy-start.3 = (s32[2]{0:T(128)S(1)}, s32[2]{0:T(128)}, u32[]{:S(2)}) copy-start(s32[2]{0:T(128)} %parent.1) | copy-start | bytes 28
  125.7 44.2 %all-to-all-start.2 = ((f32[32,96,128]{2,1,0:T(8,128)}), f32[32,96,128]{2,1,0:T(8,128)S(1)}, u32[]{:S(2)}, u32[]{:S(2)}) async-start(f32[32,96,128]{2,1,0:T(8,128)} %bitcast.7), calls=%async_computation.2 | async-start | bytes 3145728 | tf_op jit(solution)/shard_map/all_to_all | solution.py:527

commit v5 on v4

--- a/solution.py
+++ b/solution.py
@@ -17,7 +17,7 @@
 BF16 = jnp.bfloat16
 MIB = 1024 * 1024
 FIRST_UNITS = 1
-HEAD = 512
+HEAD = 768
 PIECE = 128
 
 
@@ -206,53 +206,68 @@
         + [pl.BlockSpec(memory_space=pl.ANY)] * len(more),
         out_specs=pl.BlockSpec((block, columns), lambda g: (g + skip, 0)),
         input_output_aliases={2: 0} if more else {},
-        compiler_params=params(48),
+        compiler_params=params(60),
         cost_estimate=pl.CostEstimate(
             flops=2 * rest * pairs * occupied * 3, bytes_accessed=4 * rest * (pairs + columns), transcendentals=0
         ),
     )(pair, chol, *more)
 
 
-def bias_kernel(own, half, place, rotated, contracted, noise, out, stacked):
+def bias_kernel(own, half, place, rotated, noise, contracted, out, stacked, loaded, sems):
     devices = rotated.shape[0]
     slots = own * devices
-
-    @pl.when(pl.program_id(0) == 0)
-    def _():
-        for i in range(half):
-            for s in range(own):
-                high, low = split(rotated[:, s * half + i, :])
-                at = s * devices
-                stacked[at : at + devices, i * LANES : (i + 1) * LANES] = high
-                stacked[slots + at : slots + at + devices, i * LANES : (i + 1) * LANES] = low
-
-    b_high, b_low = split(contracted[...])
-    both = dot_nt(stacked[...], b_high) + dot_nt(stacked[...], b_low)
-    value = -TIME_ROOT * (both[:slots] + both[slots:])
+    count = sems.shape[0]
+    block = loaded.shape[0] // count
+    copies = []
+    for g in range(count):
+        at = pl.ds(g * block, block)
+        copies.append(pltpu.make_async_copy(contracted.at[at], loaded.at[at], sems.at[g]))
+    for copy in copies:
+        copy.start()
+    for i in range(half):
+        for s in range(own):
+            high, low = split(rotated[:, s * half + i, :])
+            at = s * devices
+            stacked[at : at + devices, i * LANES : (i + 1) * LANES] = high
+            stacked[slots + at : slots + at + devices, i * LANES : (i + 1) * LANES] = low
     rows = jax.lax.broadcasted_iota(jnp.int32, (slots, 1), 0)
-    for s in range(own):
-        value += jnp.where(rows == s * devices + place[0], noise[s : s + 1, :], 0.0)
-    out[...] = value
+
+    def step(g, carry):
+        at = pl.ds(pl.multiple_of(g * block, LANES), block)
+        pltpu.make_async_copy(contracted.at[at], loaded.at[at], sems.at[g]).wait()
+        b_high, b_low = split(loaded[at, :])
+        both = dot_nt(stacked[...], b_high) + dot_nt(stacked[...], b_low)
+        value = -TIME_ROOT * (both[:slots] + both[slots:])
+        for s in range(own):
+            value += jnp.where(rows == s * devices + place[0], noise[s : s + 1, at], 0.0)
+        out[:, at] = value
+        return carry
+
+    lax.fori_loop(0, count, step, 0)
 
 
 def partial_fields(own, half, place, rotated, contracted, noise):
     vectors, columns = contracted.shape
     devices = rotated.shape[0]
-    block = 512
+    count = vectors // 512
     return pl.pallas_call(
         functools.partial(bias_kernel, own, half),
-        grid=(vectors // block,),
+        grid=(1,),
         out_shape=jax.ShapeDtypeStruct((own * devices, vectors), F32),
         in_specs=[
             pl.BlockSpec(memory_space=pltpu.SMEM),
             whole(rotated.shape),
-            pl.BlockSpec((block, columns), lambda g: (g, 0)),
-            pl.BlockSpec((own, block), lambda g: (0, g)),
+            whole(noise.shape),
+            pl.BlockSpec(memory_space=pl.ANY),
         ],
-        out_specs=pl.BlockSpec((own * devices, block), lambda g: (0, g)),
-        scratch_shapes=[pltpu.VMEM((2 * own * devices, columns), BF16)],
-        compiler_params=params(48),
-    )(place, rotated, contracted, noise)
+        out_specs=whole((own * devices, vectors)),
+        scratch_shapes=[
+            pltpu.VMEM((2 * own * devices, columns), BF16),
+            pltpu.VMEM(contracted.shape, F32),
+            pltpu.SemaphoreType.DMA((count,)),
+        ],
+        compiler_params=params(52),
+    )(place, rotated, noise, contracted)
 
 
 def send(x, walk_size, chol_size, target):

time: 176 us -> 172 us (0.977)
  Pallas kernels: 88.8 us -> 86.1 us
    pallas_call x1, Pallas kernels: 29.3 us -> 26.5 us  [contract(): pl.pallas_call(contract_kernel, grid=(rest // block,), out_shape=jax.Shap...]
    pallas_call x1, Pallas kernels: 10.8 us -> 13.1 us  [rotate(): pl.pallas_call(functools.partial(rotate_kernel, devices), grid=(1,), out_...]
    pallas_call x1, Pallas kernels: 8 us -> 5.81 us  [partial_fields(): pl.pallas_call(functools.partial(bias_kernel, own, half), grid=(1,), out_...]
  transfers between devices with their start and end apart: 14 -> 14, of which waited for: 13 -> 13; matrix products, arithmetic and copies ran while one was open for 1% -> 1% of each run, Pallas kernels for 31% -> 30%
where the time goes in v5:
time: 172 us; the launch traced here: 171 us
  Pallas kernels  86.1 us (50%)
  waiting for transfers between devices  53.8 us (31%)
  starting transfers between devices  28.2 us (16%)
  local copies, waits for them, and re-layouts  2.2 us (1%)
    all_to_all x2, waiting for transfers between devices, per_device(): lax.all_to_all(chunk, BOTH, split_axis=0, concat_axis=0, tiled=True)  37.4 us
    pallas_call x2, Pallas kernels, potential_tiles(): pl.pallas_call(functools.partial(potential_kernel, own, parts, base), gri...  34 us
    pallas_call x1, Pallas kernels, contract(): pl.pallas_call(contract_kernel, grid=(rest // block,), out_shape=jax.Shap...  26.5 us
    ppermute x11, waiting for transfers between devices, send(): lax.ppermute(x, BOTH, [(i, target(i)) for i in range(walk_size * chol_siz...  16.4 us
    pallas_call x1, Pallas kernels, rotate(): pl.pallas_call(functools.partial(rotate_kernel, devices), grid=(1,), out_...  13.1 us
    ppermute x11, starting transfers between devices, send(): lax.ppermute(x, BOTH, [(i, target(i)) for i in range(walk_size * chol_siz...  11.9 us
    all_to_all x2, starting transfers between devices, per_device(): lax.all_to_all(chunk, BOTH, split_axis=0, concat_axis=0, tiled=True)  8.86 us
    all_to_all x1, starting transfers between devices, per_device(): lax.all_to_all(sent, BOTH, split_axis=0, concat_axis=0, tiled=True)  7.48 us
  transfers between devices with their start and end apart: 14, of which 13 were waited for; matrix products, arithmetic and copies ran while one was open for 1% of the time, Pallas kernels for 30%

profile of v5, /device:TPU:0, one launch (start us, length us, event | category | flops | bytes accessed | tf_op | source)
XLA Modules:
  0.0 171.4 jit_solution(12604511570196545697)
XLA Ops:
  0.6 13.1 %shard_map.77 = (f32[32,40,128]{2,1,0:T(8,128)}, bf16[512,128]{1,0:T(8,128)(2,1)}, f32[2560,1024]{1,0:T(8,128)}) custom-call(s32[2]{0:T(128)} %parent.1, f32[64,512]{1,0:T(8,128)} %bitcast.11, f32[2,64,512]{2,1,0:T(8,128)} %bitcast.9, f32[2560,8192]{1,0:T(8,128)} %refs_9_.3), custom_call_target="tpu_custom_call" | custom-call | tf_op jit(solution)/shard_map/pallas_call | solution.py:153
  13.7 7.5 %all-to-all-start = ((f32[32,40,128]{2,1,0:T(8,128)}), f32[32,40,128]{2,1,0:T(8,128)S(1)}, u32[]{:S(2)}, u32[]{:S(2)}) async-start(f32[32,40,128]{2,1,0:T(8,128)} %get-tuple-element.5), calls=%async_computation | async-start | bytes 1310720 | tf_op jit(solution)/shard_map/all_to_all | solution.py:524
  21.2 0.0 copy-start
  21.2 26.5 %shard_map.78.contracted = f32[2560,1024]{1,0:T(8,128)} custom-call(bf16[512,128]{1,0:T(8,128)(2,1)} %get-tuple-element.6.pair, f32[2560,8192]{1,0:T(8,128)} %refs_9_.3, f32[2560,1024]{1,0:T(8,128)} %get-tuple-element.7.refs_0_), custom_call_target="tpu_custom_call", output_to_operand_aliasing={{}: (2, {})} | custom-call | flops 5637144576 | bytes 66060288 | tf_op jit(solution)/shard_map/pallas_call | solution.py:201
  47.8 0.0 copy-start.1
  47.8 0.0 all-to-all-done.rotated.received
  47.8 0.0 copy-done
  47.8 5.8 %shard_map.79 = f32[64,2560]{1,0:T(8,128)S(1)} custom-call(s32[1]{0:T(128)} %bitcast.5.place, f32[32,40,128]{2,1,0:T(8,128)S(1)} %all-to-all-done.rotated.received, f32[2,2560]{1,0:T(2,128)S(1)} %copy-done, f32[2560,1024]{1,0:T(8,128)} %shard_map.78.contracted), custom_call_target="tpu_custom_call" | custom-call | tf_op jit(solution)/shard_map/pallas_call | solution.py:253
  53.6 0.2 collective-permute-start
  53.9 1.5 collective-permute-done
  55.4 1.7 collective-permute-start.1
  57.1 1.4 collective-permute-start.2
  58.5 0.4 collective-permute-start.3
  59.0 1.0 collective-permute-done.1
  60.0 2.3 %collective-permute-done.2 = f32[8,2560]{1,0:T(8,128)S(1)} collective-permute-done((f32[8,2560]{1,0:T(8,128)S(1)}, f32[8,2560]{1,0:T(8,128)S(1)}, u32[]{:S(2)}, u32[]{:S(2)}) %collective-permute-start.2) | collective-permute-done | bytes 81952 | tf_op jit(solution)/shard_map/ppermute | solution.py:274
  62.3 1.6 collective-permute-done.3
  63.9 1.6 collective-permute-start.4
  65.4 2.4 %collective-permute-start.5 = (f32[8,2560]{1,0:T(8,128)S(1)}, f32[8,2560]{1,0:T(8,128)S(1)}, u32[]{:S(2)}, u32[]{:S(2)}) collective-permute-start(f32[8,2560]{1,0:T(8,128)S(1)} %add_add_fusion.1), channel_id=1, source_target_pairs={{0,4},{1,5},{2,6},{3,7},{4,0},{5,1},{6,2},{7,3},{8,12},{9,13},{10,... | collective-permute-start | bytes 245768 | tf_op jit(solution)/shard_map/ppermute | solution.py:274
  67.9 0.5 collective-permute-start.6
  68.3 0.1 copy.19
  68.4 0.1 convert_element_type.27
  68.5 0.2 collective-permute-done.4
  68.8 3.8 %collective-permute-done.5 = f32[8,2560]{1,0:T(8,128)S(1)} collective-permute-done((f32[8,2560]{1,0:T(8,128)S(1)}, f32[8,2560]{1,0:T(8,128)S(1)}, u32[]{:S(2)}, u32[]{:S(2)}) %collective-permute-start.5) | collective-permute-done | bytes 81952 | tf_op jit(solution)/shard_map/ppermute | solution.py:274
  72.5 1.7 collective-permute-done.6
  74.2 0.6 collective-permute-start.7
  74.8 0.9 collective-permute-start.8
  75.7 2.1 %collective-permute-start.9 = (f32[8,2560]{1,0:T(8,128)S(1)}, f32[8,2560]{1,0:T(8,128)S(1)}, u32[]{:S(2)}, u32[]{:S(2)}) collective-permute-start(f32[8,2560]{1,0:T(8,128)S(1)} %get-tuple-element.9), channel_id=1, source_target_pairs={{0,24},{1,25},{2,26},{3,27},{4,28},{5,29},{6,30},{7,31},{8,16},{9,... | collective-permute-start | bytes 245768 | tf_op jit(solution)/shard_map/ppermute | solution.py:274
  77.8 0.1 fusion.5
  77.9 0.3 shard_map.81.refs_10_
  78.2 0.5 collective-permute-done.7
  78.7 0.5 collective-permute-done.8
  79.3 1.8 %collective-permute-done.9 = f32[8,2560]{1,0:T(8,128)S(1)} collective-permute-done((f32[8,2560]{1,0:T(8,128)S(1)}, f32[8,2560]{1,0:T(8,128)S(1)}, u32[]{:S(2)}, u32[]{:S(2)}) %collective-permute-start.9) | collective-permute-done | bytes 81952 | tf_op jit(solution)/shard_map/ppermute | solution.py:274
  81.1 0.1 collective-permute-start.10
  81.2 1.6 collective-permute-done.10
  82.8 1.4 shard_map.80.fields
  84.2 0.0 copy-done.1
  84.3 9.6 %shard_map.82 = f32[1792,128]{1,0:T(8,128)} custom-call(bf16[128,2560]{1,0:T(8,128)(2,1)S(1)} %shard_map.80.fields, f32[2560,8192]{1,0:T(8,128)} %refs_9_.3, f32[2560,8192]{1,0:T(8,128)} %refs_9_.3, f32[2560,8192]{1,0:T(8,128)} %refs_9_.3, f32[2560,8192]{1,0:T(8,128)} %refs_9_.3, f32[2560,8192]{1,0:T(8,128)} %refs_9_.3, f32[2560,8192]{1,0:T(8,128)} %refs_9_.3, ...), custom_call_target="tpu_custom_call" | custom-call | flops 2013265920 | bytes 20971520 | tf_op jit(solution)/shard_map/pallas_call | solution.py:423
  93.9 3.5 %all-to-all-start.1 = ((f32[32,56,128]{2,1,0:T(8,128)}), f32[32,56,128]{2,1,0:T(8,128)}, u32[]{:S(2)}, u32[]{:S(2)}) async-start(f32[32,56,128]{2,1,0:T(8,128)} %bitcast.6), calls=%async_computation.1 | async-start | bytes 1835008 | tf_op jit(solution)/shard_map/all_to_all | solution.py:542
  97.4 0.0 copy-start.2
  97.4 24.3 %shard_map.83 = f32[3072,128]{1,0:T(8,128)} custom-call(bf16[128,2560]{1,0:T(8,128)(2,1)S(1)} %shard_map.80.fields, f32[2560,8192]{1,0:T(8,128)} %refs_9_.3, f32[2560,8192]{1,0:T(8,128)} %refs_9_.3, f32[2560,8192]{1,0:T(8,128)} %refs_9_.3, f32[2560,8192]{1,0:T(8,128)} %refs_9_.3, f32[2560,8192]{1,0:T(8,128)} %refs_9_.3, f32[2560,8192]{1,0:T(8,128)} %refs_9_.3, ...), custom_call_target="tpu_custom_call" | custom-call | flops 6039797760 | bytes 62914560 | tf_op jit(solution)/shard_map/pallas_call | solution.py:423
  121.8 0.4 all-to-all-done.1.refs_0_
  122.2 5.4 %all-to-all-start.2 = ((f32[32,96,128]{2,1,0:T(8,128)}), f32[32,96,128]{2,1,0:T(8,128)S(1)}, u32[]{:S(2)}, u32[]{:S(2)}) async-start(f32[32,96,128]{2,1,0:T(8,128)} %bitcast.7), calls=%async_computation.2 | async-start | bytes 3145728 | tf_op jit(solution)/shard_map/all_to_all | solution.py:542
  127.5 0.0 copy-done.2
  127.6 1.9 %gather_fusion = f32[2]{0:T(128)} fusion(f32[32,56,128]{2,1,0:T(8,128)} %all-to-all-done.1.refs_0_, s32[2]{0:T(128)S(1)} %fusion.24), kind=kCustom, calls=%fused_computation | custom fusion | bytes 40 | tf_op jit(solution)/shard_map/gather | solution.py:546
  129.5 37.0 %all-to-all-done.2.refs_1_ = f32[32,96,128]{2,1,0:T(8,128)S(1)} async-done(((f32[32,96,128]{2,1,0:T(8,128)}), f32[32,96,128]{2,1,0:T(8,128)S(1)}, u32[]{:S(2)}, u32[]{:S(2)}) %all-to-all-start.2) | async-done | bytes 1572896 | tf_op jit(solution)/shard_map/all_to_all | solution.py:542
  166.4 4.9 %shard_map.84 = f32[2,64,512]{2,1,0:T(8,128)} custom-call(f32[32,56,128]{2,1,0:T(8,128)} %all-to-all-done.1.refs_0_, f32[32,96,128]{2,1,0:T(8,128)S(1)} %all-to-all-done.2.refs_1_), custom_call_target="tpu_custom_call" | custom-call | tf_op jit(solution)/shard_map/pallas_call | solution.py:499
  (13 shorter events, 0.3 us)
Async XLA Ops:
  13.7 34.1 %all-to-all-start = ((f32[32,40,128]{2,1,0:T(8,128)}), f32[32,40,128]{2,1,0:T(8,128)S(1)}, u32[]{:S(2)}, u32[]{:S(2)}) async-start(f32[32,40,128]{2,1,0:T(8,128)} %get-tuple-element.5), calls=%async_computation | async-start | bytes 1310720 | tf_op jit(solution)/shard_map/all_to_all | solution.py:524
  21.2 26.5 %copy-start = (f32[2,2560]{1,0:T(2,128)S(1)}, f32[2,2560]{1,0:T(2,128)}, u32[]{:S(2)}) copy-start(f32[2,2560]{1,0:T(2,128)} %refs_12_.1) | copy-start | bytes 61444
  47.8 36.5 %copy-start.1 = (f32[2]{0:T(128)S(1)}, f32[2]{0:T(128)}, u32[]{:S(2)}) copy-start(f32[2]{0:T(128)} %refs_14_.1) | copy-start | bytes 28
  53.6 1.7 collective-permute-start
  55.4 4.6 %collective-permute-start.1 = (f32[8,2560]{1,0:T(8,128)S(1)}, f32[8,2560]{1,0:T(8,128)S(1)}, u32[]{:S(2)}, u32[]{:S(2)}) collective-permute-start(f32[8,2560]{1,0:T(8,128)S(1)} %get-tuple-element.12), channel_id=1, source_target_pairs={{0,8},{1,9},{2,10},{3,11},{4,12},{5,13},{6,14},{7,15},{8,0},{9,1},... | collective-permute-start | bytes 245768 | tf_op jit(solution)/shard_map/ppermute | solution.py:274
  57.1 5.2 %collective-permute-start.2 = (f32[8,2560]{1,0:T(8,128)S(1)}, f32[8,2560]{1,0:T(8,128)S(1)}, u32[]{:S(2)}, u32[]{:S(2)}) collective-permute-start(f32[8,2560]{1,0:T(8,128)S(1)} %get-tuple-element.14), channel_id=1, source_target_pairs={{0,16},{1,17},{2,18},{3,19},{4,20},{5,21},{6,22},{7,23},{8,24},{9,... | collective-permute-start | bytes 245768 | tf_op jit(solution)/shard_map/ppermute | solution.py:274
  58.5 5.3 %collective-permute-start.3 = (f32[8,2560]{1,0:T(8,128)S(1)}, f32[8,2560]{1,0:T(8,128)S(1)}, u32[]{:S(2)}, u32[]{:S(2)}) collective-permute-start(f32[8,2560]{1,0:T(8,128)S(1)} %get-tuple-element.13), channel_id=1, source_target_pairs={{0,24},{1,25},{2,26},{3,27},{4,28},{5,29},{6,30},{7,31},{8,16},{9,... | collective-permute-start | bytes 245768 | tf_op jit(solution)/shard_map/ppermute | solution.py:274
  63.9 4.9 %collective-permute-start.4 = (f32[8,2560]{1,0:T(8,128)S(1)}, f32[8,2560]{1,0:T(8,128)S(1)}, u32[]{:S(2)}, u32[]{:S(2)}) collective-permute-start(f32[8,2560]{1,0:T(8,128)S(1)} %add_add_fusion.1), channel_id=1, source_target_pairs={{0,2},{1,3},{2,0},{3,1},{4,6},{5,7},{6,4},{7,5},{8,10},{9,11},{10,... | collective-permute-start | bytes 245768 | tf_op jit(solution)/shard_map/ppermute | solution.py:274
  65.4 7.1 %collective-permute-start.5 = (f32[8,2560]{1,0:T(8,128)S(1)}, f32[8,2560]{1,0:T(8,128)S(1)}, u32[]{:S(2)}, u32[]{:S(2)}) collective-permute-start(f32[8,2560]{1,0:T(8,128)S(1)} %add_add_fusion.1), channel_id=1, source_target_pairs={{0,4},{1,5},{2,6},{3,7},{4,0},{5,1},{6,2},{7,3},{8,12},{9,13},{10,... | collective-permute-start | bytes 245768 | tf_op jit(solution)/shard_map/ppermute | solution.py:274
  67.9 6.3 %collective-permute-start.6 = (f32[8,2560]{1,0:T(8,128)S(1)}, f32[8,2560]{1,0:T(8,128)S(1)}, u32[]{:S(2)}, u32[]{:S(2)}) collective-permute-start(f32[8,2560]{1,0:T(8,128)S(1)} %add_add_fusion.1), channel_id=1, source_target_pairs={{0,6},{1,7},{2,4},{3,5},{4,2},{5,3},{6,0},{7,1},{8,14},{9,15},{10,... | collective-permute-start | bytes 245768 | tf_op jit(solution)/shard_map/ppermute | solution.py:274
  74.2 4.5 %collective-permute-start.7 = (f32[8,2560]{1,0:T(8,128)S(1)}, f32[8,2560]{1,0:T(8,128)S(1)}, u32[]{:S(2)}, u32[]{:S(2)}) collective-permute-start(f32[8,2560]{1,0:T(8,128)S(1)} %get-tuple-element.9), channel_id=1, source_target_pairs={{0,8},{1,9},{2,10},{3,11},{4,12},{5,13},{6,14},{7,15},{8,0},{9,1},... | collective-permute-start | bytes 245768 | tf_op jit(solution)/shard_map/ppermute | solution.py:274
  74.8 4.4 %collective-permute-start.8 = (f32[8,2560]{1,0:T(8,128)S(1)}, f32[8,2560]{1,0:T(8,128)S(1)}, u32[]{:S(2)}, u32[]{:S(2)}) collective-permute-start(f32[8,2560]{1,0:T(8,128)S(1)} %get-tuple-element.9), channel_id=1, source_target_pairs={{0,16},{1,17},{2,18},{3,19},{4,20},{5,21},{6,22},{7,23},{8,24},{9,... | collective-permute-start | bytes 245768 | tf_op jit(solution)/shard_map/ppermute | solution.py:274
  75.7 5.3 %collective-permute-start.9 = (f32[8,2560]{1,0:T(8,128)S(1)}, f32[8,2560]{1,0:T(8,128)S(1)}, u32[]{:S(2)}, u32[]{:S(2)}) collective-permute-start(f32[8,2560]{1,0:T(8,128)S(1)} %get-tuple-element.9), channel_id=1, source_target_pairs={{0,24},{1,25},{2,26},{3,27},{4,28},{5,29},{6,30},{7,31},{8,16},{9,... | collective-permute-start | bytes 245768 | tf_op jit(solution)/shard_map/ppermute | solution.py:274
  81.1 1.7 collective-permute-start.10
  93.9 28.3 %all-to-all-start.1 = ((f32[32,56,128]{2,1,0:T(8,128)}), f32[32,56,128]{2,1,0:T(8,128)}, u32[]{:S(2)}, u32[]{:S(2)}) async-start(f32[32,56,128]{2,1,0:T(8,128)} %bitcast.6), calls=%async_computation.1 | async-start | bytes 1835008 | tf_op jit(solution)/shard_map/all_to_all | solution.py:542
  97.4 30.1 %copy-start.2 = (s32[2]{0:T(128)S(1)}, s32[2]{0:T(128)}, u32[]{:S(2)}) copy-start(s32[2]{0:T(128)} %parent.1) | copy-start | bytes 28
  122.2 44.2 %all-to-all-start.2 = ((f32[32,96,128]{2,1,0:T(8,128)}), f32[32,96,128]{2,1,0:T(8,128)S(1)}, u32[]{:S(2)}, u32[]{:S(2)}) async-start(f32[32,96,128]{2,1,0:T(8,128)} %bitcast.7), calls=%async_computation.2 | async-start | bytes 3145728 | tf_op jit(solution)/shard_map/all_to_all | solution.py:542

commit v6 on v5

--- a/solution.py
+++ b/solution.py
@@ -314,30 +314,19 @@
     return ((row // half) ^ core) * half + ((inside // quarter) ^ walk) * quarter + inside % quarter
 
 
-def select_kernel(rows, fields, out):
-    slots = fields.shape[0]
+def select(rows, summed, out):
+    slots, vectors = summed.shape
     lane = jax.lax.broadcasted_iota(jnp.int32, (slots, slots), 1)
     pick = jnp.where(lane == rows[...], 1.0, 0.0).astype(BF16)
-    value = fields[...]
-    first, rest = split(value)
-    second, third = split(value - first.astype(F32))
-    picked = dot(pick, first) + dot(pick, second) + dot(pick, third)
-    high, low = split(TIME_ROOT * picked)
-    out[:slots, :] = high
-    out[slots:, :] = low
-
-
-def select(rows, fields):
-    slots, vectors = fields.shape
     block = 512
-    return pl.pallas_call(
-        select_kernel,
-        grid=(vectors // block,),
-        out_shape=jax.ShapeDtypeStruct((2 * slots, vectors), BF16),
-        in_specs=[whole((slots, 1)), pl.BlockSpec((slots, block), lambda g: (0, g))],
-        out_specs=pl.BlockSpec((2 * slots, block), lambda g: (0, g)),
-        compiler_params=params(16),
-    )(rows.reshape(slots, 1), fields)
+    for g in range(0, vectors, block):
+        value = summed[:, g : g + block]
+        first, rest = split(value)
+        second, third = split(value - first.astype(F32))
+        picked = dot(pick, first) + dot(pick, second) + dot(pick, third)
+        high, low = split(TIME_ROOT * picked)
+        out[:slots, g : g + block] = high
+        out[slots:, g : g + block] = low
 
 
 def carry_kernel(own, half, rows, received, out):
@@ -367,8 +356,17 @@
     )(rows.reshape(-1, 1), received)
 
 
-def potential_kernel(own, parts, base, fields, *refs):
-    chols, out = refs[:parts], refs[-1]
+def potential_kernel(own, parts, base, *refs):
+    chols = refs[:parts]
+    if len(refs) == parts + 2:
+        fields, out = refs[parts:]
+    else:
+        orbital_rows, summed, noise, rows, places, levels, out, fields = refs[parts:]
+
+        @pl.when(pl.program_id(0) == 0)
+        def _():
+            select(rows, summed, fields)
+
     slots = fields.shape[0] // 2
     devices = slots // own
     unit = SUBLANES // own
@@ -388,9 +386,8 @@
         for s in range(own):
             at = pl.ds(start + t * SUBLANES + s * unit, devices, stride=stride)
             out[at, :] = total[s * devices : (s + 1) * devices, t * LANES : (t + 1) * LANES]
-    if len(refs) == parts + 1:
+    if len(refs) == parts + 2:
         return
-    orbital_rows, summed, noise, places, levels = refs[parts:-1]
 
     @pl.when(here == 0)
     def _():
@@ -409,32 +406,35 @@
 
 def potential_tiles(own, fields, chol, orbitals, first, count, along):
     vectors = chol.shape[0]
-    slots = fields.shape[0] // 2
+    slots = along[1].shape[0] if along else fields.shape[0] // 2
     step = 256
     parts = vectors // step
     devices = slots // own
     base = own * count * orbitals // LANES
     rows = devices * base
     smem = pl.BlockSpec(memory_space=pltpu.SMEM)
-    more = []
+    more, shapes = along, []
+    specs = [whole(fields.shape)] if not along else [whole(a.shape) for a in along[:4]] + [smem, smem]
     if along:
         rows += devices * eights(along[0].shape[0] + 1)
-        more = [whole(a.shape) for a in along[:3]] + [smem, smem]
+        shapes = [jax.ShapeDtypeStruct((2 * slots, vectors), BF16)]
+    else:
+        more = (fields,)
+    shapes = [jax.ShapeDtypeStruct((rows, LANES), F32)] + shapes
     return pl.pallas_call(
         functools.partial(potential_kernel, own, parts, base),
         grid=(count,),
-        out_shape=jax.ShapeDtypeStruct((rows, LANES), F32),
-        in_specs=[whole(fields.shape)]
-        + [pl.BlockSpec((step, orbitals), lambda i, p=p: (p, first + i)) for p in range(parts)]
-        + more,
-        out_specs=whole((rows, LANES)),
+        out_shape=shapes,
+        in_specs=[pl.BlockSpec((step, orbitals), lambda i, p=p: (p, first + i)) for p in range(parts)]
+        + specs,
+        out_specs=[whole(shape.shape) for shape in shapes],
         compiler_params=params(32),
         cost_estimate=pl.CostEstimate(
             flops=2 * slots * vectors * orbitals * count * 3,
             bytes_accessed=4 * vectors * orbitals * count,
             transcendentals=0,
         ),
-    )(fields, *[chol] * parts, *along)
+    )(*[chol] * parts, *more)
 
 
 def taylor_kernel(own, chunks, base, *refs):
@@ -528,7 +528,8 @@
 
     parents = rotated[:, 2 * own * half, :own].T.reshape(own * devices).astype(jnp.int32)
     orbital_rows = carry(own, half, (parents % own) * devices + parents // own, rotated)
-    scaled = select(row_of(parents, own, walk_size, chol_size), fields)
+    parent_rows = row_of(parents, own, walk_size, chol_size).reshape(-1, 1)
+    scaled = []
     places = row_of(place * own + jnp.arange(own, dtype=jnp.int32), own, walk_size, chol_size)
 
     unit = SUBLANES // own
@@ -536,8 +537,11 @@
     cuts = [0] + ([FIRST_UNITS] if units > FIRST_UNITS else []) + [units]
     tiles = []
     for begin, end in zip(cuts[:-1], cuts[1:]):
-        along = () if begin else (orbital_rows, fields, field_noise, places, log_weight)
-        chunk = potential_tiles(own, scaled, chol, orbitals, begin * unit, (end - begin) * unit, along)
+        along = () if begin else (orbital_rows, fields, field_noise, parent_rows, places, log_weight)
+        chunk, *more = potential_tiles(
+            own, scaled[0] if begin else None, chol, orbitals, begin * unit, (end - begin) * unit, along
+        )
+        scaled += more
         chunk = chunk.reshape(devices, -1, LANES)
         tiles.append(lax.all_to_all(chunk, BOTH, split_axis=0, concat_axis=0, tiled=True))
 

time: 172 us -> 171 us (level)
  no operation moved by 1% of the time
where the time goes in v6:
time: 171 us; the launch traced here: 170 us
  Pallas kernels  85.2 us (50%)
  waiting for transfers between devices  53.8 us (31%)
  starting transfers between devices  28.1 us (16%)
  local copies, waits for them, and re-layouts  2.2 us (1%)
    all_to_all x2, waiting for transfers between devices, per_device(): lax.all_to_all(chunk, BOTH, split_axis=0, concat_axis=0, tiled=True)  37.4 us
    pallas_call x2, Pallas kernels, potential_tiles(): pl.pallas_call(functools.partial(potential_kernel, own, parts, base), gri...  34.5 us
    pallas_call x1, Pallas kernels, contract(): pl.pallas_call(contract_kernel, grid=(rest // block,), out_shape=jax.Shap...  26.5 us
    ppermute x11, waiting for transfers between devices, send(): lax.ppermute(x, BOTH, [(i, target(i)) for i in range(walk_size * chol_siz...  16.4 us
    pallas_call x1, Pallas kernels, rotate(): pl.pallas_call(functools.partial(rotate_kernel, devices), grid=(1,), out_...  13.1 us
    ppermute x11, starting transfers between devices, send(): lax.ppermute(x, BOTH, [(i, target(i)) for i in range(walk_size * chol_siz...  11.9 us
    all_to_all x2, starting transfers between devices, per_device(): lax.all_to_all(chunk, BOTH, split_axis=0, concat_axis=0, tiled=True)  8.73 us
    all_to_all x1, starting transfers between devices, per_device(): lax.all_to_all(sent, BOTH, split_axis=0, concat_axis=0, tiled=True)  7.48 us
  transfers between devices with their start and end apart: 14, of which 13 were waited for; matrix products, arithmetic and copies ran while one was open for 1% of the time, Pallas kernels for 30%

profile of v6, /device:TPU:0, one launch (start us, length us, event | category | flops | bytes accessed | tf_op | source)
XLA Modules:
  0.0 170.3 jit_solution(16949290608292666080)
XLA Ops:
  0.6 13.1 %shard_map.77 = (f32[32,40,128]{2,1,0:T(8,128)}, bf16[512,128]{1,0:T(8,128)(2,1)}, f32[2560,1024]{1,0:T(8,128)}) custom-call(s32[2]{0:T(128)} %parent.1, f32[64,512]{1,0:T(8,128)} %bitcast.11, f32[2,64,512]{2,1,0:T(8,128)} %bitcast.9, f32[2560,8192]{1,0:T(8,128)} %refs_9_.3), custom_call_target="tpu_custom_call" | custom-call | tf_op jit(solution)/shard_map/pallas_call | solution.py:153
  13.7 7.5 %all-to-all-start = ((f32[32,40,128]{2,1,0:T(8,128)}), f32[32,40,128]{2,1,0:T(8,128)S(1)}, u32[]{:S(2)}, u32[]{:S(2)}) async-start(f32[32,40,128]{2,1,0:T(8,128)} %get-tuple-element.7), calls=%async_computation | async-start | bytes 1310720 | tf_op jit(solution)/shard_map/all_to_all | solution.py:524
  21.2 0.0 copy-start
  21.2 26.5 %shard_map.79.contracted = f32[2560,1024]{1,0:T(8,128)} custom-call(bf16[512,128]{1,0:T(8,128)(2,1)} %get-tuple-element.8.pair, f32[2560,8192]{1,0:T(8,128)} %refs_9_.3, f32[2560,1024]{1,0:T(8,128)} %get-tuple-element.9.refs_0_), custom_call_target="tpu_custom_call", output_to_operand_aliasing={{}: (2, {})} | custom-call | flops 5637144576 | bytes 66060288 | tf_op jit(solution)/shard_map/pallas_call | solution.py:201
  47.8 0.0 copy-start.1
  47.8 0.0 all-to-all-done.received.rotated
  47.8 0.0 copy-done
  47.8 5.8 %shard_map.80 = f32[64,2560]{1,0:T(8,128)S(1)} custom-call(s32[1]{0:T(128)} %bitcast.5.place, f32[32,40,128]{2,1,0:T(8,128)S(1)} %all-to-all-done.received.rotated, f32[2,2560]{1,0:T(2,128)S(1)} %copy-done, f32[2560,1024]{1,0:T(8,128)} %shard_map.79.contracted), custom_call_target="tpu_custom_call" | custom-call | tf_op jit(solution)/shard_map/pallas_call | solution.py:253
  53.6 0.2 collective-permute-start
  53.9 1.5 collective-permute-done
  55.4 1.8 %collective-permute-start.1 = (f32[8,2560]{1,0:T(8,128)S(1)}, f32[8,2560]{1,0:T(8,128)S(1)}, u32[]{:S(2)}, u32[]{:S(2)}) collective-permute-start(f32[8,2560]{1,0:T(8,128)S(1)} %get-tuple-element.16), channel_id=1, source_target_pairs={{0,8},{1,9},{2,10},{3,11},{4,12},{5,13},{6,14},{7,15},{8,0},{9,1},... | collective-permute-start | bytes 245768 | tf_op jit(solution)/shard_map/ppermute | solution.py:274
  57.1 1.4 collective-permute-start.2
  58.6 0.4 collective-permute-start.3
  59.0 1.0 collective-permute-done.1
  60.0 2.3 %collective-permute-done.2 = f32[8,2560]{1,0:T(8,128)S(1)} collective-permute-done((f32[8,2560]{1,0:T(8,128)S(1)}, f32[8,2560]{1,0:T(8,128)S(1)}, u32[]{:S(2)}, u32[]{:S(2)}) %collective-permute-start.2) | collective-permute-done | bytes 81952 | tf_op jit(solution)/shard_map/ppermute | solution.py:274
  62.3 1.6 collective-permute-done.3
  63.9 1.5 collective-permute-start.4
  65.4 2.5 %collective-permute-start.5 = (f32[8,2560]{1,0:T(8,128)S(1)}, f32[8,2560]{1,0:T(8,128)S(1)}, u32[]{:S(2)}, u32[]{:S(2)}) collective-permute-start(f32[8,2560]{1,0:T(8,128)S(1)} %add_add_fusion.1), channel_id=1, source_target_pairs={{0,4},{1,5},{2,6},{3,7},{4,0},{5,1},{6,2},{7,3},{8,12},{9,13},{10,... | collective-permute-start | bytes 245768 | tf_op jit(solution)/shard_map/ppermute | solution.py:274
  67.9 0.5 collective-permute-start.6
  68.4 0.1 copy.19
  68.5 0.1 convert_element_type.27
  68.6 0.1 collective-permute-done.4
  68.7 3.9 %collective-permute-done.5 = f32[8,2560]{1,0:T(8,128)S(1)} collective-permute-done((f32[8,2560]{1,0:T(8,128)S(1)}, f32[8,2560]{1,0:T(8,128)S(1)}, u32[]{:S(2)}, u32[]{:S(2)}) %collective-permute-start.5) | collective-permute-done | bytes 81952 | tf_op jit(solution)/shard_map/ppermute | solution.py:274
  72.5 1.7 %collective-permute-done.6 = f32[8,2560]{1,0:T(8,128)S(1)} collective-permute-done((f32[8,2560]{1,0:T(8,128)S(1)}, f32[8,2560]{1,0:T(8,128)S(1)}, u32[]{:S(2)}, u32[]{:S(2)}) %collective-permute-start.6) | collective-permute-done | bytes 81952 | tf_op jit(solution)/shard_map/ppermute | solution.py:274
  74.3 0.6 collective-permute-start.7
  74.9 0.9 collective-permute-start.8
  75.7 2.1 %collective-permute-start.9 = (f32[8,2560]{1,0:T(8,128)S(1)}, f32[8,2560]{1,0:T(8,128)S(1)}, u32[]{:S(2)}, u32[]{:S(2)}) collective-permute-start(f32[8,2560]{1,0:T(8,128)S(1)} %get-tuple-element.15), channel_id=1, source_target_pairs={{0,24},{1,25},{2,26},{3,27},{4,28},{5,29},{6,30},{7,31},{8,16},{9,... | collective-permute-start | bytes 245768 | tf_op jit(solution)/shard_map/ppermute | solution.py:274
  77.8 0.1 fusion.5
  77.9 0.3 shard_map.78.refs_10_
  78.3 0.5 collective-permute-done.7
  78.8 0.5 collective-permute-done.8
  79.3 1.8 %collective-permute-done.9 = f32[8,2560]{1,0:T(8,128)S(1)} collective-permute-done((f32[8,2560]{1,0:T(8,128)S(1)}, f32[8,2560]{1,0:T(8,128)S(1)}, u32[]{:S(2)}, u32[]{:S(2)}) %collective-permute-start.9) | collective-permute-done | bytes 81952 | tf_op jit(solution)/shard_map/ppermute | solution.py:274
  81.1 0.1 collective-permute-start.10
  81.2 1.6 collective-permute-done.10
  82.8 0.0 copy-done.1
  82.8 10.1 %shard_map.81 = (f32[1792,128]{1,0:T(8,128)}, bf16[128,2560]{1,0:T(8,128)(2,1)S(1)}) custom-call(f32[2560,8192]{1,0:T(8,128)} %refs_9_.3, f32[2560,8192]{1,0:T(8,128)} %refs_9_.3, f32[2560,8192]{1,0:T(8,128)} %refs_9_.3, f32[2560,8192]{1,0:T(8,128)} %refs_9_.3, f32[2560,8192]{1,0:T(8,128)} %refs_9_.3, f32[2560,8192]{1,0:T(8,128)} %refs_9_.3, ...), custom_call_target="tpu_custom_call" | custom-call | flops 2013265920 | bytes 20971520 | tf_op jit(solution)/shard_map/pallas_call | solution.py:424
  93.0 3.4 %all-to-all-start.1 = ((f32[32,56,128]{2,1,0:T(8,128)}), f32[32,56,128]{2,1,0:T(8,128)}, u32[]{:S(2)}, u32[]{:S(2)}) async-start(f32[32,56,128]{2,1,0:T(8,128)} %bitcast.6), calls=%async_computation.1 | async-start | bytes 1835008 | tf_op jit(solution)/shard_map/all_to_all | solution.py:546
  96.3 0.0 copy-start.2
  96.4 24.3 %shard_map.82 = f32[3072,128]{1,0:T(8,128)} custom-call(f32[2560,8192]{1,0:T(8,128)} %refs_9_.3, f32[2560,8192]{1,0:T(8,128)} %refs_9_.3, f32[2560,8192]{1,0:T(8,128)} %refs_9_.3, f32[2560,8192]{1,0:T(8,128)} %refs_9_.3, f32[2560,8192]{1,0:T(8,128)} %refs_9_.3, f32[2560,8192]{1,0:T(8,128)} %refs_9_.3, f32[2560,8192]{1,0:T(8,128)} %refs_9_.3, ...), custom_call_target="tpu_custom_call" | custom-call | flops 6039797760 | bytes 62914560 | tf_op jit(solution)/shard_map/pallas_call | solution.py:424
  120.7 0.4 all-to-all-done.1.refs_0_
  121.1 5.4 %all-to-all-start.2 = ((f32[32,96,128]{2,1,0:T(8,128)}), f32[32,96,128]{2,1,0:T(8,128)S(1)}, u32[]{:S(2)}, u32[]{:S(2)}) async-start(f32[32,96,128]{2,1,0:T(8,128)} %bitcast.7), calls=%async_computation.2 | async-start | bytes 3145728 | tf_op jit(solution)/shard_map/all_to_all | solution.py:546
  126.5 0.0 copy-done.2
  126.5 1.9 %gather_fusion = f32[2]{0:T(128)} fusion(f32[32,56,128]{2,1,0:T(8,128)} %all-to-all-done.1.refs_0_, s32[2]{0:T(128)S(1)} %fusion.24), kind=kCustom, calls=%fused_computation | custom fusion | bytes 40 | tf_op jit(solution)/shard_map/gather | solution.py:550
  128.4 36.9 %all-to-all-done.2.refs_1_ = f32[32,96,128]{2,1,0:T(8,128)S(1)} async-done(((f32[32,96,128]{2,1,0:T(8,128)}), f32[32,96,128]{2,1,0:T(8,128)S(1)}, u32[]{:S(2)}, u32[]{:S(2)}) %all-to-all-start.2) | async-done | bytes 1572896 | tf_op jit(solution)/shard_map/all_to_all | solution.py:546
  165.3 4.9 %shard_map.83 = f32[2,64,512]{2,1,0:T(8,128)} custom-call(f32[32,56,128]{2,1,0:T(8,128)} %all-to-all-done.1.refs_0_, f32[32,96,128]{2,1,0:T(8,128)S(1)} %all-to-all-done.2.refs_1_), custom_call_target="tpu_custom_call" | custom-call | tf_op jit(solution)/shard_map/pallas_call | solution.py:499
  (13 shorter events, 0.3 us)
Async XLA Ops:
  13.7 34.0 %all-to-all-start = ((f32[32,40,128]{2,1,0:T(8,128)}), f32[32,40,128]{2,1,0:T(8,128)S(1)}, u32[]{:S(2)}, u32[]{:S(2)}) async-start(f32[32,40,128]{2,1,0:T(8,128)} %get-tuple-element.7), calls=%async_computation | async-start | bytes 1310720 | tf_op jit(solution)/shard_map/all_to_all | solution.py:524
  21.2 26.5 %copy-start = (f32[2,2560]{1,0:T(2,128)S(1)}, f32[2,2560]{1,0:T(2,128)}, u32[]{:S(2)}) copy-start(f32[2,2560]{1,0:T(2,128)} %refs_12_.1) | copy-start | bytes 61444
  47.8 35.1 %copy-start.1 = (f32[2]{0:T(128)S(1)}, f32[2]{0:T(128)}, u32[]{:S(2)}) copy-start(f32[2]{0:T(128)} %refs_15_.1) | copy-start | bytes 28
  53.6 1.7 collective-permute-start
  55.4 4.6 %collective-permute-start.1 = (f32[8,2560]{1,0:T(8,128)S(1)}, f32[8,2560]{1,0:T(8,128)S(1)}, u32[]{:S(2)}, u32[]{:S(2)}) collective-permute-start(f32[8,2560]{1,0:T(8,128)S(1)} %get-tuple-element.16), channel_id=1, source_target_pairs={{0,8},{1,9},{2,10},{3,11},{4,12},{5,13},{6,14},{7,15},{8,0},{9,1},... | collective-permute-start | bytes 245768 | tf_op jit(solution)/shard_map/ppermute | solution.py:274
  57.1 5.2 %collective-permute-start.2 = (f32[8,2560]{1,0:T(8,128)S(1)}, f32[8,2560]{1,0:T(8,128)S(1)}, u32[]{:S(2)}, u32[]{:S(2)}) collective-permute-start(f32[8,2560]{1,0:T(8,128)S(1)} %get-tuple-element.18), channel_id=1, source_target_pairs={{0,16},{1,17},{2,18},{3,19},{4,20},{5,21},{6,22},{7,23},{8,24},{9,... | collective-permute-start | bytes 245768 | tf_op jit(solution)/shard_map/ppermute | solution.py:274
  58.6 5.3 %collective-permute-start.3 = (f32[8,2560]{1,0:T(8,128)S(1)}, f32[8,2560]{1,0:T(8,128)S(1)}, u32[]{:S(2)}, u32[]{:S(2)}) collective-permute-start(f32[8,2560]{1,0:T(8,128)S(1)} %get-tuple-element.17), channel_id=1, source_target_pairs={{0,24},{1,25},{2,26},{3,27},{4,28},{5,29},{6,30},{7,31},{8,16},{9,... | collective-permute-start | bytes 245768 | tf_op jit(solution)/shard_map/ppermute | solution.py:274
  63.9 4.7 %collective-permute-start.4 = (f32[8,2560]{1,0:T(8,128)S(1)}, f32[8,2560]{1,0:T(8,128)S(1)}, u32[]{:S(2)}, u32[]{:S(2)}) collective-permute-start(f32[8,2560]{1,0:T(8,128)S(1)} %add_add_fusion.1), channel_id=1, source_target_pairs={{0,2},{1,3},{2,0},{3,1},{4,6},{5,7},{6,4},{7,5},{8,10},{9,11},{10,... | collective-permute-start | bytes 245768 | tf_op jit(solution)/shard_map/ppermute | solution.py:274
  65.4 7.1 %collective-permute-start.5 = (f32[8,2560]{1,0:T(8,128)S(1)}, f32[8,2560]{1,0:T(8,128)S(1)}, u32[]{:S(2)}, u32[]{:S(2)}) collective-permute-start(f32[8,2560]{1,0:T(8,128)S(1)} %add_add_fusion.1), channel_id=1, source_target_pairs={{0,4},{1,5},{2,6},{3,7},{4,0},{5,1},{6,2},{7,3},{8,12},{9,13},{10,... | collective-permute-start | bytes 245768 | tf_op jit(solution)/shard_map/ppermute | solution.py:274
  67.9 6.3 %collective-permute-start.6 = (f32[8,2560]{1,0:T(8,128)S(1)}, f32[8,2560]{1,0:T(8,128)S(1)}, u32[]{:S(2)}, u32[]{:S(2)}) collective-permute-start(f32[8,2560]{1,0:T(8,128)S(1)} %add_add_fusion.1), channel_id=1, source_target_pairs={{0,6},{1,7},{2,4},{3,5},{4,2},{5,3},{6,0},{7,1},{8,14},{9,15},{10,... | collective-permute-start | bytes 245768 | tf_op jit(solution)/shard_map/ppermute | solution.py:274
  74.3 4.5 %collective-permute-start.7 = (f32[8,2560]{1,0:T(8,128)S(1)}, f32[8,2560]{1,0:T(8,128)S(1)}, u32[]{:S(2)}, u32[]{:S(2)}) collective-permute-start(f32[8,2560]{1,0:T(8,128)S(1)} %get-tuple-element.15), channel_id=1, source_target_pairs={{0,8},{1,9},{2,10},{3,11},{4,12},{5,13},{6,14},{7,15},{8,0},{9,1},... | collective-permute-start | bytes 245768 | tf_op jit(solution)/shard_map/ppermute | solution.py:274
  74.9 4.4 %collective-permute-start.8 = (f32[8,2560]{1,0:T(8,128)S(1)}, f32[8,2560]{1,0:T(8,128)S(1)}, u32[]{:S(2)}, u32[]{:S(2)}) collective-permute-start(f32[8,2560]{1,0:T(8,128)S(1)} %get-tuple-element.15), channel_id=1, source_target_pairs={{0,16},{1,17},{2,18},{3,19},{4,20},{5,21},{6,22},{7,23},{8,24},{9,... | collective-permute-start | bytes 245768 | tf_op jit(solution)/shard_map/ppermute | solution.py:274
  75.7 5.3 %collective-permute-start.9 = (f32[8,2560]{1,0:T(8,128)S(1)}, f32[8,2560]{1,0:T(8,128)S(1)}, u32[]{:S(2)}, u32[]{:S(2)}) collective-permute-start(f32[8,2560]{1,0:T(8,128)S(1)} %get-tuple-element.15), channel_id=1, source_target_pairs={{0,24},{1,25},{2,26},{3,27},{4,28},{5,29},{6,30},{7,31},{8,16},{9,... | collective-permute-start | bytes 245768 | tf_op jit(solution)/shard_map/ppermute | solution.py:274
  81.1 1.7 collective-permute-start.10
  93.0 28.2 %all-to-all-start.1 = ((f32[32,56,128]{2,1,0:T(8,128)}), f32[32,56,128]{2,1,0:T(8,128)}, u32[]{:S(2)}, u32[]{:S(2)}) async-start(f32[32,56,128]{2,1,0:T(8,128)} %bitcast.6), calls=%async_computation.1 | async-start | bytes 1835008 | tf_op jit(solution)/shard_map/all_to_all | solution.py:546
  96.3 30.1 %copy-start.2 = (s32[2]{0:T(128)S(1)}, s32[2]{0:T(128)}, u32[]{:S(2)}) copy-start(s32[2]{0:T(128)} %parent.1) | copy-start | bytes 28
  121.1 44.2 %all-to-all-start.2 = ((f32[32,96,128]{2,1,0:T(8,128)}), f32[32,96,128]{2,1,0:T(8,128)S(1)}, u32[]{:S(2)}, u32[]{:S(2)}) async-start(f32[32,96,128]{2,1,0:T(8,128)} %bitcast.7), calls=%async_computation.2 | async-start | bytes 3145728 | tf_op jit(solution)/shard_map/all_to_all | solution.py:546

commit v7 on v6

--- a/solution.py
+++ b/solution.py
@@ -17,7 +17,7 @@
 BF16 = jnp.bfloat16
 MIB = 1024 * 1024
 FIRST_UNITS = 1
-HEAD = 768
+HEAD = 1024
 PIECE = 128
 
 

time: 171 us -> 170 us (level)
    pallas_call x1, Pallas kernels: 26.5 us -> 22.7 us  [contract(): pl.pallas_call(contract_kernel, grid=(rest // block,), out_shape=jax.Shap...]
    pallas_call x1, Pallas kernels: 13.1 us -> 15.8 us  [rotate(): pl.pallas_call(functools.partial(rotate_kernel, devices), grid=(1,), out_...]
  transfers between devices with their start and end apart: 14 -> 14, of which waited for: 13 -> 13; matrix products, arithmetic and copies ran while one was open for 1% -> 1% of each run, Pallas kernels for 30% -> 28%
where the time goes in v7:
time: 170 us; the launch traced here: 169 us
  Pallas kernels  84 us (49%)
  waiting for transfers between devices  53.8 us (32%)
  starting transfers between devices  28 us (16%)
  local copies, waits for them, and re-layouts  2.19 us (1%)
    all_to_all x2, waiting for transfers between devices, per_device(): lax.all_to_all(chunk, BOTH, split_axis=0, concat_axis=0, tiled=True)  37.4 us
    pallas_call x2, Pallas kernels, potential_tiles(): pl.pallas_call(functools.partial(potential_kernel, own, parts, base), gri...  34.5 us
    pallas_call x1, Pallas kernels, contract(): pl.pallas_call(contract_kernel, grid=(rest // block,), out_shape=jax.Shap...  22.7 us
    ppermute x11, waiting for transfers between devices, send(): lax.ppermute(x, BOTH, [(i, target(i)) for i in range(walk_size * chol_siz...  16.4 us
    pallas_call x1, Pallas kernels, rotate(): pl.pallas_call(functools.partial(rotate_kernel, devices), grid=(1,), out_...  15.8 us
    ppermute x11, starting transfers between devices, send(): lax.ppermute(x, BOTH, [(i, target(i)) for i in range(walk_size * chol_siz...  11.8 us
    all_to_all x2, starting transfers between devices, per_device(): lax.all_to_all(chunk, BOTH, split_axis=0, concat_axis=0, tiled=True)  8.75 us
    all_to_all x1, starting transfers between devices, per_device(): lax.all_to_all(sent, BOTH, split_axis=0, concat_axis=0, tiled=True)  7.49 us
  transfers between devices with their start and end apart: 14, of which 13 were waited for; matrix products, arithmetic and copies ran while one was open for 1% of the time, Pallas kernels for 28%

profile of v7, /device:TPU:0, one launch (start us, length us, event | category | flops | bytes accessed | tf_op | source)
XLA Modules:
  0.0 169.2 jit_solution(18206813852434877462)
XLA Ops:
  0.6 15.8 %shard_map.77 = (f32[32,40,128]{2,1,0:T(8,128)}, bf16[512,128]{1,0:T(8,128)(2,1)}, f32[2560,1024]{1,0:T(8,128)}) custom-call(s32[2]{0:T(128)} %parent.1, f32[64,512]{1,0:T(8,128)} %bitcast.11, f32[2,64,512]{2,1,0:T(8,128)} %bitcast.9, f32[2560,8192]{1,0:T(8,128)} %refs_9_.3), custom_call_target="tpu_custom_call" | custom-call | tf_op jit(solution)/shard_map/pallas_call | solution.py:153
  16.4 7.5 %all-to-all-start = ((f32[32,40,128]{2,1,0:T(8,128)}), f32[32,40,128]{2,1,0:T(8,128)S(1)}, u32[]{:S(2)}, u32[]{:S(2)}) async-start(f32[32,40,128]{2,1,0:T(8,128)} %get-tuple-element.7), calls=%async_computation | async-start | bytes 1310720 | tf_op jit(solution)/shard_map/all_to_all | solution.py:524
  23.9 0.0 copy-start
  23.9 22.7 %shard_map.79.contracted = f32[2560,1024]{1,0:T(8,128)} custom-call(bf16[512,128]{1,0:T(8,128)(2,1)} %get-tuple-element.8.pair, f32[2560,8192]{1,0:T(8,128)} %refs_9_.3, f32[2560,1024]{1,0:T(8,128)} %get-tuple-element.9.refs_0_), custom_call_target="tpu_custom_call", output_to_operand_aliasing={{}: (2, {})} | custom-call | flops 4831838208 | bytes 56623104 | tf_op jit(solution)/shard_map/pallas_call | solution.py:201
  46.6 0.0 copy-start.1
  46.6 0.0 all-to-all-done.received.rotated
  46.6 0.0 copy-done
  46.6 5.8 %shard_map.80 = f32[64,2560]{1,0:T(8,128)S(1)} custom-call(s32[1]{0:T(128)} %bitcast.5.place, f32[32,40,128]{2,1,0:T(8,128)S(1)} %all-to-all-done.received.rotated, f32[2,2560]{1,0:T(2,128)S(1)} %copy-done, f32[2560,1024]{1,0:T(8,128)} %shard_map.79.contracted), custom_call_target="tpu_custom_call" | custom-call | tf_op jit(solution)/shard_map/pallas_call | solution.py:253
  52.5 0.2 collective-permute-start
  52.7 1.5 collective-permute-done
  54.2 1.7 %collective-permute-start.1 = (f32[8,2560]{1,0:T(8,128)S(1)}, f32[8,2560]{1,0:T(8,128)S(1)}, u32[]{:S(2)}, u32[]{:S(2)}) collective-permute-start(f32[8,2560]{1,0:T(8,128)S(1)} %get-tuple-element.16), channel_id=1, source_target_pairs={{0,8},{1,9},{2,10},{3,11},{4,12},{5,13},{6,14},{7,15},{8,0},{9,1},... | collective-permute-start | bytes 245768 | tf_op jit(solution)/shard_map/ppermute | solution.py:274
  55.9 1.4 collective-permute-start.2
  57.4 0.4 collective-permute-start.3
  57.8 1.0 collective-permute-done.1
  58.8 2.3 %collective-permute-done.2 = f32[8,2560]{1,0:T(8,128)S(1)} collective-permute-done((f32[8,2560]{1,0:T(8,128)S(1)}, f32[8,2560]{1,0:T(8,128)S(1)}, u32[]{:S(2)}, u32[]{:S(2)}) %collective-permute-start.2) | collective-permute-done | bytes 81952 | tf_op jit(solution)/shard_map/ppermute | solution.py:274
  61.1 1.6 collective-permute-done.3
  62.7 1.5 collective-permute-start.4
  64.3 2.5 %collective-permute-start.5 = (f32[8,2560]{1,0:T(8,128)S(1)}, f32[8,2560]{1,0:T(8,128)S(1)}, u32[]{:S(2)}, u32[]{:S(2)}) collective-permute-start(f32[8,2560]{1,0:T(8,128)S(1)} %add_add_fusion.1), channel_id=1, source_target_pairs={{0,4},{1,5},{2,6},{3,7},{4,0},{5,1},{6,2},{7,3},{8,12},{9,13},{10,... | collective-permute-start | bytes 245768 | tf_op jit(solution)/shard_map/ppermute | solution.py:274
  66.7 0.5 collective-permute-start.6
  67.2 0.1 copy.19
  67.3 0.1 convert_element_type.27
  67.4 0.1 collective-permute-done.4
  67.5 3.8 %collective-permute-done.5 = f32[8,2560]{1,0:T(8,128)S(1)} collective-permute-done((f32[8,2560]{1,0:T(8,128)S(1)}, f32[8,2560]{1,0:T(8,128)S(1)}, u32[]{:S(2)}, u32[]{:S(2)}) %collective-permute-start.5) | collective-permute-done | bytes 81952 | tf_op jit(solution)/shard_map/ppermute | solution.py:274
  71.4 1.7 %collective-permute-done.6 = f32[8,2560]{1,0:T(8,128)S(1)} collective-permute-done((f32[8,2560]{1,0:T(8,128)S(1)}, f32[8,2560]{1,0:T(8,128)S(1)}, u32[]{:S(2)}, u32[]{:S(2)}) %collective-permute-start.6) | collective-permute-done | bytes 81952 | tf_op jit(solution)/shard_map/ppermute | solution.py:274
  73.1 0.6 collective-permute-start.7
  73.7 0.9 collective-permute-start.8
  74.6 2.1 %collective-permute-start.9 = (f32[8,2560]{1,0:T(8,128)S(1)}, f32[8,2560]{1,0:T(8,128)S(1)}, u32[]{:S(2)}, u32[]{:S(2)}) collective-permute-start(f32[8,2560]{1,0:T(8,128)S(1)} %get-tuple-element.15), channel_id=1, source_target_pairs={{0,24},{1,25},{2,26},{3,27},{4,28},{5,29},{6,30},{7,31},{8,16},{9,... | collective-permute-start | bytes 245768 | tf_op jit(solution)/shard_map/ppermute | solution.py:274
  76.6 0.1 fusion.5
  76.8 0.3 shard_map.78.refs_10_
  77.1 0.5 collective-permute-done.7
  77.6 0.5 collective-permute-done.8
  78.1 1.8 %collective-permute-done.9 = f32[8,2560]{1,0:T(8,128)S(1)} collective-permute-done((f32[8,2560]{1,0:T(8,128)S(1)}, f32[8,2560]{1,0:T(8,128)S(1)}, u32[]{:S(2)}, u32[]{:S(2)}) %collective-permute-start.9) | collective-permute-done | bytes 81952 | tf_op jit(solution)/shard_map/ppermute | solution.py:274
  79.9 0.1 collective-permute-start.10
  80.1 1.6 collective-permute-done.10
  81.7 0.0 copy-done.1
  81.7 10.1 %shard_map.81 = (f32[1792,128]{1,0:T(8,128)}, bf16[128,2560]{1,0:T(8,128)(2,1)S(1)}) custom-call(f32[2560,8192]{1,0:T(8,128)} %refs_9_.3, f32[2560,8192]{1,0:T(8,128)} %refs_9_.3, f32[2560,8192]{1,0:T(8,128)} %refs_9_.3, f32[2560,8192]{1,0:T(8,128)} %refs_9_.3, f32[2560,8192]{1,0:T(8,128)} %refs_9_.3, f32[2560,8192]{1,0:T(8,128)} %refs_9_.3, ...), custom_call_target="tpu_custom_call" | custom-call | flops 2013265920 | bytes 20971520 | tf_op jit(solution)/shard_map/pallas_call | solution.py:424
  91.8 3.4 %all-to-all-start.1 = ((f32[32,56,128]{2,1,0:T(8,128)}), f32[32,56,128]{2,1,0:T(8,128)}, u32[]{:S(2)}, u32[]{:S(2)}) async-start(f32[32,56,128]{2,1,0:T(8,128)} %bitcast.6), calls=%async_computation.1 | async-start | bytes 1835008 | tf_op jit(solution)/shard_map/all_to_all | solution.py:546
  95.2 0.0 copy-start.2
  95.2 24.3 %shard_map.82 = f32[3072,128]{1,0:T(8,128)} custom-call(f32[2560,8192]{1,0:T(8,128)} %refs_9_.3, f32[2560,8192]{1,0:T(8,128)} %refs_9_.3, f32[2560,8192]{1,0:T(8,128)} %refs_9_.3, f32[2560,8192]{1,0:T(8,128)} %refs_9_.3, f32[2560,8192]{1,0:T(8,128)} %refs_9_.3, f32[2560,8192]{1,0:T(8,128)} %refs_9_.3, f32[2560,8192]{1,0:T(8,128)} %refs_9_.3, ...), custom_call_target="tpu_custom_call" | custom-call | flops 6039797760 | bytes 62914560 | tf_op jit(solution)/shard_map/pallas_call | solution.py:424
  119.6 0.4 all-to-all-done.1.refs_0_
  120.0 5.4 %all-to-all-start.2 = ((f32[32,96,128]{2,1,0:T(8,128)}), f32[32,96,128]{2,1,0:T(8,128)S(1)}, u32[]{:S(2)}, u32[]{:S(2)}) async-start(f32[32,96,128]{2,1,0:T(8,128)} %bitcast.7), calls=%async_computation.2 | async-start | bytes 3145728 | tf_op jit(solution)/shard_map/all_to_all | solution.py:546
  125.3 0.0 copy-done.2
  125.4 1.9 %gather_fusion = f32[2]{0:T(128)} fusion(f32[32,56,128]{2,1,0:T(8,128)} %all-to-all-done.1.refs_0_, s32[2]{0:T(128)S(1)} %fusion.24), kind=kCustom, calls=%fused_computation | custom fusion | bytes 40 | tf_op jit(solution)/shard_map/gather | solution.py:550
  127.3 37.0 %all-to-all-done.2.refs_1_ = f32[32,96,128]{2,1,0:T(8,128)S(1)} async-done(((f32[32,96,128]{2,1,0:T(8,128)}), f32[32,96,128]{2,1,0:T(8,128)S(1)}, u32[]{:S(2)}, u32[]{:S(2)}) %all-to-all-start.2) | async-done | bytes 1572896 | tf_op jit(solution)/shard_map/all_to_all | solution.py:546
  164.2 4.9 %shard_map.83 = f32[2,64,512]{2,1,0:T(8,128)} custom-call(f32[32,56,128]{2,1,0:T(8,128)} %all-to-all-done.1.refs_0_, f32[32,96,128]{2,1,0:T(8,128)S(1)} %all-to-all-done.2.refs_1_), custom_call_target="tpu_custom_call" | custom-call | tf_op jit(solution)/shard_map/pallas_call | solution.py:499
  (13 shorter events, 0.3 us)
Async XLA Ops:
  16.4 30.2 %all-to-all-start = ((f32[32,40,128]{2,1,0:T(8,128)}), f32[32,40,128]{2,1,0:T(8,128)S(1)}, u32[]{:S(2)}, u32[]{:S(2)}) async-start(f32[32,40,128]{2,1,0:T(8,128)} %get-tuple-element.7), calls=%async_computation | async-start | bytes 1310720 | tf_op jit(solution)/shard_map/all_to_all | solution.py:524
  23.9 22.7 %copy-start = (f32[2,2560]{1,0:T(2,128)S(1)}, f32[2,2560]{1,0:T(2,128)}, u32[]{:S(2)}) copy-start(f32[2,2560]{1,0:T(2,128)} %refs_12_.1) | copy-start | bytes 61444
  46.6 35.1 %copy-start.1 = (f32[2]{0:T(128)S(1)}, f32[2]{0:T(128)}, u32[]{:S(2)}) copy-start(f32[2]{0:T(128)} %refs_15_.1) | copy-start | bytes 28
  52.5 1.7 %collective-permute-start = (f32[32,2560]{1,0:T(8,128)S(1)}, f32[32,2560]{1,0:T(8,128)S(1)}, u32[]{:S(2)}, u32[]{:S(2)}) collective-permute-start(f32[32,2560]{1,0:T(8,128)S(1)} %constant_dynamic-slice_fusion.3), channel_id=1, source_target_pairs={{0,1},{1,0},{2,3},{3,2},{4,5},{5,4},{6,7},{7,6},{8,9},{9,8},{10,11... | collective-permute-start | bytes 983048 | tf_op jit(solution)/shard_map/ppermute | solution.py:274
  54.2 4.6 %collective-permute-start.1 = (f32[8,2560]{1,0:T(8,128)S(1)}, f32[8,2560]{1,0:T(8,128)S(1)}, u32[]{:S(2)}, u32[]{:S(2)}) collective-permute-start(f32[8,2560]{1,0:T(8,128)S(1)} %get-tuple-element.16), channel_id=1, source_target_pairs={{0,8},{1,9},{2,10},{3,11},{4,12},{5,13},{6,14},{7,15},{8,0},{9,1},... | collective-permute-start | bytes 245768 | tf_op jit(solution)/shard_map/ppermute | solution.py:274
  55.9 5.2 %collective-permute-start.2 = (f32[8,2560]{1,0:T(8,128)S(1)}, f32[8,2560]{1,0:T(8,128)S(1)}, u32[]{:S(2)}, u32[]{:S(2)}) collective-permute-start(f32[8,2560]{1,0:T(8,128)S(1)} %get-tuple-element.18), channel_id=1, source_target_pairs={{0,16},{1,17},{2,18},{3,19},{4,20},{5,21},{6,22},{7,23},{8,24},{9,... | collective-permute-start | bytes 245768 | tf_op jit(solution)/shard_map/ppermute | solution.py:274
  57.4 5.3 %collective-permute-start.3 = (f32[8,2560]{1,0:T(8,128)S(1)}, f32[8,2560]{1,0:T(8,128)S(1)}, u32[]{:S(2)}, u32[]{:S(2)}) collective-permute-start(f32[8,2560]{1,0:T(8,128)S(1)} %get-tuple-element.17), channel_id=1, source_target_pairs={{0,24},{1,25},{2,26},{3,27},{4,28},{5,29},{6,30},{7,31},{8,16},{9,... | collective-permute-start | bytes 245768 | tf_op jit(solution)/shard_map/ppermute | solution.py:274
  62.7 4.8 %collective-permute-start.4 = (f32[8,2560]{1,0:T(8,128)S(1)}, f32[8,2560]{1,0:T(8,128)S(1)}, u32[]{:S(2)}, u32[]{:S(2)}) collective-permute-start(f32[8,2560]{1,0:T(8,128)S(1)} %add_add_fusion.1), channel_id=1, source_target_pairs={{0,2},{1,3},{2,0},{3,1},{4,6},{5,7},{6,4},{7,5},{8,10},{9,11},{10,... | collective-permute-start | bytes 245768 | tf_op jit(solution)/shard_map/ppermute | solution.py:274
  64.3 7.1 %collective-permute-start.5 = (f32[8,2560]{1,0:T(8,128)S(1)}, f32[8,2560]{1,0:T(8,128)S(1)}, u32[]{:S(2)}, u32[]{:S(2)}) collective-permute-start(f32[8,2560]{1,0:T(8,128)S(1)} %add_add_fusion.1), channel_id=1, source_target_pairs={{0,4},{1,5},{2,6},{3,7},{4,0},{5,1},{6,2},{7,3},{8,12},{9,13},{10,... | collective-permute-start | bytes 245768 | tf_op jit(solution)/shard_map/ppermute | solution.py:274
  66.7 6.3 %collective-permute-start.6 = (f32[8,2560]{1,0:T(8,128)S(1)}, f32[8,2560]{1,0:T(8,128)S(1)}, u32[]{:S(2)}, u32[]{:S(2)}) collective-permute-start(f32[8,2560]{1,0:T(8,128)S(1)} %add_add_fusion.1), channel_id=1, source_target_pairs={{0,6},{1,7},{2,4},{3,5},{4,2},{5,3},{6,0},{7,1},{8,14},{9,15},{10,... | collective-permute-start | bytes 245768 | tf_op jit(solution)/shard_map/ppermute | solution.py:274
  73.1 4.5 %collective-permute-start.7 = (f32[8,2560]{1,0:T(8,128)S(1)}, f32[8,2560]{1,0:T(8,128)S(1)}, u32[]{:S(2)}, u32[]{:S(2)}) collective-permute-start(f32[8,2560]{1,0:T(8,128)S(1)} %get-tuple-element.15), channel_id=1, source_target_pairs={{0,8},{1,9},{2,10},{3,11},{4,12},{5,13},{6,14},{7,15},{8,0},{9,1},... | collective-permute-start | bytes 245768 | tf_op jit(solution)/shard_map/ppermute | solution.py:274
  73.7 4.4 %collective-permute-start.8 = (f32[8,2560]{1,0:T(8,128)S(1)}, f32[8,2560]{1,0:T(8,128)S(1)}, u32[]{:S(2)}, u32[]{:S(2)}) collective-permute-start(f32[8,2560]{1,0:T(8,128)S(1)} %get-tuple-element.15), channel_id=1, source_target_pairs={{0,16},{1,17},{2,18},{3,19},{4,20},{5,21},{6,22},{7,23},{8,24},{9,... | collective-permute-start | bytes 245768 | tf_op jit(solution)/shard_map/ppermute | solution.py:274
  74.6 5.3 %collective-permute-start.9 = (f32[8,2560]{1,0:T(8,128)S(1)}, f32[8,2560]{1,0:T(8,128)S(1)}, u32[]{:S(2)}, u32[]{:S(2)}) collective-permute-start(f32[8,2560]{1,0:T(8,128)S(1)} %get-tuple-element.15), channel_id=1, source_target_pairs={{0,24},{1,25},{2,26},{3,27},{4,28},{5,29},{6,30},{7,31},{8,16},{9,... | collective-permute-start | bytes 245768 | tf_op jit(solution)/shard_map/ppermute | solution.py:274
  79.9 1.7 %collective-permute-start.10 = (f32[32,2560]{1,0:T(8,128)S(1)}, f32[32,2560]{1,0:T(8,128)S(1)}, u32[]{:S(2)}, u32[]{:S(2)}) collective-permute-start(f32[32,2560]{1,0:T(8,128)S(1)} %pad_maximum_fusion), channel_id=1, source_target_pairs={{0,1},{1,0},{2,3},{3,2},{4,5},{5,4},{6,7},{7,6},{8,9},{9,8},{10,11... | collective-permute-start | bytes 983048 | tf_op jit(solution)/shard_map/ppermute | solution.py:274
  91.8 28.2 %all-to-all-start.1 = ((f32[32,56,128]{2,1,0:T(8,128)}), f32[32,56,128]{2,1,0:T(8,128)}, u32[]{:S(2)}, u32[]{:S(2)}) async-start(f32[32,56,128]{2,1,0:T(8,128)} %bitcast.6), calls=%async_computation.1 | async-start | bytes 1835008 | tf_op jit(solution)/shard_map/all_to_all | solution.py:546
  95.2 30.1 %copy-start.2 = (s32[2]{0:T(128)S(1)}, s32[2]{0:T(128)}, u32[]{:S(2)}) copy-start(s32[2]{0:T(128)} %parent.1) | copy-start | bytes 28
  120.0 44.2 %all-to-all-start.2 = ((f32[32,96,128]{2,1,0:T(8,128)}), f32[32,96,128]{2,1,0:T(8,128)S(1)}, u32[]{:S(2)}, u32[]{:S(2)}) async-start(f32[32,96,128]{2,1,0:T(8,128)} %bitcast.7), calls=%async_computation.2 | async-start | bytes 3145728 | tf_op jit(solution)/shard_map/all_to_all | solution.py:546
